TPU v7x, 32 devices: a whole 2x2x4 slice. The times are simulated.
32 devices in a mesh: seq: 8 (over y, x, core), ctx: 4 (over z).
Axes of the slice: x: 2, y: 2, z: 4, core: 2. Of those that a mesh axis runs over, the one named last changes fastest.
Arguments:
- tokens: bfloat16 [32, 1024, 768], P('seq', 'ctx'), may hold values from -6 to 6
- lengths: int32 [32], P('seq'), may hold values from 256 to 1024, as said below
- query_key_value_weight: bfloat16 [768, 2304], replicated, may hold values from -0.21875 to 0.21875
- attention_out_weight: bfloat16 [768, 768], replicated, may hold values from -0.875 to 0.875
- up_weight: bfloat16 [768, 3072], replicated, may hold values from -0.21875 to 0.21875
- down_weight: bfloat16 [3072, 768], replicated, may hold values from -0.109375 to 0.109375
- ln1_gain: float32 [768], replicated, may hold values from 0.1 to 1.9
- ln1_shift: float32 [768], replicated, may hold values from -1.5 to 1.5
- ln2_gain: float32 [768], replicated, may hold values from 0.1 to 1.9
- ln2_shift: float32 [768], replicated, may hold values from -1.5 to 1.5
- cotangent: bfloat16 [32, 1024, 768], P('seq', 'ctx'), may hold values from -6 to 6
Outputs:
- output: bfloat16 [32, 1024, 768], P('seq', 'ctx')
- grad_tokens: bfloat16 [32, 1024, 768], P('seq', 'ctx')
- grad_w_qkv: float32 [768, 2304], P('seq')
- grad_w_out: float32 [768, 768], P('seq')
- grad_w_up: float32 [768, 3072], P('seq')
- grad_w_down: float32 [3072, 768], P('seq')
- grad_ln1_gain: float32 [768], P('seq')
- grad_ln1_shift: float32 [768], P('seq')
- grad_ln2_gain: float32 [768], P('seq')
- grad_ln2_shift: float32 [768], P('seq')
Inputs may be any that keep to these rules, and one draw needn't show every extreme that they name: `lengths`: in each aligned group of 4 sequences, one has exactly 1024 live positions.
All inputs are finite; a program needn't handle non-finite values.
Results may differ from a plain program's by a relative error of at most 0.014.
Values may be sent and summed in bfloat16 or wider, within the bound.
A program may use at most 384 MiB of HBM per device.

v0:
```python
import jax
import jax.numpy as jnp
from jax import lax
from jax.sharding import PartitionSpec as P

H = 24
HD = 32


epsilon = 1e-05


def layer_norm(rows, gain, shift):
    average = jnp.mean(rows, axis=-1, keepdims=True)
    centred = rows - average
    spread = jnp.mean(centred * centred, axis=-1, keepdims=True)
    return centred * lax.rsqrt(spread + epsilon) * gain + shift


def exact_gelu(value):
    return jax.nn.gelu(value, approximate=False)


def by_pairs(function, pieces):
    split = jax.tree.map(
        lambda tensor: tensor.reshape((tensor.shape[0] // 2, 2) + tensor.shape[1:]), pieces
    )
    result = lax.map(function, split)
    return jax.tree.map(lambda tensor: tensor.reshape((-1,) + tensor.shape[2:]), result)


def split_heads(queries, pairs):
    group, count, width = queries.shape
    span = pairs.shape[1]
    heads_q = queries.reshape(group, count, H, HD)
    heads_k = pairs[..., :width].reshape(group, span, H, HD)
    heads_v = pairs[..., width:].reshape(group, span, H, HD)
    return (heads_q, heads_k, heads_v)


def masked_scores(heads_q, heads_k, block_lengths, query_places, key_places):
    scores = jnp.einsum(
        "gqhd,gkhd->ghqk", heads_q, heads_k, preferred_element_type=jnp.float32
    ) * HD ** (-0.5)
    causal = key_places[None, :] <= query_places[:, None]
    live = key_places[None, :] < block_lengths[:, None]
    allowed = causal[None, None] & live[:, None, None, :]
    return jnp.where(allowed, scores, -1e30)


def block_probs(heads_q, heads_k, block_lengths, first):
    query_places = first + jnp.arange(heads_q.shape[1], dtype=jnp.int32)
    key_places = jnp.arange(heads_k.shape[1], dtype=jnp.int32)
    scores = masked_scores(heads_q, heads_k, block_lengths, query_places, key_places)
    summit = jnp.max(scores, axis=-1, keepdims=True)
    expo = jnp.exp(scores - summit)
    denom = jnp.sum(expo, axis=-1, keepdims=True)
    return (expo / denom, summit, denom)


def per_device(
    tokens,
    lengths,
    query_key_value_weight,
    attention_out_weight,
    up_weight,
    down_weight,
    ln1_gain,
    ln1_shift,
    ln2_gain,
    ln2_shift,
    cotangent,
):
    count_seqs, block, width = tokens.shape
    first = lax.axis_index("ctx") * block
    row_places = first + jnp.arange(block, dtype=jnp.int32)
    valid = (row_places[None, :] < lengths[:, None])[..., None]
    inputs = tokens.astype(jnp.float32)
    normed_input, ln1_pull = jax.vjp(layer_norm, inputs, ln1_gain, ln1_shift)
    normed_low = normed_input.astype(jnp.bfloat16)
    packed_rows = jnp.einsum(
        "sbd,de->sbe", normed_low, query_key_value_weight, preferred_element_type=jnp.float32
    ).astype(jnp.bfloat16)
    queries = packed_rows[..., :width]
    pairs = packed_rows[..., width:]
    gathered = lax.all_gather(pairs, "ctx", axis=1, tiled=True)

    def forward_group(pieces):
        group_q, group_pairs, group_lengths = pieces
        heads_q, heads_k, heads_v = split_heads(group_q, group_pairs)
        probs = block_probs(heads_q, heads_k, group_lengths, first)[0]
        mixed_heads = jnp.einsum(
            "ghqk,gkhd->gqhd",
            probs.astype(jnp.bfloat16),
            heads_v,
            preferred_element_type=jnp.float32,
        )
        return mixed_heads.reshape(group_q.shape)

    mixed_low = by_pairs(forward_group, (queries, gathered, lengths)).astype(jnp.bfloat16)
    middle = inputs + jnp.einsum(
        "sbd,de->sbe", mixed_low, attention_out_weight, preferred_element_type=jnp.float32
    )
    normed_middle, ln2_pull = jax.vjp(layer_norm, middle, ln2_gain, ln2_shift)
    normed_two_low = normed_middle.astype(jnp.bfloat16)
    hidden_state = jnp.einsum(
        "sbd,df->sbf", normed_two_low, up_weight, preferred_element_type=jnp.float32
    )
    active_tokens, gelu_pull = jax.vjp(exact_gelu, hidden_state)
    active_low = active_tokens.astype(jnp.bfloat16)
    total = middle + jnp.einsum(
        "sbf,fd->sbd", active_low, down_weight, preferred_element_type=jnp.float32
    )
    output = jnp.where(valid, total, 0.0).astype(jnp.bfloat16)
    upstream = jnp.where(valid, cotangent.astype(jnp.float32), 0.0)
    upstream_low = upstream.astype(jnp.bfloat16)
    grad_down = jnp.einsum(
        "sbf,sbd->fd", active_low, upstream_low, preferred_element_type=jnp.float32
    )
    grad_active = jnp.einsum(
        "sbd,fd->sbf", upstream_low, down_weight, preferred_element_type=jnp.float32
    )
    grad_hidden = gelu_pull(grad_active)[0].astype(jnp.bfloat16)
    grad_up = jnp.einsum(
        "sbd,sbf->df", normed_two_low, grad_hidden, preferred_element_type=jnp.float32
    )
    grad_normed_two = jnp.einsum(
        "sbf,df->sbd", grad_hidden, up_weight, preferred_element_type=jnp.float32
    )
    grad_middle_norm, grad_gain_two, grad_shift_two = ln2_pull(grad_normed_two)
    grad_middle = upstream + grad_middle_norm
    grad_branch = grad_middle.astype(jnp.bfloat16)
    grad_out = jnp.einsum("sbd,sbe->de", mixed_low, grad_branch, preferred_element_type=jnp.float32)
    grad_mixed = jnp.einsum(
        "sbe,de->sbd", grad_branch, attention_out_weight, preferred_element_type=jnp.float32
    ).astype(jnp.bfloat16)
    keys_again = lax.all_gather(pairs, "ctx", axis=1, tiled=True)

    def backward_group(pieces):
        group_q, group_pairs, group_lengths, group_grad = pieces
        heads_q, heads_k, heads_v = split_heads(group_q, group_pairs)
        grad_heads = group_grad.reshape(heads_q.shape)
        probs = block_probs(heads_q, heads_k, group_lengths, first)[0]
        grad_values = jnp.einsum(
            "ghqk,gqhd->gkhd",
            probs.astype(jnp.bfloat16),
            grad_heads,
            preferred_element_type=jnp.float32,
        )
        grad_probs = jnp.einsum(
            "gqhd,gkhd->ghqk", grad_heads, heads_v, preferred_element_type=jnp.float32
        )
        grad_scores = probs * (grad_probs - jnp.sum(probs * grad_probs, axis=-1, keepdims=True))
        grad_scores = grad_scores.astype(jnp.bfloat16)
        grad_queries = jnp.einsum(
            "ghqk,gkhd->gqhd", grad_scores, heads_k, preferred_element_type=jnp.float32
        ) * HD ** (-0.5)
        grad_keys = jnp.einsum(
            "ghqk,gqhd->gkhd", grad_scores, heads_q, preferred_element_type=jnp.float32
        ) * HD ** (-0.5)
        span = group_pairs.shape[1]
        grad_pairs = jnp.concatenate(
            [
                grad_keys.reshape(group_q.shape[0], span, -1),
                grad_values.reshape(group_q.shape[0], span, -1),
            ],
            axis=-1,
        )
        return (grad_queries.reshape(group_q.shape), grad_pairs)

    grad_queries, grad_pairs = by_pairs(backward_group, (queries, keys_again, lengths, grad_mixed))
    own_grads = lax.psum_scatter(
        grad_pairs.astype(jnp.bfloat16), "ctx", scatter_dimension=1, tiled=True
    ).astype(jnp.float32)
    grad_packed = jnp.concatenate([grad_queries, own_grads], axis=-1).astype(jnp.bfloat16)
    grad_qkv = jnp.einsum(
        "sbd,sbe->de", normed_low, grad_packed, preferred_element_type=jnp.float32
    )
    grad_normed = jnp.einsum(
        "sbe,de->sbd", grad_packed, query_key_value_weight, preferred_element_type=jnp.float32
    )
    grad_input_norm, grad_gain_one, grad_shift_one = ln1_pull(grad_normed)
    grad_tokens = (grad_middle + grad_input_norm).astype(jnp.bfloat16)
    summed = (
        lax.psum_scatter(grad_qkv, "seq", scatter_dimension=0, tiled=True),
        lax.psum_scatter(grad_out, "seq", scatter_dimension=0, tiled=True),
        lax.psum_scatter(grad_up, "seq", scatter_dimension=0, tiled=True),
        lax.psum_scatter(grad_down, "seq", scatter_dimension=0, tiled=True),
        lax.psum_scatter(grad_gain_one, "seq", scatter_dimension=0, tiled=True),
        lax.psum_scatter(grad_shift_one, "seq", scatter_dimension=0, tiled=True),
        lax.psum_scatter(grad_gain_two, "seq", scatter_dimension=0, tiled=True),
        lax.psum_scatter(grad_shift_two, "seq", scatter_dimension=0, tiled=True),
    )
    summed = (
        lax.psum(summed[0].astype(jnp.bfloat16), "ctx").astype(jnp.float32),
        lax.psum(summed[1].astype(jnp.bfloat16), "ctx").astype(jnp.float32),
        lax.psum(summed[2].astype(jnp.bfloat16), "ctx").astype(jnp.float32),
        lax.psum(summed[3].astype(jnp.bfloat16), "ctx").astype(jnp.float32),
        lax.psum(summed[4].astype(jnp.bfloat16), "ctx").astype(jnp.float32),
        lax.psum(summed[5].astype(jnp.bfloat16), "ctx").astype(jnp.float32),
        lax.psum(summed[6].astype(jnp.bfloat16), "ctx").astype(jnp.float32),
        lax.psum(summed[7].astype(jnp.bfloat16), "ctx").astype(jnp.float32),
    )
    return (
        output,
        grad_tokens,
        summed[0],
        summed[1],
        summed[2],
        summed[3],
        summed[4],
        summed[5],
        summed[6],
        summed[7],
    )


def solution(mesh):
    placed = (
        P("seq", "ctx", None),
        P("seq"),
        P(),
        P(),
        P(),
        P(),
        P(),
        P(),
        P(),
        P(),
        P("seq", "ctx", None),
    )
    return jax.shard_map(
        per_device,
        mesh=mesh,
        in_specs=placed,
        out_specs=(
            P("seq", "ctx", None),
            P("seq", "ctx", None),
            P("seq", None),
            P("seq", None),
            P("seq", None),
            P("seq", None),
            P("seq"),
            P("seq"),
            P("seq"),
            P("seq"),
        ),
        check_vma=False,
    )
```

profile of v0, /device:TPU:0, one launch (start us, length us, event | category | flops | bytes accessed | tf_op | source)
XLA Modules:
  0.0 1381.3 jit_solution(7456806447706585844)
XLA Ops:
  28.7 214.5 %all-gather.2.cloned.1.call-done = bf16[4,1024,1536]{2,1,0:T(8,128)(2,1)} async-done(((bf16[4,256,1536]{2,1,0:T(8,128)(2,1)}), bf16[4,1024,1536]{2,1,0:T(8,128)(2,1)}) %all-gather.2.cloned.1.call-update) | async-done | bytes 12582928 | tf_op jit(solution)/shard_map/all_gather | solution.py:86
  243.2 16.7 %copy.32 = bf16[2,2,1024,1536]{2,3,1,0:T(8,128)(2,1)} copy(bf16[2,2,1024,1536]{3,2,1,0:T(8,128)(2,1)} %bitcast.171) | data formatting | bytes 25165824 | tf_op jit(solution)/shard_map/while | solution.py:28
  261.2 114.9 %while.22 = (s32[]{:T(128)}, bf16[2,2,256,768]{2,3,1,0:T(8,128)(2,1)}, bf16[2,2,1024,1536]{2,3,1,0:T(8,128)(2,1)}, s32[]{:T(128)}, s32[2,2]{1,0:T(2,128)S(1)}, /*index=5*/bf16[2,2,256,768]{2,3,1,0:T(8,128)(2,1)}, s32[]{:T(128)}) while((s32[]{:T(128)}, bf16[2,2,256,768]{2,3,1,0:T(8,128)(2,1)}, bf16[2,2,1024,1536]{2,3,1,0:T(8,128)(2,1)}, ...), condition=%wide.region_5.6_spmd, body=%wide.region_2.5_spmd.sunk | while | flops 1686899968 | bytes 138516624 | solution.py:28
  271.4 25.0 %fusion.129 = (f32[2,24,256]{2,1,0:T(8,128)}, f32[2,24,256,1024]{3,2,1,0:T(8,128)}) fusion(pred[2,256,1024]{2,1,0:T(8,128)(4,1)} %broadcast_and_fusion.4, bf16[2,256,24,32]{1,3,2,0:T(8,128)(2,1)} %bitcast.169, bf16[2,1024,24,32]{1,3,2,0:T(8,128)(2,1)} %bitcast.165), kind=kOutput, calls=%fused_computation.142.clone.1 | convolution fusion | flops 855639040 | bytes 54837248 | tf_op jit(solution)/shard_map/while/body/eval_jaxpr/sub | solution.py:56
  296.4 20.1 %fusion.130 = bf16[2,24,32,256]{3,2,1,0:T(8,128)(2,1)} fusion(bf16[2,1024,24,32]{1,3,2,0:T(8,128)(2,1)} %bitcast.164, f32[2,24,256,1024]{3,2,1,0:T(8,128)} %get-tuple-element.274, f32[2,24,256]{2,1,0:T(8,128)} %get-tuple-element.275), kind=kOutput, calls=%fused_computation.8.clone.1 | convolution fusion | flops 830472192 | bytes 54312960 | tf_op jit(solution)/shard_map/while/body/eval_jaxpr/ghqk,gkhd->gqhd/dot_general | solution.py:92
  328.8 25.0 %fusion.129 = (f32[2,24,256]{2,1,0:T(8,128)}, f32[2,24,256,1024]{3,2,1,0:T(8,128)}) fusion(pred[2,256,1024]{2,1,0:T(8,128)(4,1)} %broadcast_and_fusion.4, bf16[2,256,24,32]{1,3,2,0:T(8,128)(2,1)} %bitcast.169, bf16[2,1024,24,32]{1,3,2,0:T(8,128)(2,1)} %bitcast.165), kind=kOutput, calls=%fused_computation.142.clone.1 | convolution fusion | flops 855639040 | bytes 54837248 | tf_op jit(solution)/shard_map/while/body/eval_jaxpr/sub | solution.py:56
  353.8 20.1 %fusion.130 = bf16[2,24,32,256]{3,2,1,0:T(8,128)(2,1)} fusion(bf16[2,1024,24,32]{1,3,2,0:T(8,128)(2,1)} %bitcast.164, f32[2,24,256,1024]{3,2,1,0:T(8,128)} %get-tuple-element.274, f32[2,24,256]{2,1,0:T(8,128)} %get-tuple-element.275), kind=kOutput, calls=%fused_computation.8.clone.1 | convolution fusion | flops 830472192 | bytes 54312960 | tf_op jit(solution)/shard_map/while/body/eval_jaxpr/ghqk,gkhd->gqhd/dot_general | solution.py:92
  391.6 29.5 %multiply_convert_fusion.1 = (bf16[4,256,3072]{2,1,0:T(8,128)(2,1)}, f32[4,256,3072]{2,1,0:T(8,128)}) fusion(f32[4,256,3072]{2,1,0:T(8,128)S(1)} %get-tuple-element.181, u8[256,3072]{1,0:T(8,128)(4,1)S(1)} %get-tuple-element.117, u8[256,3072]{1,0:T(8,128)(4,1)S(1)} %get-tuple-element.116), kind=kLoop, calls=%fused_computation.58 | loop fusion | flops 220200960 | bytes 33030144 | tf_op jit(solution)/shard_map/convert_element_type | solution.py:110
  421.1 16.4 %add_convert_fusion = bf16[4,256,3072]{2,1,0:T(8,128)(2,1)} fusion(f32[4,256,3072]{2,1,0:T(8,128)} %get-tuple-element.168, f32[4,256,3072]{2,1,0:T(8,128)} %copy-done.8, bf16[3072,768]{1,0:T(8,128)(2,1)} %param.20, bf16[4,256,768]{2,1,0:T(8,128)(2,1)} %param.25, pred[4,256]{1,0:T(4,128)(4,1)} %broadcast_compare_fusion), kind=kOutput, calls=%fused_computation.57 | convolution fusion | flops 4878237696 | bytes 37749760 | tf_op jit(solution)/shard_map/sbd,fd->sbf/dot_general | solution.py:120
  455.3 328.4 %while.23 = (s32[]{:T(128)}, bf16[2,2,256,768]{2,3,1,0:T(8,128)(2,1)}, bf16[2,2,1024,1536]{2,3,1,0:T(8,128)(2,1)}, bf16[2,2,1024,1536]{2,3,1,0:T(8,128)(2,1)}, s...) while((s32[]{:T(128)}, ...), condition=%wide.region_14.15_spmd, body=%wide.region_10.14_spmd.sunk | while | flops 4207402240 | bytes 471374080 | solution.py:28
  470.8 25.0 %fusion.143 = (f32[2,24,256]{2,1,0:T(8,128)}, f32[2,24,256,1024]{3,2,1,0:T(8,128)}) fusion(pred[2,256,1024]{2,1,0:T(8,128)(4,1)} %broadcast_and_fusion.5, bf16[2,256,24,32]{1,3,2,0:T(8,128)(2,1)} %bitcast.160, bf16[2,1024,24,32]{1,3,2,0:T(8,128)(2,1)} %bitcast.156), kind=kOutput, calls=%fused_computation.144.clone.1 | convolution fusion | flops 855639040 | bytes 54837248 | tf_op jit(solution)/shard_map/while/body/eval_jaxpr/sub | solution.py:56
  495.8 19.5 %fusion.144 = bf16[2,24,32,1024]{3,2,1,0:T(8,128)(2,1)} fusion(bf16[2,256,24,32]{1,3,2,0:T(8,128)(2,1)} %bitcast.167, f32[2,24,256,1024]{3,2,1,0:T(8,128)} %get-tuple-element.285, f32[2,24,256]{2,1,0:T(8,128)} %get-tuple-element.286), kind=kOutput, calls=%fused_computation.27.clone.1 | convolution fusion | flops 830472192 | bytes 54312960 | tf_op jit(solution)/shard_map/while/body/eval_jaxpr/ghqk,gqhd->gkhd/dot_general | solution.py:144
  515.3 33.4 %multiply_reduce_fusion.5 = (f32[2,24,256]{2,1,0:T(8,128)}, f32[2,24,256,1024]{3,2,1,0:T(8,128)}) fusion(f32[2,24,256,1024]{3,2,1,0:T(8,128)} %get-tuple-element.285, f32[2,24,256]{2,1,0:T(8,128)} %get-tuple-element.286, bf16[2,256,24,32]{1,3,2,0:T(8,128)(2,1)} %bitcast.168, bf16[2,1024,24,32]{1,3,2,0:T(8,128)(2,1)} %bitcast.163), kind=kOutput, calls=%fused_computation.23.clone.1 | convolution fusion | flops 843042816 | bytes 104693760 | tf_op jit(solution)/shard_map/while/body/eval_jaxpr/gqhd,gkhd->ghqk/dot_general | solution.py:150
  548.7 40.4 %multiply_convert_fusion.3 = bf16[2,24,256,1024]{3,2,1,0:T(8,128)(2,1)} fusion(f32[2,24,256,1024]{3,2,1,0:T(8,128)} %get-tuple-element.288, f32[2,24,256]{2,1,0:T(8,128)} %get-tuple-element.289, f32[2,24,256,1024]{3,2,1,0:T(8,128)} %get-tuple-element.285, f32[2,24,256]{2,1,0:T(8,128)} %get-tuple-element.286), kind=kLoop, calls=%fused_computation.22.clone.1 | loop fusion | flops 50331648 | bytes 125927424 | tf_op jit(solution)/shard_map/while/body/eval_jaxpr/convert_element_type | solution.py:154
  589.1 13.8 %convolution_multiply_fusion.2 = bf16[2,24,32,256]{3,2,1,0:T(8,128)(2,1)} fusion(bf16[2,1024,24,32]{1,3,2,0:T(8,128)(2,1)} %bitcast.157, bf16[2,24,256,1024]{3,2,1,0:T(8,128)(2,1)} %multiply_convert_fusion.3), kind=kOutput, calls=%fused_computation.38.clone.1 | convolution fusion | flops 806092800 | bytes 29097984 | tf_op jit(solution)/shard_map/while/body/eval_jaxpr/ghqk,gkhd->gqhd/dot_general | solution.py:155
  603.0 13.0 broadcast_multiply_fusion.4
  634.7 25.0 %fusion.143 = (f32[2,24,256]{2,1,0:T(8,128)}, f32[2,24,256,1024]{3,2,1,0:T(8,128)}) fusion(pred[2,256,1024]{2,1,0:T(8,128)(4,1)} %broadcast_and_fusion.5, bf16[2,256,24,32]{1,3,2,0:T(8,128)(2,1)} %bitcast.160, bf16[2,1024,24,32]{1,3,2,0:T(8,128)(2,1)} %bitcast.156), kind=kOutput, calls=%fused_computation.144.clone.1 | convolution fusion | flops 855639040 | bytes 54837248 | tf_op jit(solution)/shard_map/while/body/eval_jaxpr/sub | solution.py:56
  659.8 19.5 %fusion.144 = bf16[2,24,32,1024]{3,2,1,0:T(8,128)(2,1)} fusion(bf16[2,256,24,32]{1,3,2,0:T(8,128)(2,1)} %bitcast.167, f32[2,24,256,1024]{3,2,1,0:T(8,128)} %get-tuple-element.285, f32[2,24,256]{2,1,0:T(8,128)} %get-tuple-element.286), kind=kOutput, calls=%fused_computation.27.clone.1 | convolution fusion | flops 830472192 | bytes 54312960 | tf_op jit(solution)/shard_map/while/body/eval_jaxpr/ghqk,gqhd->gkhd/dot_general | solution.py:144
  679.2 33.4 %multiply_reduce_fusion.5 = (f32[2,24,256]{2,1,0:T(8,128)}, f32[2,24,256,1024]{3,2,1,0:T(8,128)}) fusion(f32[2,24,256,1024]{3,2,1,0:T(8,128)} %get-tuple-element.285, f32[2,24,256]{2,1,0:T(8,128)} %get-tuple-element.286, bf16[2,256,24,32]{1,3,2,0:T(8,128)(2,1)} %bitcast.168, bf16[2,1024,24,32]{1,3,2,0:T(8,128)(2,1)} %bitcast.163), kind=kOutput, calls=%fused_computation.23.clone.1 | convolution fusion | flops 843042816 | bytes 104693760 | tf_op jit(solution)/shard_map/while/body/eval_jaxpr/gqhd,gkhd->ghqk/dot_general | solution.py:150
  712.6 40.4 %multiply_convert_fusion.3 = bf16[2,24,256,1024]{3,2,1,0:T(8,128)(2,1)} fusion(f32[2,24,256,1024]{3,2,1,0:T(8,128)} %get-tuple-element.288, f32[2,24,256]{2,1,0:T(8,128)} %get-tuple-element.289, f32[2,24,256,1024]{3,2,1,0:T(8,128)} %get-tuple-element.285, f32[2,24,256]{2,1,0:T(8,128)} %get-tuple-element.286), kind=kLoop, calls=%fused_computation.22.clone.1 | loop fusion | flops 50331648 | bytes 125927424 | tf_op jit(solution)/shard_map/while/body/eval_jaxpr/convert_element_type | solution.py:154
  753.1 13.8 %convolution_multiply_fusion.2 = bf16[2,24,32,256]{3,2,1,0:T(8,128)(2,1)} fusion(bf16[2,1024,24,32]{1,3,2,0:T(8,128)(2,1)} %bitcast.157, bf16[2,24,256,1024]{3,2,1,0:T(8,128)(2,1)} %multiply_convert_fusion.3), kind=kOutput, calls=%fused_computation.38.clone.1 | convolution fusion | flops 806092800 | bytes 29097984 | tf_op jit(solution)/shard_map/while/body/eval_jaxpr/ghqk,gkhd->gqhd/dot_general | solution.py:155
  766.9 13.0 broadcast_multiply_fusion.4
  783.7 16.6 %copy.39 = bf16[2,2,1024,1536]{3,2,1,0:T(8,128)(2,1)} copy(bf16[2,2,1024,1536]{2,3,1,0:T(8,128)(2,1)} %get-tuple-element.87) | data formatting | bytes 25165824 | tf_op jit(solution)/shard_map/convert_element_type | solution.py:173
  816.4 11.1 convolution_bitcast_fusion.1
  830.2 180.4 %reduce-scatter.6.cloned.1.call-done = bf16[4,256,1536]{2,1,0:T(8,128)(2,1)} async-done(((bf16[4,1024,1536]{2,1,0:T(8,128)(2,1)}), bf16[4,256,1536]{2,1,0:T(8,128)(2,1)}) %reduce-scatter.6.cloned.1.call-update) | async-done | bytes 3145744 | tf_op jit(solution)/shard_map/reduce_scatter | solution.py:172
  1033.1 24.5 %reduce-scatter.10.cloned.1.call-done = f32[96,768]{1,0:T(8,128)} async-done(((f32[768,768]{1,0:T(8,128)}), f32[96,768]{1,0:T(8,128)}) %reduce-scatter.10.cloned.1.call-update) | async-done | bytes 294928 | tf_op jit(solution)/shard_map/reduce_scatter | solution.py:186
  1059.2 78.6 %reduce-scatter.14.cloned.1.call-done = f32[384,768]{1,0:T(8,128)} async-done(((f32[3072,768]{1,0:T(8,128)}), f32[384,768]{1,0:T(8,128)}) %reduce-scatter.14.cloned.1.call-update) | async-done | bytes 1179664 | tf_op jit(solution)/shard_map/reduce_scatter | solution.py:188
  1140.0 78.1 %reduce-scatter.12.cloned.1.call-done = f32[96,3072]{1,0:T(8,128)} async-done(((f32[768,3072]{1,0:T(8,128)}), f32[96,3072]{1,0:T(8,128)}) %reduce-scatter.12.cloned.1.call-update) | async-done | bytes 1179664 | tf_op jit(solution)/shard_map/reduce_scatter | solution.py:187
  1220.2 67.2 %reduce-scatter.8.cloned.1.call-done = f32[96,2304]{1,0:T(8,128)} async-done(((f32[768,2304]{1,0:T(8,128)}), f32[96,2304]{1,0:T(8,128)}) %reduce-scatter.8.cloned.1.call-update) | async-done | bytes 884752 | tf_op jit(solution)/shard_map/reduce_scatter | solution.py:185
  1299.3 25.2 %all-reduce.4 = (bf16[768]{0:T(1024)(128)(2,1)}, bf16[768]{0:T(1024)(128)(2,1)}, bf16[768]{0:T(1024)(128)(2,1)}, bf16[768]{0:T(1024)(128)(2,1)}) all-reduce(f32[768]{0:T(1024)} %get-tuple-element.120, f32[768]{0:T(1024)} %get-tuple-element.123, f32[768]{0:T(1024)} %get-tuple-element.118, ...), channel_id=7, replica_groups=mesh['seq'=8,'ctx'=4] {'seq'}, use_global_device_ids=true, to_apply=%region_27.28.clone | all-reduce | flops 3072 | bytes 18432
  1329.5 12.6 all-reduce.5
  1353.0 14.3 %all-reduce.9.cloned.1.call-done = (bf16[96,2304]{1,0:T(8,128)(2,1)}, bf16[96,768]{1,0:T(8,128)(2,1)}, bf16[96,3072]{1,0:T(8,128)(2,1)}, bf16[384,768]{1,0:T(8,128)(2,1)}) async-done(((bf16[96,2304]{1,0:T(8,128)(2,1)}, bf16[96,768]{1,0:T(8,128)(2,1)}, bf16[96,3072]{1,0:T(8,128)(2,1)}, bf16[384,768]{1,0:T(8,128)(2,1)}), (bf16[96,2304]{1,0:T(8,128)(2,1)}, bf16[96,768]{1,0:T(8,128)(2,1)}, ...) | async-done | bytes 1769488 | tf_op jit(solution)/shard_map/psum | solution.py:195
  (196 shorter events, 198.6 us)
Async XLA Ops:
  7.2 236.0 %all-gather.2.cloned.1.call-start = ((), (), s32[]{:S(2)}) async-start(), calls=%async_computation.5 | async-start | bytes 15728640 | tf_op jit(solution)/shard_map/all_gather | solution.py:86
  9.1 9.0 copy-start.23
  11.7 6.4 copy-start.25
  22.2 988.4 %reduce-scatter.6.cloned.1.call-start = ((), (), s32[]{:S(2)}) async-start(), calls=%async_computation.6 | async-start | bytes 15728640 | tf_op jit(solution)/shard_map/reduce_scatter | solution.py:172
  380.0 11.6 copy-start.3
  380.0 68.0 %copy-start.19 = (f32[4,256]{1,0:T(4,128)}, f32[4,256]{1,0:T(4,128)S(1)}, u32[]{:S(2)}) copy-start(f32[4,256]{1,0:T(4,128)S(1)} %broadcast_multiply_fusion.1) | copy-start | bytes 12292
  380.5 67.5 %copy-start.21 = (f32[4,256]{1,0:T(4,128)}, f32[4,256]{1,0:T(4,128)S(1)}, u32[]{:S(2)}) copy-start(f32[4,256]{1,0:T(4,128)S(1)} %fusion.65) | copy-start | bytes 12292
  391.6 29.5 %copy-start.8 = (f32[4,256,3072]{2,1,0:T(8,128)}, f32[4,256,3072]{2,1,0:T(8,128)S(1)}, u32[]{:S(2)}) copy-start(f32[4,256,3072]{2,1,0:T(8,128)S(1)} %get-tuple-element.181) | copy-start | bytes 37748740
  437.6 10.5 copy-start.4
  449.3 4.8 copy-start.5
  449.3 4.7 copy-start.27
  603.0 13.0 copy-start.1
  603.0 13.0 copy-start.10
  603.0 13.1 copy-start.2
  766.9 13.0 copy-start.1
  766.9 13.0 copy-start.10
  766.9 13.1 copy-start.2
  800.4 4.9 copy-start.34
  800.4 257.1 %reduce-scatter.10.cloned.1.call-start = ((), (), s32[]{:S(2)}) async-start(), calls=%async_computation.8 | async-start | bytes 2654208 | tf_op jit(solution)/shard_map/reduce_scatter | solution.py:186
  805.3 332.5 %reduce-scatter.14.cloned.1.call-start = ((), (), s32[]{:S(2)}) async-start(), calls=%async_computation.10 | async-start | bytes 10616832 | tf_op jit(solution)/shard_map/reduce_scatter | solution.py:188
  815.7 402.3 %reduce-scatter.12.cloned.1.call-start = ((), (), s32[]{:S(2)}) async-start(), calls=%async_computation.9 | async-start | bytes 10616832 | tf_op jit(solution)/shard_map/reduce_scatter | solution.py:187
  827.5 183.1 %copy-start.24 = (f32[4,256]{1,0:T(4,128)S(1)}, f32[4,256]{1,0:T(4,128)}, u32[]{:S(2)}) copy-start(f32[4,256]{1,0:T(4,128)} %copy-done.23) | copy-start | bytes 12292
  827.5 183.1 %copy-start.26 = (f32[4,256]{1,0:T(4,128)S(1)}, f32[4,256]{1,0:T(4,128)}, u32[]{:S(2)}) copy-start(f32[4,256]{1,0:T(4,128)} %copy-done.25) | copy-start | bytes 12292
  827.5 183.1 %copy-start.31 = (f32[768]{0:T(1024)S(1)}, f32[768]{0:T(1024)}, u32[]{:S(2)}) copy-start(f32[768]{0:T(1024)} %param.21) | copy-start | bytes 9220
  827.5 183.1 %copy-start.38 = (f32[768]{0:T(1024)S(1)}, f32[768]{0:T(1024)}, u32[]{:S(2)}) copy-start(f32[768]{0:T(1024)} %param.22) | copy-start | bytes 9220
  827.5 459.9 %reduce-scatter.8.cloned.1.call-start = ((), (), s32[]{:S(2)}) async-start(), calls=%async_computation.7 | async-start | bytes 7962624 | tf_op jit(solution)/shard_map/reduce_scatter | solution.py:185
  1020.5 346.8 %all-reduce.9.cloned.1.call-start = ((), (), s32[]{:S(2)}) async-start(), calls=%async_computation.11 | async-start | bytes 3538944 | tf_op jit(solution)/shard_map/psum | solution.py:195
  1289.4 7.7 copy-start.30
  1289.4 7.7 copy-start.6
  1289.4 7.7 copy-start.32
  1297.1 50.4 %copy-start.28 = (f32[4,256]{1,0:T(4,128)S(1)}, f32[4,256]{1,0:T(4,128)}, u32[]{:S(2)}) copy-start(f32[4,256]{1,0:T(4,128)} %copy-done.27) | copy-start | bytes 12292
  1367.3 5.9 copy-start.14
  (19 other events, 44.6 us)
Sparse Core Ops, SparseCore 0:
  22.3 220.8 all-gather.1
  800.5 210.0 reduce-scatter.5
  1014.0 43.5 reduce-scatter.9
  1061.3 76.4 reduce-scatter.13
  1141.6 76.4 reduce-scatter.11
  1221.9 65.4 reduce-scatter.7
  1290.6 76.6 all-reduce.8
where the time goes:
time: 1390 us; the launch traced here: 1380 us
  waiting for transfers between devices  658 us (47%)
  matrix products  405 us (29%)
  other arithmetic  157 us (11%)
  local copies, waits for them, and re-layouts  107 us (8%)
  blocking collectives  37.9 us (3%)
  between operations  15.4 us (1%)
    all_gather x1, waiting for transfers between devices, per_device(): gathered = lax.all_gather(pairs, 'ctx', axis=1, tiled=True)  215 us
    reduce_scatter x1, waiting for transfers between devices, per_device(): lax.psum_scatter(grad_pairs.astype(jnp.bfloat16), 'ctx', scatter_dimensio...  180 us
    sub x4, matrix products, block_probs(): expo = jnp.exp(scores - summit)  100 us
    convert_element_type x2, other arithmetic, backward_group(): grad_scores = grad_scores.astype(jnp.bfloat16)  80.9 us
    reduce_scatter x1, waiting for transfers between devices, per_device(): lax.psum_scatter(grad_down, 'seq', scatter_dimension=0, tiled=True)  78.6 us
    reduce_scatter x1, waiting for transfers between devices, per_device(): lax.psum_scatter(grad_up, 'seq', scatter_dimension=0, tiled=True)  78.1 us
    reduce_scatter x1, waiting for transfers between devices, per_device(): lax.psum_scatter(grad_qkv, 'seq', scatter_dimension=0, tiled=True)  67.2 us
    dot_general x2, matrix products, backward_group(): jnp.einsum('gqhd,gkhd->ghqk', grad_heads, heads_v, preferred_element_type...  66.8 us
  transfers between devices with their start and end apart: 7, of which 7 were waited for; matrix products, arithmetic and copies ran while one was open for 6% of the time, Pallas kernels for 0%

commit v1 on v0

v1 whole, which is shorter than its diff:
```python
import math

import jax
import jax.numpy as jnp
from jax import lax
from jax.experimental import pallas as pl
from jax.experimental.pallas import tpu as pltpu
from jax.sharding import PartitionSpec as P

HD = 32
LANES = 128
HEADS = LANES // HD
BLOCK = 256
SCALE = HD ** (-0.5)
SCALE_LOG2 = SCALE * math.log2(math.e)
BF16 = jnp.bfloat16
F32 = jnp.float32
epsilon = 1e-05
MIB = 2**20


def layer_norm(rows, gain, shift):
    average = jnp.mean(rows, axis=-1, keepdims=True)
    centred = rows - average
    spread = jnp.mean(centred * centred, axis=-1, keepdims=True)
    return centred * lax.rsqrt(spread + epsilon) * gain + shift


def exact_gelu(value):
    return jax.nn.gelu(value, approximate=False)


def dot(a, b, dim_a, dim_b):
    return lax.dot_general(
        a, b, (((dim_a,), (dim_b,)), ((), ())), preferred_element_type=F32
    )


def only_head(rows, head):
    lanes = lax.broadcasted_iota(jnp.int32, rows.shape, 1)
    return jnp.where(lanes // HD == head, rows, 0)


def mask_diagonal(scores, block, first, length):
    keys = first + lax.broadcasted_iota(jnp.int32, (block, block), 0)
    queries = first + lax.broadcasted_iota(jnp.int32, (block, block), 1)
    allowed = (keys <= queries) & (keys < length)
    below = scores.shape[0] - block
    diagonal = jnp.where(allowed, scores[below:], -1e30)
    return jnp.concatenate([scores[:below], diagonal], 0) if below else diagonal


def attention_forward_kernel(length_ref, q_ref, k_ref, v_ref, mixed_ref, log_ref, v_t, mixed_t):
    length = length_ref[0]
    count = q_ref.shape[0] // BLOCK
    v_t[...] = v_ref[...].T

    def scores_of(i, head):
        span = (i + 1) * BLOCK
        query = only_head(q_ref[i * BLOCK : span, :], head)
        return mask_diagonal(dot(k_ref[0:span, :], query, 1, 1), BLOCK, i * BLOCK, length)

    steps = [(i, head) for i in range(count) for head in range(HEADS)]
    scores = scores_of(*steps[0])
    for number, (i, head) in enumerate(steps):
        span = (i + 1) * BLOCK
        following = scores_of(*steps[number + 1]) if number + 1 < len(steps) else None
        summit = jnp.max(scores, axis=0, keepdims=True)
        expo = jnp.exp2(scores * SCALE_LOG2 - summit * SCALE_LOG2)
        denom = jnp.sum(expo, axis=0, keepdims=True)
        part = dot(v_t[head * HD : (head + 1) * HD, 0:span], expo.astype(BF16), 1, 0)
        mixed_t[head * HD : (head + 1) * HD, :] = part / denom
        log_ref[0, head : head + 1, i * BLOCK : span] = summit * SCALE_LOG2 + jnp.log2(denom)
        if head == HEADS - 1:
            mixed_ref[i * BLOCK : span, :] = mixed_t[...].T.astype(BF16)
        scores = following


def attention_backward_kernel(
    length_ref, q_ref, k_ref, v_ref, mixed_ref, grad_ref, log_ref,
    grad_q_ref, grad_k_ref, grad_v_ref, k_t, grad_q_t, probs_low, grads_low, sum_k, sum_v,
):
    length = length_ref[0]
    count = q_ref.shape[0] // BLOCK
    k_t[...] = k_ref[...].T

    def rows_of(i):
        rows = slice(i * BLOCK, (i + 1) * BLOCK)
        product = (grad_ref[rows, :].astype(F32) * mixed_ref[rows, :].astype(F32)).T
        queries = [only_head(q_ref[rows, :], head) for head in range(HEADS)]
        grads = [only_head(grad_ref[rows, :], head) for head in range(HEADS)]
        inner = [
            jnp.sum(product[head * HD : (head + 1) * HD], axis=0, keepdims=True)
            for head in range(HEADS)
        ]
        return (queries, grads, inner)

    prepared = [rows_of(i) for i in range(count)]

    def products_of(i, head):
        span = (i + 1) * BLOCK
        scores = dot(k_ref[0:span, :], prepared[i][0][head], 1, 1)
        return (scores, dot(v_ref[0:span, :], prepared[i][1][head], 1, 1))

    steps = [(i, head) for i in range(count) for head in range(HEADS)]
    current = products_of(*steps[0])
    for number, (i, head) in enumerate(steps):
        below = i * BLOCK
        span = below + BLOCK
        following = products_of(*steps[number + 1]) if number + 1 < len(steps) else None
        scores, grad_probs = current
        scores = mask_diagonal(scores, BLOCK, below, length)
        probs = jnp.exp2(scores * SCALE_LOG2 - log_ref[0, head : head + 1, below:span])
        grad_scores = (probs * (grad_probs - prepared[i][2][head])).astype(BF16)
        columns = slice(head * BLOCK, (head + 1) * BLOCK)
        probs_low[0:span, columns] = probs.astype(BF16)
        grads_low[0:span, columns] = grad_scores
        grad_q_t[head * HD : (head + 1) * HD, :] = dot(
            k_t[head * HD : (head + 1) * HD, 0:span], grad_scores, 1, 0
        )
        if head == HEADS - 1:
            grad_q_ref[below:span, :] = (grad_q_t[...].T * SCALE).astype(BF16)
            grad_v = dot(probs_low[0:span, :], jnp.concatenate(prepared[i][1], 0), 1, 0)
            grad_k = dot(grads_low[0:span, :], jnp.concatenate(prepared[i][0], 0), 1, 0)
            if below:
                sum_v[0:below, :] += grad_v[:below]
                sum_k[0:below, :] += grad_k[:below]
            sum_v[below:span, :] = grad_v[below:]
            sum_k[below:span, :] = grad_k[below:]
        current = following
    grad_k_ref[...] = (sum_k[...] * SCALE).astype(BF16)
    grad_v_ref[...] = sum_v[...].astype(BF16)


def column_blocks(rows, first):
    return pl.BlockSpec((rows, LANES), lambda group, length: (0, first + group))


def attention_forward(length, packed):
    rows, width = packed.shape[0], packed.shape[1] // 3
    groups = width // LANES
    blocks = lambda part: column_blocks(rows, part * groups)
    return pl.pallas_call(
        attention_forward_kernel,
        grid_spec=pltpu.PrefetchScalarGridSpec(
            num_scalar_prefetch=1,
            grid=(groups,),
            in_specs=[blocks(0), blocks(1), blocks(2)],
            out_specs=[
                blocks(0),
                pl.BlockSpec((1, HEADS, rows), lambda group, length: (group, 0, 0)),
            ],
            scratch_shapes=[pltpu.VMEM((LANES, rows), BF16), pltpu.VMEM((LANES, BLOCK), F32)],
        ),
        out_shape=[
            jax.ShapeDtypeStruct((rows, width), BF16),
            jax.ShapeDtypeStruct((groups, HEADS, rows), F32),
        ],
        compiler_params=pltpu.CompilerParams(vmem_limit_bytes=56 * MIB),
        cost_estimate=pl.CostEstimate(flops=16 * 10**9, bytes_accessed=7 * 10**6, transcendentals=0),
        name="attention_forward",
    )(length, packed, packed, packed)


def attention_backward(length, packed, mixed, grad_mixed, logs):
    rows, width = mixed.shape
    groups = width // LANES
    blocks = lambda part: column_blocks(rows, part * groups)
    return pl.pallas_call(
        attention_backward_kernel,
        grid_spec=pltpu.PrefetchScalarGridSpec(
            num_scalar_prefetch=1,
            grid=(groups,),
            in_specs=[
                blocks(0),
                blocks(1),
                blocks(2),
                blocks(0),
                blocks(0),
                pl.BlockSpec((1, HEADS, rows), lambda group, length: (group, 0, 0)),
            ],
            out_specs=[blocks(0)] * 3,
            scratch_shapes=[
                pltpu.VMEM((LANES, rows), BF16),
                pltpu.VMEM((LANES, BLOCK), F32),
                pltpu.VMEM((rows, HEADS * BLOCK), BF16),
                pltpu.VMEM((rows, HEADS * BLOCK), BF16),
                pltpu.VMEM((rows, LANES), F32),
                pltpu.VMEM((rows, LANES), F32),
            ],
        ),
        out_shape=[jax.ShapeDtypeStruct((rows, width), BF16)] * 3,
        compiler_params=pltpu.CompilerParams(vmem_limit_bytes=56 * MIB),
        cost_estimate=pl.CostEstimate(flops=40 * 10**9, bytes_accessed=12 * 10**6, transcendentals=0),
        name="attention_backward",
    )(length, packed, packed, packed, mixed, grad_mixed, logs)


def exchange(value, axis, size, bit):
    return lax.ppermute(value, axis, [(i, i ^ (1 << bit)) for i in range(size)])


def halve(value, axis, size, bit, dim):
    mine = (lax.axis_index(axis) >> bit) & 1
    kept = lax.dynamic_index_in_dim(value, mine, dim, keepdims=False)
    sent = lax.dynamic_index_in_dim(value, 1 - mine, dim, keepdims=False)
    got = exchange(sent, axis, size, bit)
    return (kept.astype(F32) + got.astype(F32)).astype(BF16)


def scatter_over_seq(value, size, order):
    bits = list(range(size.bit_length() - 1))
    value = value.reshape((2,) * len(bits) + value.shape[1:])
    left = bits[::-1]
    for bit in order:
        value = halve(value, "seq", size, bit, left.index(bit))
        left.remove(bit)
    return value


def sum_over_ctx(value, size):
    bits = list(range(size.bit_length() - 1))
    rows, columns = value.shape
    value = value.reshape((2,) * len(bits) + (rows // size, columns))
    left = bits[::-1]
    for bit in bits:
        value = halve(value, "ctx", size, bit, left.index(bit))
        left.remove(bit)
    for bit in bits[::-1]:
        got = exchange(value, "ctx", size, bit)
        low = ((lax.axis_index("ctx") >> bit) & 1) == 0
        value = jnp.stack([jnp.where(low, value, got), jnp.where(low, got, value)])
    value = value.transpose(tuple(bits[::-1]) + (len(bits), len(bits) + 1))
    return value.reshape(rows, columns)


def sum_weight(grad, seq_size, ctx_size):
    rows, columns = grad.shape
    blocks = grad.astype(BF16).reshape(seq_size, rows // seq_size, columns)
    order = list(range(seq_size.bit_length() - 1))
    other = order[:1] + order[1:][::-1]
    half = columns // 2
    first = scatter_over_seq(blocks[:, :, :half], seq_size, order)
    second = scatter_over_seq(blocks[:, :, half:], seq_size, other)
    summed = jnp.concatenate([first, second], axis=-1)
    return sum_over_ctx(summed, ctx_size).astype(F32)


def make_per_device(seq_size, ctx_size):
    def to_sequence(value):
        moved = lax.all_to_all(value, "ctx", 0, 0, tiled=True)
        return moved.reshape(-1, value.shape[-1])

    def to_blocks(value, shape):
        return lax.all_to_all(value.reshape(shape), "ctx", 0, 0, tiled=True)

    def per_device(
        tokens,
        lengths,
        query_key_value_weight,
        attention_out_weight,
        up_weight,
        down_weight,
        ln1_gain,
        ln1_shift,
        ln2_gain,
        ln2_shift,
        cotangent,
    ):
        shape = tokens.shape
        length = lax.dynamic_slice_in_dim(lengths, lax.axis_index("ctx"), 1)
        inputs = to_sequence(tokens).astype(F32)
        rows, width = inputs.shape
        valid = (jnp.arange(rows, dtype=jnp.int32) < length[0])[:, None]
        normed_input, ln1_pull = jax.vjp(layer_norm, inputs, ln1_gain, ln1_shift)
        normed_low = normed_input.astype(BF16)
        packed = jnp.dot(
            normed_low, query_key_value_weight, preferred_element_type=F32
        ).astype(BF16)
        mixed_low, logs = attention_forward(length, packed)
        middle = inputs + jnp.dot(mixed_low, attention_out_weight, preferred_element_type=F32)
        normed_middle, ln2_pull = jax.vjp(layer_norm, middle, ln2_gain, ln2_shift)
        normed_two_low = normed_middle.astype(BF16)
        hidden_state = jnp.dot(normed_two_low, up_weight, preferred_element_type=F32)
        active_tokens, gelu_pull = jax.vjp(exact_gelu, hidden_state)
        active_low = active_tokens.astype(BF16)
        total = middle + jnp.dot(active_low, down_weight, preferred_element_type=F32)
        output = to_blocks(jnp.where(valid, total, 0.0).astype(BF16), shape)
        upstream = jnp.where(valid, to_sequence(cotangent).astype(F32), 0.0)
        upstream_low = upstream.astype(BF16)
        grad_down = dot(active_low, upstream_low, 0, 0)
        grad_active = dot(upstream_low, down_weight, 1, 1)
        grad_hidden = gelu_pull(grad_active)[0].astype(BF16)
        grad_up = dot(normed_two_low, grad_hidden, 0, 0)
        grad_normed_two = dot(grad_hidden, up_weight, 1, 1)
        grad_middle_norm, grad_gain_two, grad_shift_two = ln2_pull(grad_normed_two)
        grad_middle = upstream + grad_middle_norm
        grad_branch = grad_middle.astype(BF16)
        grad_out = dot(mixed_low, grad_branch, 0, 0)
        grad_mixed = dot(grad_branch, attention_out_weight, 1, 1).astype(BF16)
        grad_packed = jnp.concatenate(
            attention_backward(length, packed, mixed_low, grad_mixed, logs), axis=-1
        )
        grad_qkv = dot(normed_low, grad_packed, 0, 0)
        grad_normed = dot(grad_packed, query_key_value_weight, 1, 1)
        grad_input_norm, grad_gain_one, grad_shift_one = ln1_pull(grad_normed)
        grad_tokens = to_blocks((grad_middle + grad_input_norm).astype(BF16), shape)
        vectors = jnp.stack([grad_gain_one, grad_shift_one, grad_gain_two, grad_shift_two])
        vectors = lax.psum(vectors, ("seq", "ctx"))
        share = width // seq_size
        vectors = lax.dynamic_slice_in_dim(vectors, lax.axis_index("seq") * share, share, 1)
        return (
            output,
            grad_tokens,
            sum_weight(grad_qkv, seq_size, ctx_size),
            sum_weight(grad_out, seq_size, ctx_size),
            sum_weight(grad_up, seq_size, ctx_size),
            sum_weight(grad_down, seq_size, ctx_size),
            vectors[0],
            vectors[1],
            vectors[2],
            vectors[3],
        )

    return per_device


def solution(mesh):
    placed = (P("seq", "ctx", None), P("seq")) + (P(),) * 8 + (P("seq", "ctx", None),)
    weights = (P("seq", None),) * 4 + (P("seq"),) * 4
    return jax.shard_map(
        make_per_device(mesh.shape["seq"], mesh.shape["ctx"]),
        mesh=mesh,
        in_specs=placed,
        out_specs=(P("seq", "ctx", None),) * 2 + weights,
        check_vma=False,
    )
```

time: 1390 us -> 522 us (0.38)
  waiting for transfers between devices: 658 us -> 163 us
  matrix products: 405 us -> 107 us
  other arithmetic: 157 us -> 38.6 us
  Pallas kernels: 0 us -> 71.5 us
  local copies, waits for them, and re-layouts: 107 us -> 38.6 us
  starting transfers between devices: 0.81 us -> 52.1 us
    reduce_scatter x5 -> x0, waiting for transfers between devices: 429 us -> none  [the longest x1 180 us: per_device(): lax.psum_scatter(grad_pairs.astype(jnp.bfloat16), 'ctx', scatter_dimensio...]
    all_gather x1 -> x0, waiting for transfers between devices: 215 us -> none  [per_device(): gathered = lax.all_gather(pairs, 'ctx', axis=1, tiled=True)]
    dot_general x22 -> x12, matrix products: 305 us -> 107 us  [the longest x8 56.6 us: dot(): lax.dot_general(a, b, (((dim_a,), (dim_b,)), ((), ())), preferred_element...]
    convert_element_type x17 -> x40, other arithmetic: 136 us -> 24.3 us  [the longest x32 13.1 us: halve(): return (kept.astype(F32) + got.astype(F32)).astype(BF16)]
    ppermute x0 -> x40, waiting for transfers between devices: none -> 109 us  [exchange(): return lax.ppermute(value, axis, [(i, i ^ 1 << bit) for i in range(size)])]
    sub x4 -> x0, matrix products: 100 us -> none  [block_probs(): expo = jnp.exp(scores - summit)]
    pallas_call x0 -> x2, Pallas kernels: none -> 71.5 us  [the longest x1 43.2 us: attention_backward(): pl.pallas_call(attention_backward_kernel, grid_spec=pltpu.PrefetchScalarG...]
    all_to_all x0 -> x4, waiting for transfers between devices: none -> 54.4 us  [the longest x2 35.8 us: to_sequence(): moved = lax.all_to_all(value, 'ctx', 0, 0, tiled=True)]
  transfers between devices with their start and end apart: 7 -> 44, of which waited for: 7 -> 23; matrix products, arithmetic and copies ran while one was open for 6% -> 17% of each run, Pallas kernels for 0% -> 5%
where the time goes in v1:
time: 522 us; the launch traced here: 515 us
  waiting for transfers between devices  163 us (31%)
  matrix products  107 us (20%)
  Pallas kernels  71.5 us (14%)
  starting transfers between devices  52.1 us (10%)
  blocking collectives  41.3 us (8%)
  local copies, waits for them, and re-layouts  38.6 us (7%)
  other arithmetic  38.6 us (7%)
    ppermute x40, waiting for transfers between devices, exchange(): return lax.ppermute(value, axis, [(i, i ^ 1 << bit) for i in range(size)])  109 us
    dot_general x8, matrix products, dot(): lax.dot_general(a, b, (((dim_a,), (dim_b,)), ((), ())), preferred_element...  56.6 us
    pallas_call x1, Pallas kernels, attention_backward(): pl.pallas_call(attention_backward_kernel, grid_spec=pltpu.PrefetchScalarG...  43.2 us
    psum x1, blocking collectives, per_device(): vectors = lax.psum(vectors, ('seq', 'ctx'))  41.3 us
    all_to_all x2, waiting for transfers between devices, to_sequence(): moved = lax.all_to_all(value, 'ctx', 0, 0, tiled=True)  35.8 us
    dot_general x1, matrix products, per_device(): jnp.dot(normed_two_low, up_weight, preferred_element_type=F32)  35.1 us
    ppermute x40, starting transfers between devices, exchange(): return lax.ppermute(value, axis, [(i, i ^ 1 << bit) for i in range(size)])  32.4 us
    pallas_call x1, Pallas kernels, attention_forward(): pl.pallas_call(attention_forward_kernel, grid_spec=pltpu.PrefetchScalarGr...  28.2 us
  transfers between devices with their start and end apart: 44, of which 23 were waited for; matrix products, arithmetic and copies ran while one was open for 17% of the time, Pallas kernels for 5%

profile of v1, /device:TPU:0, one launch (start us, length us, event | category | flops | bytes accessed | tf_op | source)
XLA Modules:
  0.0 514.5 jit_solution(16771632686902351026)
XLA Ops:
  0.7 6.6 %all-to-all-start = ((bf16[4,256,768]{2,1,0:T(8,128)(2,1)}), bf16[4,256,768]{2,1,0:T(8,128)(2,1)}, u32[]{:S(2)}, u32[]{:S(2)}) async-start(bf16[4,256,768]{2,1,0:T(8,128)(2,1)} %param.11), calls=%async_computation | async-start | bytes 3145728 | tf_op jit(solution)/shard_map/all_to_all | solution.py:251
  8.5 35.8 %all-to-all-done = bf16[4,256,768]{2,1,0:T(8,128)(2,1)} async-done(((bf16[4,256,768]{2,1,0:T(8,128)(2,1)}), bf16[4,256,768]{2,1,0:T(8,128)(2,1)}, u32[]{:S(2)}, u32[]{:S(2)}) %all-to-all-start) | async-done | bytes 1572896 | tf_op jit(solution)/shard_map/all_to_all | solution.py:251
  44.3 4.4 all-to-all-start.2
  56.8 5.5 %convolution_convert_fusion.q_ref.k_ref.v_ref = bf16[1024,2304]{1,0:T(8,128)(2,1)} fusion(bf16[1024,768]{1,0:T(8,128)(2,1)S(1)} %fusion.14, bf16[768,2304]{1,0:T(8,128)(2,1)S(1)} %copy-done), kind=kOutput, calls=%fused_computation.17 | convolution fusion | flops 3626237952 | bytes 9830400 | tf_op jit(solution)/shard_map/dot_general | solution.py:277
  62.3 28.2 %attention_forward.1 = (bf16[1024,768]{1,0:T(8,128)(2,1)}, f32[6,4,1024]{2,1,0:T(4,128)}) custom-call(s32[1]{0:T(128)} %dynamic_slice.222.length_ref, bf16[1024,2304]{1,0:T(8,128)(2,1)} %convolution_convert_fusion.q_ref.k_ref.v_ref, bf16[1024,2304]{1,0:T(8,128)(2,1)} %convolution_convert_fusion.q_ref.k_ref.v_ref, ...), custom_call_target="tpu_custom_call" | custom-call | flops 16000000000 | bytes 7000000 | tf_op jit(solution)/shard_map/attention_forward/pallas_call | solution.py:143
  90.5 3.6 fusion.62
  95.9 35.1 %multiply_convert_fusion = (bf16[1024,3072]{1,0:T(8,128)(2,1)}, f32[1024,3072]{1,0:T(8,128)}, f32[1024,3072]{1,0:T(8,128)}) fusion(bf16[768,3072]{1,0:T(8,128)(2,1)S(1)} %bitcast.342, f32[1024,768]{1,0:T(8,128)S(1)} %get-tuple-element.61, f32[768]{0:T(1024)S(1)} %copy-done.52, f32[768]{0:T(1024)S(1)} %copy-done.48, f32[1024]{0:T(1024)S(1)} %fusion.52, ...), kind=kOutput, calls=%fused_computation.3 | convolution fusion | flops 5040242688 | bytes 39335936 | tf_op jit(solution)/shard_map/dot_general | solution.py:284
  132.8 15.9 %add_convert_fusion = bf16[1024,3072]{1,0:T(8,128)(2,1)} fusion(f32[1024,3072]{1,0:T(8,128)} %get-tuple-element.29, f32[1024,3072]{1,0:T(8,128)} %get-tuple-element.62, bf16[1024,768]{1,0:T(8,128)(2,1)S(1)} %fusion.7, bf16[3072,768]{1,0:T(8,128)(2,1)} %param.16), kind=kOutput, calls=%fused_computation.2 | convolution fusion | flops 4875878400 | bytes 37748736 | tf_op jit(solution)/shard_map/dot_general | solution.py:34
  148.7 9.3 %multiply_reduce_fusion = (f32[768]{0:T(1024)S(1)}, f32[1024]{0:T(1024)S(1)}, f32[768]{0:T(1024)S(1)}, f32[1024,768]{1,0:T(8,128)S(1)}) fusion(f32[1024,768]{1,0:T(8,128)S(1)} %copy-done.4, f32[1024]{0:T(1024)S(1)} %fusion.52, f32[1024]{0:T(1024)S(1)} %broadcast_multiply_fusion, f32[768]{0:T(1024)S(1)} %copy-done.49, ...), kind=kOutput, calls=%fused_computation.41 | convolution fusion | flops 4838126592 | bytes 17323008 | tf_op jit(solution)/shard_map/dot_general | solution.py:34
  158.1 8.2 %convolution_convert_fusion.2 = bf16[768,3072]{1,0:T(8,128)(2,1)} fusion(bf16[1024,3072]{1,0:T(8,128)(2,1)S(1)} %copy-done.55, f32[1024,768]{1,0:T(8,128)S(1)} %copy-done.4, f32[768]{0:T(1024)S(1)} %copy-done.53, f32[768]{0:T(1024)S(1)} %copy-done.49, f32[1024]{0:T(1024)S(1)} %fusion.52, f32[1024]{0:T(1024)S(1)} %broadcast_multiply_fusion), kind=kOutput, calls=%fused_computation.19 | convolution fusion | flops 4838129664 | bytes 14170112 | tf_op jit(solution)/shard_map/dot_general | solution.py:34
  176.1 7.1 %convolution_convert_fusion.1 = bf16[3072,768]{1,0:T(8,128)(2,1)} fusion(bf16[1024,3072]{1,0:T(8,128)(2,1)S(1)} %bitcast.346, bf16[1024,768]{1,0:T(8,128)(2,1)S(1)} %fusion.7), kind=kOutput, calls=%fused_computation.18 | convolution fusion | flops 4834197504 | bytes 12582912 | tf_op jit(solution)/shard_map/dot_general | solution.py:34
  183.2 6.2 %select_convert_fusion = bf16[1024,768]{1,0:T(8,128)(2,1)} fusion(f32[1024,768]{1,0:T(8,128)S(1)} %copy-done.4, bf16[1024,3072]{1,0:T(8,128)(2,1)S(1)} %bitcast.346, bf16[3072,768]{1,0:T(8,128)(2,1)S(1)} %bitcast.344, pred[1024]{0:T(1024)(128)(4,1)S(1)} %iota_compare_fusion), kind=kOutput, calls=%fused_computation.44 | convolution fusion | flops 4834197504 | bytes 15729664 | tf_op jit(solution)/shard_map/dot_general | solution.py:287
  189.4 43.2 %attention_backward.1 = (bf16[1024,768]{1,0:T(8,128)(2,1)}, bf16[1024,768]{1,0:T(8,128)(2,1)}, bf16[1024,768]{1,0:T(8,128)(2,1)}) custom-call(s32[1]{0:T(128)} %dynamic_slice.222.length_ref, bf16[1024,2304]{1,0:T(8,128)(2,1)} %convolution_convert_fusion.q_ref.k_ref.v_ref, bf16[1024,2304]{1,0:T(8,128)(2,1)} %convolution_convert_fusion.q_ref.k_ref.v_ref, ...), custom_call_target="tpu_custom_call" | custom-call | flops 40000000000 | bytes 12000000 | tf_op jit(solution)/shard_map/attention_backward/pallas_call | solution.py:169
  236.0 5.5 %convolution_convert_fusion.3 = bf16[768,2304]{1,0:T(8,128)(2,1)} fusion(bf16[1024,768]{1,0:T(8,128)(2,1)S(1)} %copy-done.24, bf16[1024,2304]{1,0:T(8,128)(2,1)S(1)} %constant_dynamic-update-slice_fusion), kind=kOutput, calls=%fused_computation.20 | convolution fusion | flops 3625648128 | bytes 9830400 | tf_op jit(solution)/shard_map/dot_general | solution.py:34
  241.5 5.5 %fusion.16 = (f32[1024]{0:T(1024)S(1)}, f32[1024,768]{1,0:T(8,128)S(1)}) fusion(bf16[4,256,768]{2,1,0:T(8,128)(2,1)} %all-to-all-done, f32[768]{0:T(1024)S(1)} %copy-done.39, f32[1024]{0:T(1024)S(1)} %bitcast.336, bf16[1024,2304]{1,0:T(8,128)(2,1)S(1)} %constant_dynamic-update-slice_fusion, bf16[768,2304]{1,0:T(8,128)(2,1)S(1)} %copy-done), kind=kOutput, calls=%fused_computation.38 | convolution fusion | flops 3627809792 | bytes 12987392 | tf_op jit(solution)/shard_map/dot_general | solution.py:34
  248.6 3.5 fusion.15
  252.8 41.3 %psum.7 = f32[4,768]{1,0:T(4,128)} all-reduce(f32[4,768]{1,0:T(4,128)} %pad_maximum_fusion.8), channel_id=1, replica_groups=mesh['seq'=8,'ctx'=4] {'seq','ctx'}, use_global_device_ids=true, to_apply=%region_12.13 | all-reduce | flops 3072 | bytes 24576 | tf_op jit(solution)/shard_map/psum | solution.py:309
  310.7 3.9 collective-permute-done.11
  335.7 4.0 add_convert_fusion.1
  341.7 3.3 collective-permute-done.18
  347.6 4.4 all-to-all-start.3
  352.0 3.9 collective-permute-done.19
  376.1 27.5 %collective-permute-done.2 = bf16[96,1152]{1,0:T(8,128)(2,1)S(1)} collective-permute-done((bf16[96,1152]{1,0:T(8,128)(2,1)S(1)}, bf16[96,1152]{1,0:T(8,128)(2,1)S(1)}, u32[]{:S(2)}, u32[]{:S(2)}) %collective-permute-start.2) | collective-permute-done | bytes 221216 | tf_op jit(solution)/shard_map/ppermute | solution.py:200
  404.5 5.4 %collective-permute-done.5 = bf16[96,1152]{1,0:T(8,128)(2,1)S(1)} collective-permute-done((bf16[96,1152]{1,0:T(8,128)(2,1)S(1)}, bf16[96,1152]{1,0:T(8,128)(2,1)S(1)}, u32[]{:S(2)}, u32[]{:S(2)}) %collective-permute-start.5) | collective-permute-done | bytes 221216 | tf_op jit(solution)/shard_map/ppermute | solution.py:200
  416.3 8.5 %collective-permute-done.7 = bf16[24,2304]{1,0:T(8,128)(2,1)S(1)} collective-permute-done((bf16[24,2304]{1,0:T(8,128)(2,1)S(1)}, bf16[24,2304]{1,0:T(8,128)(2,1)S(1)}, u32[]{:S(2)}, u32[]{:S(2)}) %collective-permute-start.7) | collective-permute-done | bytes 110624 | tf_op jit(solution)/shard_map/ppermute | solution.py:200
  425.8 4.8 collective-permute-done.8
  437.1 4.4 all-to-all-start.1
  443.8 13.1 %collective-permute-done.36 = bf16[2,96,768]{2,1,0:T(8,128)(2,1)} collective-permute-done((bf16[2,96,768]{2,1,0:T(8,128)(2,1)}, bf16[2,96,768]{2,1,0:T(8,128)(2,1)}, u32[]{:S(2)}, u32[]{:S(2)}) %collective-permute-start.36) | collective-permute-done | bytes 294944 | tf_op jit(solution)/shard_map/ppermute | solution.py:200
  458.7 6.2 %collective-permute-done.26 = bf16[2,24,3072]{2,1,0:T(8,128)(2,1)} collective-permute-done((bf16[2,24,3072]{2,1,0:T(8,128)(2,1)}, bf16[2,24,3072]{2,1,0:T(8,128)(2,1)}, u32[]{:S(2)}, u32[]{:S(2)}) %collective-permute-start.26) | collective-permute-done | bytes 294944 | tf_op jit(solution)/shard_map/ppermute | solution.py:200
  466.7 18.6 %all-to-all-done.1 = bf16[4,256,768]{2,1,0:T(8,128)(2,1)} async-done(((bf16[4,256,768]{2,1,0:T(8,128)(2,1)}), bf16[4,256,768]{2,1,0:T(8,128)(2,1)}, u32[]{:S(2)}, u32[]{:S(2)}) %all-to-all-start.1) | async-done | bytes 1572896 | tf_op jit(solution)/shard_map/all_to_all | solution.py:255
  492.9 3.4 collective-permute-done.38
  500.5 4.1 collective-permute-done.39
  (331 shorter events, 131.9 us)
Async XLA Ops:
  0.7 43.7 %all-to-all-start = ((bf16[4,256,768]{2,1,0:T(8,128)(2,1)}), bf16[4,256,768]{2,1,0:T(8,128)(2,1)}, u32[]{:S(2)}, u32[]{:S(2)}) async-start(bf16[4,256,768]{2,1,0:T(8,128)(2,1)} %param.11), calls=%async_computation | async-start | bytes 3145728 | tf_op jit(solution)/shard_map/all_to_all | solution.py:251
  44.3 86.7 %all-to-all-start.2 = ((bf16[4,256,768]{2,1,0:T(8,128)(2,1)}), bf16[4,256,768]{2,1,0:T(8,128)(2,1)}, u32[]{:S(2)}, u32[]{:S(2)}) async-start(bf16[4,256,768]{2,1,0:T(8,128)(2,1)} %param.21), calls=%async_computation.2 | async-start | bytes 3145728 | tf_op jit(solution)/shard_map/all_to_all | solution.py:251
  299.8 62.1 %collective-permute-start.30 = (bf16[2,2,384,384]{3,2,1,0:T(8,128)(2,1)}, bf16[2,2,384,384]{3,2,1,0:T(8,128)(2,1)}, u32[]{:S(2)}, u32[]{:S(2)}) collective-permute-start(bf16[2,2,384,384]{3,2,1,0:T(8,128)(2,1)} %dynamic-slice_bitcast_fusion.1), channel_id=1, source_target_pairs={{0,4},{4,0},{8,12},{12,8},{16,20},{20,16},{24,28},{28,24},{1,5},{5... | collective-permute-start | bytes 3538952 | tf_op jit(solution)/shard_map/ppermute | solution.py:200
  301.4 63.2 %collective-permute-start.33 = (bf16[2,2,384,384]{3,2,1,0:T(8,128)(2,1)}, bf16[2,2,384,384]{3,2,1,0:T(8,128)(2,1)}, u32[]{:S(2)}, u32[]{:S(2)}) collective-permute-start(bf16[2,2,384,384]{3,2,1,0:T(8,128)(2,1)} %dynamic-slice_bitcast_fusion), channel_id=1, source_target_pairs={{0,4},{4,0},{8,12},{12,8},{16,20},{20,16},{24,28},{28,24},{1,5},{5... | collective-permute-start | bytes 3538952 | tf_op jit(solution)/shard_map/ppermute | solution.py:200
  303.2 64.6 %collective-permute-start.20 = (bf16[2,2,96,1536]{3,2,1,0:T(8,128)(2,1)}, bf16[2,2,96,1536]{3,2,1,0:T(8,128)(2,1)}, u32[]{:S(2)}, u32[]{:S(2)}) collective-permute-start(bf16[2,2,96,1536]{3,2,1,0:T(8,128)(2,1)} %dynamic-slice_bitcast_fusion.3), channel_id=1, source_target_pairs={{0,4},{4,0},{8,12},{12,8},{16,20},{20,16},{24,28},{28,24},{1,5},{5... | collective-permute-start | bytes 3538952 | tf_op jit(solution)/shard_map/ppermute | solution.py:200
  307.6 50.0 %collective-permute-start = (bf16[2,2,96,1152]{3,2,1,0:T(8,128)(2,1)}, bf16[2,2,96,1152]{3,2,1,0:T(8,128)(2,1)}, u32[]{:S(2)}, u32[]{:S(2)}) collective-permute-start(bf16[2,2,96,1152]{3,2,1,0:T(8,128)(2,1)} %dynamic-slice_bitcast_fusion.5), channel_id=1, source_target_pairs={{0,4},{4,0},{8,12},{12,8},{16,20},{20,16},{24,28},{28,24},{1,5},{5... | collective-permute-start | bytes 2654216 | tf_op jit(solution)/shard_map/ppermute | solution.py:200
  308.2 6.4 %collective-permute-start.11 = (bf16[2,96,384]{2,1,0:T(8,128)(2,1)S(1)}, bf16[2,96,384]{2,1,0:T(8,128)(2,1)S(1)}, u32[]{:S(2)}, u32[]{:S(2)}) collective-permute-start(bf16[2,96,384]{2,1,0:T(8,128)(2,1)S(1)} %dynamic-slice_bitcast_fusion.26), channel_id=1, source_target_pairs={{0,8},{4,12},{8,0},{12,4},{16,24},{20,28},{24,16},{28,20},{1,9},{5... | collective-permute-start | bytes 442376 | tf_op jit(solution)/shard_map/ppermute | solution.py:200
  346.3 9.7 %collective-permute-start.19 = (bf16[2,24,768]{2,1,0:T(8,128)(2,1)}, bf16[2,24,768]{2,1,0:T(8,128)(2,1)}, u32[]{:S(2)}, u32[]{:S(2)}) collective-permute-start(bf16[2,24,768]{2,1,0:T(8,128)(2,1)} %pad_maximum_fusion.7), channel_id=1, source_target_pairs={{0,1},{1,0},{2,3},{3,2},{4,5},{5,4},{6,7},{7,6},{8,9},{9,8},{10,11... | collective-permute-start | bytes 221192 | tf_op jit(solution)/shard_map/ppermute | solution.py:200
  347.6 89.5 %all-to-all-start.3 = ((bf16[4,256,768]{2,1,0:T(8,128)(2,1)}), bf16[4,256,768]{2,1,0:T(8,128)(2,1)}, u32[]{:S(2)}, u32[]{:S(2)}) async-start(bf16[4,256,768]{2,1,0:T(8,128)(2,1)} %bitcast.311), calls=%async_computation.3 | async-start | bytes 3145728 | tf_op jit(solution)/shard_map/all_to_all | solution.py:255
  357.7 12.4 %collective-permute-start.23 = (bf16[2,2,96,1536]{3,2,1,0:T(8,128)(2,1)}, bf16[2,2,96,1536]{3,2,1,0:T(8,128)(2,1)S(1)}, u32[]{:S(2)}, u32[]{:S(2)}) collective-permute-start(bf16[2,2,96,1536]{3,2,1,0:T(8,128)(2,1)} %dynamic-slice_bitcast_fusion.2), channel_id=1, source_target_pairs={{0,4},{4,0},{8,12},{12,8},{16,20},{20,16},{24,28},{28,24},{1,5},{5... | collective-permute-start | bytes 3538952 | tf_op jit(solution)/shard_map/ppermute | solution.py:200
  360.1 13.1 %collective-permute-start.1 = (bf16[2,96,1152]{2,1,0:T(8,128)(2,1)S(1)}, bf16[2,96,1152]{2,1,0:T(8,128)(2,1)S(1)}, u32[]{:S(2)}, u32[]{:S(2)}) collective-permute-start(bf16[2,96,1152]{2,1,0:T(8,128)(2,1)S(1)} %dynamic-slice_bitcast_fusion.11), channel_id=1, source_target_pairs={{0,8},{4,12},{8,0},{12,4},{16,24},{20,28},{24,16},{28,20},{1,9},{5... | collective-permute-start | bytes 1327112 | tf_op jit(solution)/shard_map/ppermute | solution.py:200
  361.8 13.3 %collective-permute-start.4 = (bf16[2,96,1152]{2,1,0:T(8,128)(2,1)S(1)}, bf16[2,96,1152]{2,1,0:T(8,128)(2,1)S(1)}, u32[]{:S(2)}, u32[]{:S(2)}) collective-permute-start(bf16[2,96,1152]{2,1,0:T(8,128)(2,1)S(1)} %dynamic-slice_bitcast_fusion.10), channel_id=1, source_target_pairs={{0,16},{4,20},{8,24},{12,28},{16,0},{20,4},{24,8},{28,12},{1,17},{... | collective-permute-start | bytes 1327112 | tf_op jit(solution)/shard_map/ppermute | solution.py:200
  364.6 45.5 %collective-permute-start.31 = (bf16[2,384,384]{2,1,0:T(8,128)(2,1)S(1)}, bf16[2,384,384]{2,1,0:T(8,128)(2,1)S(1)}, u32[]{:S(2)}, u32[]{:S(2)}) collective-permute-start(bf16[2,384,384]{2,1,0:T(8,128)(2,1)S(1)} %dynamic-slice_bitcast_fusion.7), channel_id=1, source_target_pairs={{0,8},{4,12},{8,0},{12,4},{16,24},{20,28},{24,16},{28,20},{1,9},{5... | collective-permute-start | bytes 1769480 | tf_op jit(solution)/shard_map/ppermute | solution.py:200
  367.8 43.5 %collective-permute-start.34 = (bf16[2,384,384]{2,1,0:T(8,128)(2,1)S(1)}, bf16[2,384,384]{2,1,0:T(8,128)(2,1)S(1)}, u32[]{:S(2)}, u32[]{:S(2)}) collective-permute-start(bf16[2,384,384]{2,1,0:T(8,128)(2,1)S(1)} %dynamic-slice_bitcast_fusion.6), channel_id=1, source_target_pairs={{0,16},{4,20},{8,24},{12,28},{16,0},{20,4},{24,8},{28,12},{1,17},{... | collective-permute-start | bytes 1769480 | tf_op jit(solution)/shard_map/ppermute | solution.py:200
  370.0 43.0 %collective-permute-start.21 = (bf16[2,96,1536]{2,1,0:T(8,128)(2,1)S(1)}, bf16[2,96,1536]{2,1,0:T(8,128)(2,1)S(1)}, u32[]{:S(2)}, u32[]{:S(2)}) collective-permute-start(bf16[2,96,1536]{2,1,0:T(8,128)(2,1)S(1)} %dynamic-slice_bitcast_fusion.9), channel_id=1, source_target_pairs={{0,8},{4,12},{8,0},{12,4},{16,24},{20,28},{24,16},{28,20},{1,9},{5... | collective-permute-start | bytes 1769480 | tf_op jit(solution)/shard_map/ppermute | solution.py:200
  373.2 42.9 %collective-permute-start.24 = (bf16[2,96,1536]{2,1,0:T(8,128)(2,1)S(1)}, bf16[2,96,1536]{2,1,0:T(8,128)(2,1)S(1)}, u32[]{:S(2)}, u32[]{:S(2)}) collective-permute-start(bf16[2,96,1536]{2,1,0:T(8,128)(2,1)S(1)} %dynamic-slice_bitcast_fusion.8), channel_id=1, source_target_pairs={{0,16},{4,20},{8,24},{12,28},{16,0},{20,4},{24,8},{28,12},{1,17},{... | collective-permute-start | bytes 1769480 | tf_op jit(solution)/shard_map/ppermute | solution.py:200
  375.2 28.5 %collective-permute-start.2 = (bf16[96,1152]{1,0:T(8,128)(2,1)S(1)}, bf16[96,1152]{1,0:T(8,128)(2,1)S(1)}, u32[]{:S(2)}, u32[]{:S(2)}) collective-permute-start(bf16[96,1152]{1,0:T(8,128)(2,1)S(1)} %dynamic-slice_bitcast_fusion.22), channel_id=1, source_target_pairs={{0,16},{4,20},{8,24},{12,28},{16,0},{20,4},{24,8},{28,12},{1,17},{... | collective-permute-start | bytes 663560 | tf_op jit(solution)/shard_map/ppermute | solution.py:200
  410.3 21.2 %collective-permute-start.32 = (bf16[384,384]{1,0:T(8,128)(2,1)S(1)}, bf16[384,384]{1,0:T(8,128)(2,1)S(1)}, u32[]{:S(2)}, u32[]{:S(2)}) collective-permute-start(bf16[384,384]{1,0:T(8,128)(2,1)S(1)} %dynamic-slice_bitcast_fusion.14), channel_id=1, source_target_pairs={{0,16},{4,20},{8,24},{12,28},{16,0},{20,4},{24,8},{28,12},{1,17},{... | collective-permute-start | bytes 884744 | tf_op jit(solution)/shard_map/ppermute | solution.py:200
  411.6 20.0 %collective-permute-start.35 = (bf16[384,384]{1,0:T(8,128)(2,1)S(1)}, bf16[384,384]{1,0:T(8,128)(2,1)S(1)}, u32[]{:S(2)}, u32[]{:S(2)}) collective-permute-start(bf16[384,384]{1,0:T(8,128)(2,1)S(1)} %dynamic-slice_bitcast_fusion.13), channel_id=1, source_target_pairs={{0,8},{4,12},{8,0},{12,4},{16,24},{20,28},{24,16},{28,20},{1,9},{5... | collective-permute-start | bytes 884744 | tf_op jit(solution)/shard_map/ppermute | solution.py:200
  413.3 22.1 %collective-permute-start.22 = (bf16[96,1536]{1,0:T(8,128)(2,1)S(1)}, bf16[96,1536]{1,0:T(8,128)(2,1)S(1)}, u32[]{:S(2)}, u32[]{:S(2)}) collective-permute-start(bf16[96,1536]{1,0:T(8,128)(2,1)S(1)} %dynamic-slice_bitcast_fusion.17), channel_id=1, source_target_pairs={{0,16},{4,20},{8,24},{12,28},{16,0},{20,4},{24,8},{28,12},{1,17},{... | collective-permute-start | bytes 884744 | tf_op jit(solution)/shard_map/ppermute | solution.py:200
  416.1 8.8 %collective-permute-start.7 = (bf16[24,2304]{1,0:T(8,128)(2,1)S(1)}, bf16[24,2304]{1,0:T(8,128)(2,1)S(1)}, u32[]{:S(2)}, u32[]{:S(2)}) collective-permute-start(bf16[24,2304]{1,0:T(8,128)(2,1)S(1)} %dynamic-slice_bitcast_fusion.27), channel_id=1, source_target_pairs={{0,2},{1,3},{2,0},{3,1},{4,6},{5,7},{6,4},{7,5},{8,10},{9,11},{10,... | collective-permute-start | bytes 331784 | tf_op jit(solution)/shard_map/ppermute | solution.py:200
  425.0 10.4 %collective-permute-start.25 = (bf16[96,1536]{1,0:T(8,128)(2,1)S(1)}, bf16[96,1536]{1,0:T(8,128)(2,1)S(1)}, u32[]{:S(2)}, u32[]{:S(2)}) collective-permute-start(bf16[96,1536]{1,0:T(8,128)(2,1)S(1)} %dynamic-slice_bitcast_fusion.16), channel_id=1, source_target_pairs={{0,8},{4,12},{8,0},{12,4},{16,24},{20,28},{24,16},{28,20},{1,9},{5... | collective-permute-start | bytes 884744 | tf_op jit(solution)/shard_map/ppermute | solution.py:200
  431.5 10.1 %collective-permute-start.9 = (bf16[2,24,2304]{2,1,0:T(8,128)(2,1)}, bf16[2,24,2304]{2,1,0:T(8,128)(2,1)}, u32[]{:S(2)}, u32[]{:S(2)}) collective-permute-start(bf16[2,24,2304]{2,1,0:T(8,128)(2,1)} %pad_maximum_fusion.5), channel_id=1, source_target_pairs={{0,1},{1,0},{2,3},{3,2},{4,5},{5,4},{6,7},{7,6},{8,9},{9,8},{10,11... | collective-permute-start | bytes 663560 | tf_op jit(solution)/shard_map/ppermute | solution.py:200
  433.3 23.6 %collective-permute-start.36 = (bf16[2,96,768]{2,1,0:T(8,128)(2,1)}, bf16[2,96,768]{2,1,0:T(8,128)(2,1)}, u32[]{:S(2)}, u32[]{:S(2)}) collective-permute-start(bf16[2,96,768]{2,1,0:T(8,128)(2,1)} %dynamic-slice_bitcast_fusion.12), channel_id=1, source_target_pairs={{0,1},{1,0},{2,3},{3,2},{4,5},{5,4},{6,7},{7,6},{8,9},{9,8},{10,11... | collective-permute-start | bytes 884744 | tf_op jit(solution)/shard_map/ppermute | solution.py:200
  437.1 27.8 %collective-permute-start.26 = (bf16[2,24,3072]{2,1,0:T(8,128)(2,1)}, bf16[2,24,3072]{2,1,0:T(8,128)(2,1)}, u32[]{:S(2)}, u32[]{:S(2)}) collective-permute-start(bf16[2,24,3072]{2,1,0:T(8,128)(2,1)} %dynamic-slice_bitcast_fusion.15), channel_id=1, source_target_pairs={{0,1},{1,0},{2,3},{3,2},{4,5},{5,4},{6,7},{7,6},{8,9},{9,8},{10,11... | collective-permute-start | bytes 884744 | tf_op jit(solution)/shard_map/ppermute | solution.py:200
  437.1 48.2 %all-to-all-start.1 = ((bf16[4,256,768]{2,1,0:T(8,128)(2,1)}), bf16[4,256,768]{2,1,0:T(8,128)(2,1)}, u32[]{:S(2)}, u32[]{:S(2)}) async-start(bf16[4,256,768]{2,1,0:T(8,128)(2,1)} %bitcast.327), calls=%async_computation.1 | async-start | bytes 3145728 | tf_op jit(solution)/shard_map/all_to_all | solution.py:255
  458.7 29.1 %collective-permute-start.37 = (bf16[96,768]{1,0:T(8,128)(2,1)}, bf16[96,768]{1,0:T(8,128)(2,1)}, u32[]{:S(2)}, u32[]{:S(2)}) collective-permute-start(bf16[96,768]{1,0:T(8,128)(2,1)} %dynamic-slice_bitcast_fusion.23), channel_id=1, source_target_pairs={{0,2},{1,3},{2,0},{3,1},{4,6},{5,7},{6,4},{7,5},{8,10},{9,11},{10,... | collective-permute-start | bytes 442376 | tf_op jit(solution)/shard_map/ppermute | solution.py:200
  466.7 24.2 %collective-permute-start.27 = (bf16[24,3072]{1,0:T(8,128)(2,1)}, bf16[24,3072]{1,0:T(8,128)(2,1)}, u32[]{:S(2)}, u32[]{:S(2)}) collective-permute-start(bf16[24,3072]{1,0:T(8,128)(2,1)} %dynamic-slice_bitcast_fusion.24), channel_id=1, source_target_pairs={{0,2},{1,3},{2,0},{3,1},{4,6},{5,7},{6,4},{7,5},{8,10},{9,11},{10,... | collective-permute-start | bytes 442376 | tf_op jit(solution)/shard_map/ppermute | solution.py:200
  488.8 7.5 %collective-permute-start.38 = (bf16[96,768]{1,0:T(8,128)(2,1)S(1)}, bf16[96,768]{1,0:T(8,128)(2,1)S(1)}, u32[]{:S(2)}, u32[]{:S(2)}) collective-permute-start(bf16[96,768]{1,0:T(8,128)(2,1)S(1)} %fusion.43), channel_id=1, source_target_pairs={{0,2},{1,3},{2,0},{3,1},{4,6},{5,7},{6,4},{7,5},{8,10},{9,11},{10,... | collective-permute-start | bytes 442376 | tf_op jit(solution)/shard_map/ppermute | solution.py:200
  492.0 7.5 %collective-permute-start.28 = (bf16[24,3072]{1,0:T(8,128)(2,1)S(1)}, bf16[24,3072]{1,0:T(8,128)(2,1)S(1)}, u32[]{:S(2)}, u32[]{:S(2)}) collective-permute-start(bf16[24,3072]{1,0:T(8,128)(2,1)S(1)} %fusion.44), channel_id=1, source_target_pairs={{0,2},{1,3},{2,0},{3,1},{4,6},{5,7},{6,4},{7,5},{8,10},{9,11},{10,... | collective-permute-start | bytes 442376 | tf_op jit(solution)/shard_map/ppermute | solution.py:200
  496.3 8.3 %collective-permute-start.39 = (bf16[2,96,768]{2,1,0:T(8,128)(2,1)S(1)}, bf16[2,96,768]{2,1,0:T(8,128)(2,1)S(1)}, u32[]{:S(2)}, u32[]{:S(2)}) collective-permute-start(bf16[2,96,768]{2,1,0:T(8,128)(2,1)S(1)} %pad_maximum_fusion.4), channel_id=1, source_target_pairs={{0,1},{1,0},{2,3},{3,2},{4,5},{5,4},{6,7},{7,6},{8,9},{9,8},{10,11... | collective-permute-start | bytes 884744 | tf_op jit(solution)/shard_map/ppermute | solution.py:200
  499.5 8.2 %collective-permute-start.29 = (bf16[2,24,3072]{2,1,0:T(8,128)(2,1)S(1)}, bf16[2,24,3072]{2,1,0:T(8,128)(2,1)S(1)}, u32[]{:S(2)}, u32[]{:S(2)}) collective-permute-start(bf16[2,24,3072]{2,1,0:T(8,128)(2,1)S(1)} %pad_maximum_fusion.3), channel_id=1, source_target_pairs={{0,1},{1,0},{2,3},{3,2},{4,5},{5,4},{6,7},{7,6},{8,9},{9,8},{10,11... | collective-permute-start | bytes 884744 | tf_op jit(solution)/shard_map/ppermute | solution.py:200
  (77 other events, 914.5 us)

commit v2 on v1

--- a/solution.py
+++ b/solution.py
@@ -1,3 +1,4 @@
+import functools
 import math
 
 import jax
@@ -15,25 +16,66 @@
 SCALE_LOG2 = SCALE * math.log2(math.e)
 BF16 = jnp.bfloat16
 F32 = jnp.float32
+MESH = pl.DeviceIdType.MESH
 epsilon = 1e-05
 MIB = 2**20
-
-
-def layer_norm(rows, gain, shift):
-    average = jnp.mean(rows, axis=-1, keepdims=True)
-    centred = rows - average
-    spread = jnp.mean(centred * centred, axis=-1, keepdims=True)
-    return centred * lax.rsqrt(spread + epsilon) * gain + shift
-
-
-def exact_gelu(value):
-    return jax.nn.gelu(value, approximate=False)
+ANY = pl.BlockSpec(memory_space=pl.ANY)
+SMEM = pl.BlockSpec(memory_space=pltpu.SMEM)
+ONE = pl.Buffered(1)
 
 
 def dot(a, b, dim_a, dim_b):
     return lax.dot_general(
         a, b, (((dim_a,), (dim_b,)), ((), ())), preferred_element_type=F32
     )
+
+
+def whole(shape):
+    return pl.BlockSpec(shape, lambda step: (0,) * len(shape), pipeline_mode=ONE)
+
+
+def struct(shape, kind=BF16):
+    return jax.ShapeDtypeStruct(shape, kind)
+
+
+def greet(partners):
+    barrier = pltpu.get_barrier_semaphore()
+    for partner in partners:
+        pl.semaphore_signal(barrier, inc=1, device_id=partner, device_id_type=MESH)
+    pl.semaphore_wait(barrier, len(partners))
+
+
+def to_partner(source, target, send_sem, recv_sem, partner):
+    return pltpu.make_async_remote_copy(
+        src_ref=source,
+        dst_ref=target,
+        send_sem=send_sem,
+        recv_sem=recv_sem,
+        device_id=partner,
+        device_id_type=MESH,
+    )
+
+
+def normalise(rows):
+    centred = rows - jnp.mean(rows, axis=-1, keepdims=True)
+    inverse = lax.rsqrt(jnp.mean(centred * centred, axis=-1, keepdims=True) + epsilon)
+    return (centred * inverse, inverse)
+
+
+def normalise_backward(grad, hat, inverse, gain):
+    grad_hat = grad * gain
+    along = jnp.mean(grad_hat * hat, axis=-1, keepdims=True)
+    return inverse * (grad_hat - jnp.mean(grad_hat, axis=-1, keepdims=True) - hat * along)
+
+
+def gelu_and_slope(value):
+    bell = jnp.exp2(value * value * (-0.5 * math.log2(math.e)))
+    t = 1.0 / (1.0 + jnp.abs(value) * (0.3275911 * math.sqrt(0.5)))
+    series = (1.061405429 * t - 1.453152027) * t + 1.421413741
+    series = ((series * t - 0.284496736) * t + 0.254829592) * t
+    tail = (0.5 * series) * bell
+    cdf = jnp.where(value >= 0, 1.0 - tail, tail)
+    return (value * cdf, cdf + value * (bell * (1.0 / math.sqrt(2.0 * math.pi))))
 
 
 def only_head(rows, head):
@@ -50,15 +92,19 @@
     return jnp.concatenate([scores[:below], diagonal], 0) if below else diagonal
 
 
-def attention_forward_kernel(length_ref, q_ref, k_ref, v_ref, mixed_ref, log_ref, v_t, mixed_t):
-    length = length_ref[0]
-    count = q_ref.shape[0] // BLOCK
-    v_t[...] = v_ref[...].T
+def attend(group, length, packed, mixed_ref, log_ref, v_t, mixed_t):
+    rows, width = packed.shape[0], packed.shape[1] // 3
+    count = rows // BLOCK
+    columns = [
+        pl.ds(pl.multiple_of(part * width + group * LANES, LANES), LANES) for part in range(3)
+    ]
+    v_t[...] = packed[:, columns[2]].T
 
     def scores_of(i, head):
         span = (i + 1) * BLOCK
-        query = only_head(q_ref[i * BLOCK : span, :], head)
-        return mask_diagonal(dot(k_ref[0:span, :], query, 1, 1), BLOCK, i * BLOCK, length)
+        query = only_head(packed[i * BLOCK : span, columns[0]], head)
+        scores = dot(packed[0:span, columns[1]], query, 1, 1)
+        return mask_diagonal(scores, BLOCK, i * BLOCK, length)
 
     steps = [(i, head) for i in range(count) for head in range(HEADS)]
     scores = scores_of(*steps[0])
@@ -74,6 +120,265 @@
         if head == HEADS - 1:
             mixed_ref[i * BLOCK : span, :] = mixed_t[...].T.astype(BF16)
         scores = following
+
+
+def front_kernel(
+    ctx, length_ref, tokens, cotangent, weight, gain, shift,
+    inputs_out, normed_out, packed_out, cotangent_out, mixed_ref, log_ref,
+    inputs, normed, packed, v_t, mixed_t, send, recv, cot_send, cot_recv, local,
+):
+    step = pl.program_id(0)
+    me = lax.axis_index("ctx")
+    block = tokens.shape[1]
+    offsets = [1] + list(range(2, ctx))
+
+    def token_copy(offset):
+        return to_partner(
+            tokens.at[me ^ offset], inputs.at[me], send.at[offset], recv.at[offset],
+            {"ctx": me ^ offset},
+        )
+
+    def cotangent_copy(offset):
+        return to_partner(
+            cotangent.at[me ^ offset], cotangent_out.at[me], cot_send.at[offset],
+            cot_recv.at[offset], {"ctx": me ^ offset},
+        )
+
+    own_cotangent = pltpu.make_async_copy(cotangent.at[me], cotangent_out.at[me], local.at[1])
+    keeps = [
+        pltpu.make_async_copy(inputs, inputs_out, local.at[2]),
+        pltpu.make_async_copy(normed, normed_out, local.at[3]),
+        pltpu.make_async_copy(packed, packed_out, local.at[4]),
+    ]
+
+    @pl.when(step == 0)
+    def _():
+        own = pltpu.make_async_copy(tokens.at[me], inputs.at[me], local.at[0])
+        own.start()
+        greet([{"ctx": me ^ offset} for offset in offsets])
+        for offset in offsets[::-1]:
+            token_copy(offset).start()
+
+        def project(source):
+            hat, _ = normalise(inputs[source].astype(F32))
+            low = (hat * gain[...] + shift[...]).astype(BF16)
+            rows = pl.ds(pl.multiple_of(source * block, block), block)
+            normed[rows, :] = low
+            packed[rows, :] = dot(low, weight[...], 1, 0).astype(BF16)
+
+        own.wait()
+        project(me)
+        for offset in offsets:
+            token_copy(offset).wait_recv()
+            if offset == offsets[-1]:
+                for earlier in offsets:
+                    token_copy(earlier).wait_send()
+                own_cotangent.start()
+                for later in offsets[::-1]:
+                    cotangent_copy(later).start()
+            project(me ^ offset)
+        for keep in keeps:
+            keep.start()
+
+    @pl.when(step > 0)
+    def _():
+        attend(step - 1, length_ref[0], packed, mixed_ref, log_ref, v_t, mixed_t)
+
+    @pl.when(step == pl.num_programs(0) - 1)
+    def _():
+        for keep in keeps:
+            keep.wait()
+        own_cotangent.wait()
+        for offset in offsets:
+            cotangent_copy(offset).wait()
+
+
+def front(ctx, length, tokens, cotangent, weight, gain, shift):
+    blocks, block, width = tokens.shape
+    rows, groups = blocks * block, width // LANES
+    group_of = lambda step: jnp.maximum(step - 1, 0)
+    return pl.pallas_call(
+        functools.partial(front_kernel, ctx),
+        grid=(1 + groups,),
+        in_specs=[SMEM, ANY, ANY, whole(weight.shape), whole(gain.shape), whole(shift.shape)],
+        out_specs=[
+            ANY, ANY, ANY, ANY,
+            pl.BlockSpec((rows, LANES), lambda step: (0, group_of(step))),
+            pl.BlockSpec((1, HEADS, rows), lambda step: (group_of(step), 0, 0)),
+        ],
+        out_shape=[
+            struct(tokens.shape),
+            struct((rows, width)),
+            struct((rows, 3 * width)),
+            struct(tokens.shape),
+            struct((rows, width)),
+            struct((groups, HEADS, rows), F32),
+        ],
+        scratch_shapes=[
+            pltpu.VMEM(tokens.shape, BF16),
+            pltpu.VMEM((rows, width), BF16),
+            pltpu.VMEM((rows, 3 * width), BF16),
+            pltpu.VMEM((LANES, rows), BF16),
+            pltpu.VMEM((LANES, BLOCK), F32),
+            pltpu.SemaphoreType.DMA((ctx,)),
+            pltpu.SemaphoreType.DMA((ctx,)),
+            pltpu.SemaphoreType.DMA((ctx,)),
+            pltpu.SemaphoreType.DMA((ctx,)),
+            pltpu.SemaphoreType.DMA((5,)),
+        ],
+        compiler_params=pltpu.CompilerParams(
+            vmem_limit_bytes=56 * MIB, collective_id=0, has_side_effects=True
+        ),
+        name="front",
+    )(length, tokens, cotangent, weight, gain, shift)
+
+
+def feed_forward_kernel(
+    blocks, length_ref, inputs, mixed, cotangent, out_weight, up_weight, down_weight, gain, shift,
+    output, grad_middle_ref, grad_mixed_ref, grad_down_ref, grad_up_ref, grad_out_ref, grad_norm_ref,
+    normed, upstream, branch, active, hidden, staged, send, recv, local,
+):
+    step = pl.program_id(0)
+    me = lax.axis_index("ctx")
+    block = staged.shape[1]
+    width = normed.shape[1]
+    wide = active.shape[1]
+    cuts = wide // width
+
+    def output_copy(row):
+        return to_partner(
+            staged.at[row], output.at[me], send.at[row], recv.at[me], {"ctx": row}
+        )
+
+    own_output = pltpu.make_async_copy(staged.at[me], output.at[me], local)
+
+    @pl.when(step == 0)
+    def _():
+        greet([{"ctx": me ^ offset} for offset in range(1, blocks)])
+        grad_norm_ref[...] = jnp.zeros_like(grad_norm_ref)
+
+    @pl.when(step < blocks)
+    def _():
+        rows = pl.ds(pl.multiple_of(step * block, block), block)
+        middle = inputs[step].astype(F32) + dot(mixed[rows, :], out_weight[...], 1, 0)
+        hat, inverse = normalise(middle)
+        low = (hat * gain[...] + shift[...]).astype(BF16)
+        normed[rows, :] = low
+        places = step * block + lax.broadcasted_iota(jnp.int32, (block, 1), 0)
+        valid = places < length_ref[0]
+        upstream_full = jnp.where(valid, cotangent[step].astype(F32), 0.0)
+        upstream_low = upstream_full.astype(BF16)
+        upstream[rows, :] = upstream_low
+
+        def products_of(cut):
+            part = slice(cut * width, (cut + 1) * width)
+            return (
+                dot(low, up_weight[:, part], 1, 0),
+                dot(upstream_low, down_weight[part, :], 1, 1),
+            )
+
+        current = products_of(0)
+        total, grad_normed = middle, 0.0
+        for cut in range(cuts):
+            part = slice(cut * width, (cut + 1) * width)
+            following = products_of(cut + 1) if cut + 1 < cuts else None
+            value, slope = gelu_and_slope(current[0])
+            value = value.astype(BF16)
+            grad_hidden = (slope * current[1]).astype(BF16)
+            active[rows, part] = value
+            hidden[rows, part] = grad_hidden
+            total = total + dot(value, down_weight[part, :], 1, 0)
+            grad_normed = grad_normed + dot(grad_hidden, up_weight[:, part], 1, 1)
+            current = following
+        staged[step] = jnp.where(valid, total, 0.0).astype(BF16)
+
+        @pl.when(step != me)
+        def _():
+            output_copy(step).start()
+
+        @pl.when(step == me)
+        def _():
+            own_output.start()
+
+        grad_norm_ref[0:1, :] += jnp.sum(grad_normed * hat, axis=0, keepdims=True)
+        grad_norm_ref[1:2, :] += jnp.sum(grad_normed, axis=0, keepdims=True)
+        grad_middle = upstream_full + normalise_backward(grad_normed, hat, inverse, gain[...])
+        grad_middle_ref[...] = grad_middle
+        grad_branch = grad_middle.astype(BF16)
+        branch[rows, :] = grad_branch
+        grad_mixed_ref[...] = dot(grad_branch, out_weight[...], 1, 1).astype(BF16)
+
+    @pl.when(step == blocks)
+    def _():
+        grad_out_ref[...] = dot(mixed[...], branch[...], 0, 0).astype(BF16)
+
+    @pl.when(step >= blocks)
+    def _():
+        size = grad_down_ref.shape[0]
+        part = pl.ds(pl.multiple_of((step - blocks) * size, size), size)
+        grad_down_ref[...] = dot(active[:, part], upstream[...], 0, 0).astype(BF16)
+        grad_up_ref[...] = dot(normed[...], hidden[:, part], 0, 0).astype(BF16)
+
+    @pl.when(step == pl.num_programs(0) - 1)
+    def _():
+        own_output.wait()
+        for row in range(blocks):
+
+            @pl.when(row != me)
+            def _():
+                copy = output_copy(row)
+                copy.wait_send()
+                to_partner(
+                    staged.at[row], output.at[row], send.at[row], recv.at[row], {"ctx": row}
+                ).wait_recv()
+
+
+def feed_forward(length, inputs, mixed, cotangent, out_weight, up_weight, down_weight, gain, shift):
+    blocks, block, width = inputs.shape
+    rows, wide = blocks * block, up_weight.shape[1]
+    size = 512
+    steps = blocks + wide // size
+    early = lambda step: jnp.minimum(step, blocks - 1)
+    late = lambda step: jnp.maximum(step - blocks, 0)
+    operands = (inputs, mixed, cotangent, out_weight, up_weight, down_weight, gain, shift)
+    return pl.pallas_call(
+        functools.partial(feed_forward_kernel, blocks),
+        grid=(steps,),
+        in_specs=[SMEM] + [whole(operand.shape) for operand in operands],
+        out_specs=[
+            ANY,
+            pl.BlockSpec((block, width), lambda step: (early(step), 0)),
+            pl.BlockSpec((block, width), lambda step: (early(step), 0)),
+            pl.BlockSpec((size, width), lambda step: (late(step), 0)),
+            pl.BlockSpec((width, size), lambda step: (0, late(step))),
+            whole((width, width)),
+            whole((8, width)),
+        ],
+        out_shape=[
+            struct(inputs.shape),
+            struct((rows, width), F32),
+            struct((rows, width)),
+            struct((wide, width)),
+            struct((width, wide)),
+            struct((width, width)),
+            struct((8, width), F32),
+        ],
+        scratch_shapes=[
+            pltpu.VMEM((rows, width), BF16),
+            pltpu.VMEM((rows, width), BF16),
+            pltpu.VMEM((rows, width), BF16),
+            pltpu.VMEM((rows, wide), BF16),
+            pltpu.VMEM((rows, wide), BF16),
+            pltpu.VMEM(inputs.shape, BF16),
+            pltpu.SemaphoreType.DMA((blocks,)),
+            pltpu.SemaphoreType.DMA((blocks,)),
+            pltpu.SemaphoreType.DMA,
+        ],
+        compiler_params=pltpu.CompilerParams(
+            vmem_limit_bytes=60 * MIB, collective_id=1, has_side_effects=True
+        ),
+        name="feed_forward",
+    )(length, *operands)
 
 
 def attention_backward_kernel(
@@ -134,32 +439,6 @@
 
 def column_blocks(rows, first):
     return pl.BlockSpec((rows, LANES), lambda group, length: (0, first + group))
-
-
-def attention_forward(length, packed):
-    rows, width = packed.shape[0], packed.shape[1] // 3
-    groups = width // LANES
-    blocks = lambda part: column_blocks(rows, part * groups)
-    return pl.pallas_call(
-        attention_forward_kernel,
-        grid_spec=pltpu.PrefetchScalarGridSpec(
-            num_scalar_prefetch=1,
-            grid=(groups,),
-            in_specs=[blocks(0), blocks(1), blocks(2)],
-            out_specs=[
-                blocks(0),
-                pl.BlockSpec((1, HEADS, rows), lambda group, length: (group, 0, 0)),
-            ],
-            scratch_shapes=[pltpu.VMEM((LANES, rows), BF16), pltpu.VMEM((LANES, BLOCK), F32)],
-        ),
-        out_shape=[
-            jax.ShapeDtypeStruct((rows, width), BF16),
-            jax.ShapeDtypeStruct((groups, HEADS, rows), F32),
-        ],
-        compiler_params=pltpu.CompilerParams(vmem_limit_bytes=56 * MIB),
-        cost_estimate=pl.CostEstimate(flops=16 * 10**9, bytes_accessed=7 * 10**6, transcendentals=0),
-        name="attention_forward",
-    )(length, packed, packed, packed)
 
 
 def attention_backward(length, packed, mixed, grad_mixed, logs):
@@ -247,13 +526,6 @@
 
 
 def make_per_device(seq_size, ctx_size):
-    def to_sequence(value):
-        moved = lax.all_to_all(value, "ctx", 0, 0, tiled=True)
-        return moved.reshape(-1, value.shape[-1])
-
-    def to_blocks(value, shape):
-        return lax.all_to_all(value.reshape(shape), "ctx", 0, 0, tiled=True)
-
     def per_device(
         tokens,
         lengths,
@@ -268,44 +540,27 @@
         cotangent,
     ):
         shape = tokens.shape
+        width = shape[-1]
         length = lax.dynamic_slice_in_dim(lengths, lax.axis_index("ctx"), 1)
-        inputs = to_sequence(tokens).astype(F32)
-        rows, width = inputs.shape
-        valid = (jnp.arange(rows, dtype=jnp.int32) < length[0])[:, None]
-        normed_input, ln1_pull = jax.vjp(layer_norm, inputs, ln1_gain, ln1_shift)
-        normed_low = normed_input.astype(BF16)
-        packed = jnp.dot(
-            normed_low, query_key_value_weight, preferred_element_type=F32
-        ).astype(BF16)
-        mixed_low, logs = attention_forward(length, packed)
-        middle = inputs + jnp.dot(mixed_low, attention_out_weight, preferred_element_type=F32)
-        normed_middle, ln2_pull = jax.vjp(layer_norm, middle, ln2_gain, ln2_shift)
-        normed_two_low = normed_middle.astype(BF16)
-        hidden_state = jnp.dot(normed_two_low, up_weight, preferred_element_type=F32)
-        active_tokens, gelu_pull = jax.vjp(exact_gelu, hidden_state)
-        active_low = active_tokens.astype(BF16)
-        total = middle + jnp.dot(active_low, down_weight, preferred_element_type=F32)
-        output = to_blocks(jnp.where(valid, total, 0.0).astype(BF16), shape)
-        upstream = jnp.where(valid, to_sequence(cotangent).astype(F32), 0.0)
-        upstream_low = upstream.astype(BF16)
-        grad_down = dot(active_low, upstream_low, 0, 0)
-        grad_active = dot(upstream_low, down_weight, 1, 1)
-        grad_hidden = gelu_pull(grad_active)[0].astype(BF16)
-        grad_up = dot(normed_two_low, grad_hidden, 0, 0)
-        grad_normed_two = dot(grad_hidden, up_weight, 1, 1)
-        grad_middle_norm, grad_gain_two, grad_shift_two = ln2_pull(grad_normed_two)
-        grad_middle = upstream + grad_middle_norm
-        grad_branch = grad_middle.astype(BF16)
-        grad_out = dot(mixed_low, grad_branch, 0, 0)
-        grad_mixed = dot(grad_branch, attention_out_weight, 1, 1).astype(BF16)
+        row = lambda vector: vector.reshape(1, width)
+        inputs, normed_low, packed, cotangent, mixed_low, logs = front(
+            ctx_size, length, tokens, cotangent, query_key_value_weight, row(ln1_gain), row(ln1_shift)
+        )
+        output, grad_middle, grad_mixed, grad_down, grad_up, grad_out, grad_norm_two = feed_forward(
+            length, inputs, mixed_low, cotangent, attention_out_weight, up_weight, down_weight,
+            row(ln2_gain), row(ln2_shift),
+        )
         grad_packed = jnp.concatenate(
             attention_backward(length, packed, mixed_low, grad_mixed, logs), axis=-1
         )
         grad_qkv = dot(normed_low, grad_packed, 0, 0)
         grad_normed = dot(grad_packed, query_key_value_weight, 1, 1)
-        grad_input_norm, grad_gain_one, grad_shift_one = ln1_pull(grad_normed)
-        grad_tokens = to_blocks((grad_middle + grad_input_norm).astype(BF16), shape)
-        vectors = jnp.stack([grad_gain_one, grad_shift_one, grad_gain_two, grad_shift_two])
+        hat, inverse = normalise(inputs.reshape(-1, width).astype(F32))
+        grad_gain_one = jnp.sum(grad_normed * hat, axis=0)
+        grad_shift_one = jnp.sum(grad_normed, axis=0)
+        grad_inputs = grad_middle + normalise_backward(grad_normed, hat, inverse, ln1_gain)
+        grad_tokens = lax.all_to_all(grad_inputs.astype(BF16).reshape(shape), "ctx", 0, 0, tiled=True)
+        vectors = jnp.stack([grad_gain_one, grad_shift_one, grad_norm_two[0], grad_norm_two[1]])
         vectors = lax.psum(vectors, ("seq", "ctx"))
         share = width // seq_size
         vectors = lax.dynamic_slice_in_dim(vectors, lax.axis_index("seq") * share, share, 1)

time: 522 us -> 459 us (0.88)
  Pallas kernels: 71.5 us -> 174 us
  matrix products: 107 us -> 11.3 us
  waiting for transfers between devices: 163 us -> 110 us
  other arithmetic: 38.6 us -> 20 us
  local copies, waits for them, and re-layouts: 38.6 us -> 45.9 us
    pallas_call x1 -> x2, Pallas kernels: 28.2 us -> 131 us  [the longest x1 78 us: front(): pl.pallas_call(functools.partial(front_kernel, ctx), grid=(1 + groups,),...]
    all_to_all x4 -> x1, waiting for transfers between devices: 54.4 us -> 0.01 us  [per_device(): lax.all_to_all(grad_inputs.astype(BF16).reshape(shape), 'ctx', 0, 0, tile...]
    dot_general x4 -> x0, matrix products: 50.4 us -> none  [the longest x1 35.1 us: per_device(): jnp.dot(normed_two_low, up_weight, preferred_element_type=F32)]
    dot_general x8 -> x2, matrix products: 56.6 us -> 11.3 us  [dot(): lax.dot_general(a, b, (((dim_a,), (dim_b,)), ((), ())), preferred_element...]
    convert_element_type x4 -> x1, other arithmetic: 10.9 us -> 2.2 us  [per_device(): grad_inputs.astype(BF16).reshape(shape)]
    reduce_sum x5 -> x2, other arithmetic: 9.19 us -> 0.86 us  [the longest x1 0.58 us: normalise(): jnp.mean(centred * centred, axis=-1, keepdims=True) + epsilon]
    unnamed x136 -> x50, local copies, waits for them, and re-layouts: 17.8 us -> 11.1 us
    all_to_all x4 -> x1, starting transfers between devices: 19.7 us -> 16.3 us  [per_device(): lax.all_to_all(grad_inputs.astype(BF16).reshape(shape), 'ctx', 0, 0, tile...]
  transfers between devices with their start and end apart: 44 -> 41, of which waited for: 23 -> 21; matrix products, arithmetic and copies ran while one was open for 17% -> 12% of each run, Pallas kernels for 5% -> 10%
where the time goes in v2:
time: 459 us; the launch traced here: 452 us
  Pallas kernels  174 us (38%)
  waiting for transfers between devices  110 us (24%)
  starting transfers between devices  48.9 us (11%)
  local copies, waits for them, and re-layouts  45.9 us (10%)
  blocking collectives  40.2 us (9%)
  other arithmetic  20 us (4%)
  matrix products  11.3 us (2%)
    ppermute x40, waiting for transfers between devices, exchange(): return lax.ppermute(value, axis, [(i, i ^ 1 << bit) for i in range(size)])  110 us
    pallas_call x1, Pallas kernels, front(): pl.pallas_call(functools.partial(front_kernel, ctx), grid=(1 + groups,),...  78 us
    pallas_call x1, Pallas kernels, feed_forward(): pl.pallas_call(functools.partial(feed_forward_kernel, blocks), grid=(step...  53.2 us
    pallas_call x1, Pallas kernels, attention_backward(): pl.pallas_call(attention_backward_kernel, grid_spec=pltpu.PrefetchScalarG...  43.1 us
    psum x1, blocking collectives, per_device(): vectors = lax.psum(vectors, ('seq', 'ctx'))  40.2 us
    ppermute x40, starting transfers between devices, exchange(): return lax.ppermute(value, axis, [(i, i ^ 1 << bit) for i in range(size)])  32.6 us
    all_to_all x1, starting transfers between devices, per_device(): lax.all_to_all(grad_inputs.astype(BF16).reshape(shape), 'ctx', 0, 0, tile...  16.3 us
    convert_element_type x32, other arithmetic, halve(): return (kept.astype(F32) + got.astype(F32)).astype(BF16)  13.2 us
  transfers between devices with their start and end apart: 41, of which 21 were waited for; matrix products, arithmetic and copies ran while one was open for 12% of the time, Pallas kernels for 10%

profile of v2, /device:TPU:0, one launch (start us, length us, event | category | flops | bytes accessed | tf_op | source)
XLA Modules:
  0.0 451.9 jit_solution(866070903275398425)
XLA Ops:
  7.0 78.0 %front.1 = (bf16[4,256,768]{2,1,0:T(8,128)(2,1)}, bf16[1024,768]{1,0:T(8,128)(2,1)}, bf16[1024,2304]{1,0:T(8,128)(2,1)}, bf16[4,256,768]{2,1,0:T(8,128)(2,1)}, b...) custom-call(s32[1]{0:T(128)} %dynamic_slice.222.length_ref, bf16[4,256,768]{2,1,0:T(8,128)(2,1)} %tokens.1, ...), custom_call_target="tpu_custom_call" | custom-call | tf_op jit(solution)/shard_map/front/pallas_call | solution.py:200
  85.0 53.2 %feed_forward.1 = (bf16[4,256,768]{2,1,0:T(8,128)(2,1)}, f32[1024,768]{1,0:T(8,128)}, bf16[1024,768]{1,0:T(8,128)(2,1)}, bf16[3072,768]{1,0:T(8,128)(2,1)}, bf16...) custom-call(s32[1]{0:T(128)} %dynamic_slice.222.length_ref, ...), custom_call_target="tpu_custom_call" | custom-call | tf_op jit(solution)/shard_map/feed_forward/pallas_call | solution.py:344
  138.2 4.4 fusion.34
  142.6 2.6 dynamic-slice_bitcast_fusion.1
  153.4 43.1 %attention_backward.1 = (bf16[1024,768]{1,0:T(8,128)(2,1)}, bf16[1024,768]{1,0:T(8,128)(2,1)}, bf16[1024,768]{1,0:T(8,128)(2,1)}) custom-call(s32[1]{0:T(128)} %dynamic_slice.222.length_ref, bf16[1024,2304]{1,0:T(8,128)(2,1)} %get-tuple-element.31.q_ref.k_ref.v_ref, bf16[1024,2304]{1,0:T(8,128)(2,1)} %get-tuple-element.31.q_ref.k_ref.v_ref, ...), custom_call_target="tpu_custom_call" | custom-call | flops 40000000000 | bytes 12000000 | tf_op jit(solution)/shard_map/attention_backward/pallas_call | solution.py:448
  201.2 4.6 %multiply_reduce_fusion = (f32[768]{0:T(1024)S(1)}, f32[1024]{0:T(1024)S(1)}, f32[1024]{0:T(1024)S(1)}, f32[768]{0:T(1024)S(1)}, f32[1024,768]{1,0:T(8,128)S(1)}) fusion(bf16[4,256,768]{2,1,0:T(8,128)(2,1)S(1)} %copy-done, f32[1024]{0:T(1024)S(1)} %bitcast.292, f32[1024]{0:T(1024)S(1)} %bitcast.290, f32[768]{0:T(1024)S(1)} %copy-done.21, ...), kind=kOutput, calls=%fused_computation.3 | convolution fusion | flops 3631739392 | bytes 13001728 | tf_op jit(solution)/shard_map/dot_general | solution.py:28
  205.9 2.2 add_convert_fusion
  208.1 16.3 %all-to-all-start = ((bf16[4,256,768]{2,1,0:T(8,128)(2,1)}), bf16[4,256,768]{2,1,0:T(8,128)(2,1)}, u32[]{:S(2)}, u32[]{:S(2)}) async-start(bf16[4,256,768]{2,1,0:T(8,128)(2,1)} %bitcast.269), calls=%async_computation | async-start | bytes 3145728 | tf_op jit(solution)/shard_map/all_to_all | solution.py:562
  224.4 6.7 %convolution_convert_fusion = bf16[768,2304]{1,0:T(8,128)(2,1)S(1)} fusion(bf16[1024,768]{1,0:T(8,128)(2,1)} %get-tuple-element.37, bf16[1024,2304]{1,0:T(8,128)(2,1)} %copy-done.17), kind=kOutput, calls=%fused_computation | convolution fusion | flops 3625648128 | bytes 9830400 | tf_op jit(solution)/shard_map/dot_general | solution.py:28
  240.6 3.7 collective-permute-done.11
  245.9 3.9 collective-permute-done.14
  251.4 2.8 collective-permute-done.12
  255.7 2.8 collective-permute-done.15
  266.5 2.7 collective-permute-start.17
  269.9 40.2 %psum.7 = f32[4,768]{1,0:T(4,128)} all-reduce(f32[4,768]{1,0:T(4,128)S(1)} %pad_maximum_fusion.8), channel_id=1, replica_groups=mesh['seq'=8,'ctx'=4] {'seq','ctx'}, use_global_device_ids=true, to_apply=%region_6.0 | all-reduce | flops 3072 | bytes 24576 | tf_op jit(solution)/shard_map/psum | solution.py:564
  313.0 4.1 collective-permute-done.18
  320.0 3.8 collective-permute-done.19
  327.8 2.3 collective-permute-start.1
  341.1 2.5 collective-permute-start.24
  344.6 27.8 %collective-permute-done.2 = bf16[96,1152]{1,0:T(8,128)(2,1)S(1)} collective-permute-done((bf16[96,1152]{1,0:T(8,128)(2,1)S(1)}, bf16[96,1152]{1,0:T(8,128)(2,1)S(1)}, u32[]{:S(2)}, u32[]{:S(2)}) %collective-permute-start.2) | collective-permute-done | bytes 221216 | tf_op jit(solution)/shard_map/ppermute | solution.py:479
  373.2 5.6 %collective-permute-done.5 = bf16[96,1152]{1,0:T(8,128)(2,1)S(1)} collective-permute-done((bf16[96,1152]{1,0:T(8,128)(2,1)S(1)}, bf16[96,1152]{1,0:T(8,128)(2,1)S(1)}, u32[]{:S(2)}, u32[]{:S(2)}) %collective-permute-start.5) | collective-permute-done | bytes 221216 | tf_op jit(solution)/shard_map/ppermute | solution.py:479
  385.6 8.5 %collective-permute-done.7 = bf16[24,2304]{1,0:T(8,128)(2,1)S(1)} collective-permute-done((bf16[24,2304]{1,0:T(8,128)(2,1)S(1)}, bf16[24,2304]{1,0:T(8,128)(2,1)S(1)}, u32[]{:S(2)}, u32[]{:S(2)}) %collective-permute-start.7) | collective-permute-done | bytes 110624 | tf_op jit(solution)/shard_map/ppermute | solution.py:479
  395.2 5.1 %collective-permute-done.8 = bf16[24,2304]{1,0:T(8,128)(2,1)S(1)} collective-permute-done((bf16[24,2304]{1,0:T(8,128)(2,1)S(1)}, bf16[24,2304]{1,0:T(8,128)(2,1)S(1)}, u32[]{:S(2)}, u32[]{:S(2)}) %collective-permute-start.8) | collective-permute-done | bytes 110624 | tf_op jit(solution)/shard_map/ppermute | solution.py:479
  403.2 7.2 %collective-permute-done.9 = bf16[2,24,2304]{2,1,0:T(8,128)(2,1)S(1)} collective-permute-done((bf16[2,24,2304]{2,1,0:T(8,128)(2,1)S(1)}, bf16[2,24,2304]{2,1,0:T(8,128)(2,1)S(1)}, u32[]{:S(2)}, u32[]{:S(2)}) %collective-permute-start.9) | collective-permute-done | bytes 221216 | tf_op jit(solution)/shard_map/ppermute | solution.py:479
  411.4 2.5 collective-permute-done.36
  414.2 5.0 %collective-permute-done.26 = bf16[2,24,3072]{2,1,0:T(8,128)(2,1)S(1)} collective-permute-done((bf16[2,24,3072]{2,1,0:T(8,128)(2,1)S(1)}, bf16[2,24,3072]{2,1,0:T(8,128)(2,1)S(1)}, u32[]{:S(2)}, u32[]{:S(2)}) %collective-permute-start.26) | collective-permute-done | bytes 294944 | tf_op jit(solution)/shard_map/ppermute | solution.py:479
  420.0 7.4 %collective-permute-done.37 = bf16[96,768]{1,0:T(8,128)(2,1)S(1)} collective-permute-done((bf16[96,768]{1,0:T(8,128)(2,1)S(1)}, bf16[96,768]{1,0:T(8,128)(2,1)S(1)}, u32[]{:S(2)}, u32[]{:S(2)}) %collective-permute-start.37) | collective-permute-done | bytes 147488 | tf_op jit(solution)/shard_map/ppermute | solution.py:479
  427.5 2.8 collective-permute-done.27
  430.5 4.6 %collective-permute-done.38 = bf16[96,768]{1,0:T(8,128)(2,1)S(1)} collective-permute-done((bf16[96,768]{1,0:T(8,128)(2,1)S(1)}, bf16[96,768]{1,0:T(8,128)(2,1)S(1)}, u32[]{:S(2)}, u32[]{:S(2)}) %collective-permute-start.38) | collective-permute-done | bytes 147488 | tf_op jit(solution)/shard_map/ppermute | solution.py:479
  435.3 2.6 collective-permute-done.28
  438.0 4.9 %collective-permute-done.39 = bf16[2,96,768]{2,1,0:T(8,128)(2,1)S(1)} collective-permute-done((bf16[2,96,768]{2,1,0:T(8,128)(2,1)S(1)}, bf16[2,96,768]{2,1,0:T(8,128)(2,1)S(1)}, u32[]{:S(2)}, u32[]{:S(2)}) %collective-permute-start.39) | collective-permute-done | bytes 294944 | tf_op jit(solution)/shard_map/ppermute | solution.py:479
  449.1 2.7 copy.52
  (216 shorter events, 83.8 us)
Async XLA Ops:
  145.2 185.2 %collective-permute-start.30 = (bf16[2,2,384,384]{3,2,1,0:T(8,128)(2,1)}, bf16[2,2,384,384]{3,2,1,0:T(8,128)(2,1)}, u32[]{:S(2)}, u32[]{:S(2)}) collective-permute-start(bf16[2,2,384,384]{3,2,1,0:T(8,128)(2,1)} %dynamic-slice_bitcast_fusion.1), channel_id=1, source_target_pairs={{0,4},{4,0},{8,12},{12,8},{16,20},{20,16},{24,28},{28,24},{1,5},{5... | collective-permute-start | bytes 3538952 | tf_op jit(solution)/shard_map/ppermute | solution.py:479
  146.4 186.7 %collective-permute-start.33 = (bf16[2,2,384,384]{3,2,1,0:T(8,128)(2,1)}, bf16[2,2,384,384]{3,2,1,0:T(8,128)(2,1)}, u32[]{:S(2)}, u32[]{:S(2)}) collective-permute-start(bf16[2,2,384,384]{3,2,1,0:T(8,128)(2,1)} %dynamic-slice_bitcast_fusion), channel_id=1, source_target_pairs={{0,4},{4,0},{8,12},{12,8},{16,20},{20,16},{24,28},{28,24},{1,5},{5... | collective-permute-start | bytes 3538952 | tf_op jit(solution)/shard_map/ppermute | solution.py:479
  150.0 186.4 %collective-permute-start.20 = (bf16[2,2,96,1536]{3,2,1,0:T(8,128)(2,1)}, bf16[2,2,96,1536]{3,2,1,0:T(8,128)(2,1)}, u32[]{:S(2)}, u32[]{:S(2)}) collective-permute-start(bf16[2,2,96,1536]{3,2,1,0:T(8,128)(2,1)} %dynamic-slice_bitcast_fusion.3), channel_id=1, source_target_pairs={{0,4},{4,0},{8,12},{12,8},{16,20},{20,16},{24,28},{28,24},{1,5},{5... | collective-permute-start | bytes 3538952 | tf_op jit(solution)/shard_map/ppermute | solution.py:479
  151.9 85.0 %collective-permute-start.10 = (bf16[2,2,96,384]{3,2,1,0:T(8,128)(2,1)}, bf16[2,2,96,384]{3,2,1,0:T(8,128)(2,1)}, u32[]{:S(2)}, u32[]{:S(2)}) collective-permute-start(bf16[2,2,96,384]{3,2,1,0:T(8,128)(2,1)} %dynamic-slice_bitcast_fusion.19), channel_id=1, source_target_pairs={{0,4},{4,0},{8,12},{12,8},{16,20},{20,16},{24,28},{28,24},{1,5},{5... | collective-permute-start | bytes 884744 | tf_op jit(solution)/shard_map/ppermute | solution.py:479
  152.6 85.4 %collective-permute-start.13 = (bf16[2,2,96,384]{3,2,1,0:T(8,128)(2,1)}, bf16[2,2,96,384]{3,2,1,0:T(8,128)(2,1)}, u32[]{:S(2)}, u32[]{:S(2)}) collective-permute-start(bf16[2,2,96,384]{3,2,1,0:T(8,128)(2,1)} %dynamic-slice_bitcast_fusion.18), channel_id=1, source_target_pairs={{0,4},{4,0},{8,12},{12,8},{16,20},{20,16},{24,28},{28,24},{1,5},{5... | collective-permute-start | bytes 884744 | tf_op jit(solution)/shard_map/ppermute | solution.py:479
  208.1 211.9 %all-to-all-start = ((bf16[4,256,768]{2,1,0:T(8,128)(2,1)}), bf16[4,256,768]{2,1,0:T(8,128)(2,1)}, u32[]{:S(2)}, u32[]{:S(2)}) async-start(bf16[4,256,768]{2,1,0:T(8,128)(2,1)} %bitcast.269), calls=%async_computation | async-start | bytes 3145728 | tf_op jit(solution)/shard_map/all_to_all | solution.py:562
  236.9 88.6 %collective-permute-start = (bf16[2,2,96,1152]{3,2,1,0:T(8,128)(2,1)}, bf16[2,2,96,1152]{3,2,1,0:T(8,128)(2,1)}, u32[]{:S(2)}, u32[]{:S(2)}) collective-permute-start(bf16[2,2,96,1152]{3,2,1,0:T(8,128)(2,1)} %dynamic-slice_bitcast_fusion.5), channel_id=1, source_target_pairs={{0,4},{4,0},{8,12},{12,8},{16,20},{20,16},{24,28},{28,24},{1,5},{5... | collective-permute-start | bytes 2654216 | tf_op jit(solution)/shard_map/ppermute | solution.py:479
  238.0 6.3 %collective-permute-start.11 = (bf16[2,96,384]{2,1,0:T(8,128)(2,1)S(1)}, bf16[2,96,384]{2,1,0:T(8,128)(2,1)S(1)}, u32[]{:S(2)}, u32[]{:S(2)}) collective-permute-start(bf16[2,96,384]{2,1,0:T(8,128)(2,1)S(1)} %dynamic-slice_bitcast_fusion.26), channel_id=1, source_target_pairs={{0,8},{4,12},{8,0},{12,4},{16,24},{20,28},{24,16},{28,20},{1,9},{5... | collective-permute-start | bytes 442376 | tf_op jit(solution)/shard_map/ppermute | solution.py:479
  266.5 43.6 %collective-permute-start.17 = (bf16[24,768]{1,0:T(8,128)(2,1)}, bf16[24,768]{1,0:T(8,128)(2,1)}, u32[]{:S(2)}, u32[]{:S(2)}) collective-permute-start(bf16[24,768]{1,0:T(8,128)(2,1)} %dynamic-slice_bitcast_fusion.31), channel_id=1, source_target_pairs={{0,2},{1,3},{2,0},{3,1},{4,6},{5,7},{6,4},{7,5},{8,10},{9,11},{10,... | collective-permute-start | bytes 110600 | tf_op jit(solution)/shard_map/ppermute | solution.py:479
  325.5 12.9 %collective-permute-start.23 = (bf16[2,2,96,1536]{3,2,1,0:T(8,128)(2,1)S(1)}, bf16[2,2,96,1536]{3,2,1,0:T(8,128)(2,1)S(1)}, u32[]{:S(2)}, u32[]{:S(2)}) collective-permute-start(bf16[2,2,96,1536]{3,2,1,0:T(8,128)(2,1)S(1)} %copy-done.14), channel_id=1, source_target_pairs={{0,4},{4,0},{8,12},{12,8},{16,20},{20,16},{24,28},{28,24},{1,5},{5... | collective-permute-start | bytes 3538952 | tf_op jit(solution)/shard_map/ppermute | solution.py:479
  327.8 13.3 %collective-permute-start.1 = (bf16[2,96,1152]{2,1,0:T(8,128)(2,1)S(1)}, bf16[2,96,1152]{2,1,0:T(8,128)(2,1)S(1)}, u32[]{:S(2)}, u32[]{:S(2)}) collective-permute-start(bf16[2,96,1152]{2,1,0:T(8,128)(2,1)S(1)} %dynamic-slice_bitcast_fusion.11), channel_id=1, source_target_pairs={{0,8},{4,12},{8,0},{12,4},{16,24},{20,28},{24,16},{28,20},{1,9},{5... | collective-permute-start | bytes 1327112 | tf_op jit(solution)/shard_map/ppermute | solution.py:479
  330.4 13.3 %collective-permute-start.4 = (bf16[2,96,1152]{2,1,0:T(8,128)(2,1)S(1)}, bf16[2,96,1152]{2,1,0:T(8,128)(2,1)S(1)}, u32[]{:S(2)}, u32[]{:S(2)}) collective-permute-start(bf16[2,96,1152]{2,1,0:T(8,128)(2,1)S(1)} %dynamic-slice_bitcast_fusion.10), channel_id=1, source_target_pairs={{0,16},{4,20},{8,24},{12,28},{16,0},{20,4},{24,8},{28,12},{1,17},{... | collective-permute-start | bytes 1327112 | tf_op jit(solution)/shard_map/ppermute | solution.py:479
  333.1 46.2 %collective-permute-start.31 = (bf16[2,384,384]{2,1,0:T(8,128)(2,1)S(1)}, bf16[2,384,384]{2,1,0:T(8,128)(2,1)S(1)}, u32[]{:S(2)}, u32[]{:S(2)}) collective-permute-start(bf16[2,384,384]{2,1,0:T(8,128)(2,1)S(1)} %dynamic-slice_bitcast_fusion.7), channel_id=1, source_target_pairs={{0,8},{4,12},{8,0},{12,4},{16,24},{20,28},{24,16},{28,20},{1,9},{5... | collective-permute-start | bytes 1769480 | tf_op jit(solution)/shard_map/ppermute | solution.py:479
  336.3 44.2 %collective-permute-start.34 = (bf16[2,384,384]{2,1,0:T(8,128)(2,1)S(1)}, bf16[2,384,384]{2,1,0:T(8,128)(2,1)S(1)}, u32[]{:S(2)}, u32[]{:S(2)}) collective-permute-start(bf16[2,384,384]{2,1,0:T(8,128)(2,1)S(1)} %dynamic-slice_bitcast_fusion.6), channel_id=1, source_target_pairs={{0,16},{4,20},{8,24},{12,28},{16,0},{20,4},{24,8},{28,12},{1,17},{... | collective-permute-start | bytes 1769480 | tf_op jit(solution)/shard_map/ppermute | solution.py:479
  338.4 43.9 %collective-permute-start.21 = (bf16[2,96,1536]{2,1,0:T(8,128)(2,1)S(1)}, bf16[2,96,1536]{2,1,0:T(8,128)(2,1)S(1)}, u32[]{:S(2)}, u32[]{:S(2)}) collective-permute-start(bf16[2,96,1536]{2,1,0:T(8,128)(2,1)S(1)} %dynamic-slice_bitcast_fusion.9), channel_id=1, source_target_pairs={{0,8},{4,12},{8,0},{12,4},{16,24},{20,28},{24,16},{28,20},{1,9},{5... | collective-permute-start | bytes 1769480 | tf_op jit(solution)/shard_map/ppermute | solution.py:479
  341.1 44.4 %collective-permute-start.24 = (bf16[2,96,1536]{2,1,0:T(8,128)(2,1)S(1)}, bf16[2,96,1536]{2,1,0:T(8,128)(2,1)S(1)}, u32[]{:S(2)}, u32[]{:S(2)}) collective-permute-start(bf16[2,96,1536]{2,1,0:T(8,128)(2,1)S(1)} %dynamic-slice_bitcast_fusion.8), channel_id=1, source_target_pairs={{0,16},{4,20},{8,24},{12,28},{16,0},{20,4},{24,8},{28,12},{1,17},{... | collective-permute-start | bytes 1769480 | tf_op jit(solution)/shard_map/ppermute | solution.py:479
  343.7 28.7 %collective-permute-start.2 = (bf16[96,1152]{1,0:T(8,128)(2,1)S(1)}, bf16[96,1152]{1,0:T(8,128)(2,1)S(1)}, u32[]{:S(2)}, u32[]{:S(2)}) collective-permute-start(bf16[96,1152]{1,0:T(8,128)(2,1)S(1)} %dynamic-slice_bitcast_fusion.22), channel_id=1, source_target_pairs={{0,16},{4,20},{8,24},{12,28},{16,0},{20,4},{24,8},{28,12},{1,17},{... | collective-permute-start | bytes 663560 | tf_op jit(solution)/shard_map/ppermute | solution.py:479
  372.4 6.3 %collective-permute-start.5 = (bf16[96,1152]{1,0:T(8,128)(2,1)S(1)}, bf16[96,1152]{1,0:T(8,128)(2,1)S(1)}, u32[]{:S(2)}, u32[]{:S(2)}) collective-permute-start(bf16[96,1152]{1,0:T(8,128)(2,1)S(1)} %dynamic-slice_bitcast_fusion.21), channel_id=1, source_target_pairs={{0,8},{4,12},{8,0},{12,4},{16,24},{20,28},{24,16},{28,20},{1,9},{5... | collective-permute-start | bytes 663560 | tf_op jit(solution)/shard_map/ppermute | solution.py:479
  379.5 20.9 %collective-permute-start.32 = (bf16[384,384]{1,0:T(8,128)(2,1)S(1)}, bf16[384,384]{1,0:T(8,128)(2,1)S(1)}, u32[]{:S(2)}, u32[]{:S(2)}) collective-permute-start(bf16[384,384]{1,0:T(8,128)(2,1)S(1)} %dynamic-slice_bitcast_fusion.14), channel_id=1, source_target_pairs={{0,16},{4,20},{8,24},{12,28},{16,0},{20,4},{24,8},{28,12},{1,17},{... | collective-permute-start | bytes 884744 | tf_op jit(solution)/shard_map/ppermute | solution.py:479
  380.8 19.7 %collective-permute-start.35 = (bf16[384,384]{1,0:T(8,128)(2,1)S(1)}, bf16[384,384]{1,0:T(8,128)(2,1)S(1)}, u32[]{:S(2)}, u32[]{:S(2)}) collective-permute-start(bf16[384,384]{1,0:T(8,128)(2,1)S(1)} %dynamic-slice_bitcast_fusion.13), channel_id=1, source_target_pairs={{0,8},{4,12},{8,0},{12,4},{16,24},{20,28},{24,16},{28,20},{1,9},{5... | collective-permute-start | bytes 884744 | tf_op jit(solution)/shard_map/ppermute | solution.py:479
  382.5 20.3 %collective-permute-start.22 = (bf16[96,1536]{1,0:T(8,128)(2,1)S(1)}, bf16[96,1536]{1,0:T(8,128)(2,1)S(1)}, u32[]{:S(2)}, u32[]{:S(2)}) collective-permute-start(bf16[96,1536]{1,0:T(8,128)(2,1)S(1)} %dynamic-slice_bitcast_fusion.17), channel_id=1, source_target_pairs={{0,16},{4,20},{8,24},{12,28},{16,0},{20,4},{24,8},{28,12},{1,17},{... | collective-permute-start | bytes 884744 | tf_op jit(solution)/shard_map/ppermute | solution.py:479
  385.0 9.1 %collective-permute-start.7 = (bf16[24,2304]{1,0:T(8,128)(2,1)S(1)}, bf16[24,2304]{1,0:T(8,128)(2,1)S(1)}, u32[]{:S(2)}, u32[]{:S(2)}) collective-permute-start(bf16[24,2304]{1,0:T(8,128)(2,1)S(1)} %dynamic-slice_bitcast_fusion.27), channel_id=1, source_target_pairs={{0,2},{1,3},{2,0},{3,1},{4,6},{5,7},{6,4},{7,5},{8,10},{9,11},{10,... | collective-permute-start | bytes 331784 | tf_op jit(solution)/shard_map/ppermute | solution.py:479
  394.3 8.6 %collective-permute-start.25 = (bf16[96,1536]{1,0:T(8,128)(2,1)S(1)}, bf16[96,1536]{1,0:T(8,128)(2,1)S(1)}, u32[]{:S(2)}, u32[]{:S(2)}) collective-permute-start(bf16[96,1536]{1,0:T(8,128)(2,1)S(1)} %dynamic-slice_bitcast_fusion.16), channel_id=1, source_target_pairs={{0,8},{4,12},{8,0},{12,4},{16,24},{20,28},{24,16},{28,20},{1,9},{5... | collective-permute-start | bytes 884744 | tf_op jit(solution)/shard_map/ppermute | solution.py:479
  400.3 10.0 %collective-permute-start.9 = (bf16[2,24,2304]{2,1,0:T(8,128)(2,1)S(1)}, bf16[2,24,2304]{2,1,0:T(8,128)(2,1)S(1)}, u32[]{:S(2)}, u32[]{:S(2)}) collective-permute-start(bf16[2,24,2304]{2,1,0:T(8,128)(2,1)S(1)} %pad_maximum_fusion.5), channel_id=1, source_target_pairs={{0,1},{1,0},{2,3},{3,2},{4,5},{5,4},{6,7},{7,6},{8,9},{9,8},{10,11... | collective-permute-start | bytes 663560 | tf_op jit(solution)/shard_map/ppermute | solution.py:479
  400.7 13.2 %collective-permute-start.36 = (bf16[2,96,768]{2,1,0:T(8,128)(2,1)S(1)}, bf16[2,96,768]{2,1,0:T(8,128)(2,1)S(1)}, u32[]{:S(2)}, u32[]{:S(2)}) collective-permute-start(bf16[2,96,768]{2,1,0:T(8,128)(2,1)S(1)} %dynamic-slice_bitcast_fusion.12), channel_id=1, source_target_pairs={{0,1},{1,0},{2,3},{3,2},{4,5},{5,4},{6,7},{7,6},{8,9},{9,8},{10,11... | collective-permute-start | bytes 884744 | tf_op jit(solution)/shard_map/ppermute | solution.py:479
  403.1 16.1 %collective-permute-start.26 = (bf16[2,24,3072]{2,1,0:T(8,128)(2,1)S(1)}, bf16[2,24,3072]{2,1,0:T(8,128)(2,1)S(1)}, u32[]{:S(2)}, u32[]{:S(2)}) collective-permute-start(bf16[2,24,3072]{2,1,0:T(8,128)(2,1)S(1)} %dynamic-slice_bitcast_fusion.15), channel_id=1, source_target_pairs={{0,1},{1,0},{2,3},{3,2},{4,5},{5,4},{6,7},{7,6},{8,9},{9,8},{10,11... | collective-permute-start | bytes 884744 | tf_op jit(solution)/shard_map/ppermute | solution.py:479
  414.0 13.4 %collective-permute-start.37 = (bf16[96,768]{1,0:T(8,128)(2,1)S(1)}, bf16[96,768]{1,0:T(8,128)(2,1)S(1)}, u32[]{:S(2)}, u32[]{:S(2)}) collective-permute-start(bf16[96,768]{1,0:T(8,128)(2,1)S(1)} %dynamic-slice_bitcast_fusion.23), channel_id=1, source_target_pairs={{0,2},{1,3},{2,0},{3,1},{4,6},{5,7},{6,4},{7,5},{8,10},{9,11},{10,... | collective-permute-start | bytes 442376 | tf_op jit(solution)/shard_map/ppermute | solution.py:479
  419.3 11.0 %collective-permute-start.27 = (bf16[24,3072]{1,0:T(8,128)(2,1)S(1)}, bf16[24,3072]{1,0:T(8,128)(2,1)S(1)}, u32[]{:S(2)}, u32[]{:S(2)}) collective-permute-start(bf16[24,3072]{1,0:T(8,128)(2,1)S(1)} %dynamic-slice_bitcast_fusion.24), channel_id=1, source_target_pairs={{0,2},{1,3},{2,0},{3,1},{4,6},{5,7},{6,4},{7,5},{8,10},{9,11},{10,... | collective-permute-start | bytes 442376 | tf_op jit(solution)/shard_map/ppermute | solution.py:479
  427.4 7.7 %collective-permute-start.38 = (bf16[96,768]{1,0:T(8,128)(2,1)S(1)}, bf16[96,768]{1,0:T(8,128)(2,1)S(1)}, u32[]{:S(2)}, u32[]{:S(2)}) collective-permute-start(bf16[96,768]{1,0:T(8,128)(2,1)S(1)} %fusion.24), channel_id=1, source_target_pairs={{0,2},{1,3},{2,0},{3,1},{4,6},{5,7},{6,4},{7,5},{8,10},{9,11},{10,... | collective-permute-start | bytes 442376 | tf_op jit(solution)/shard_map/ppermute | solution.py:479
  430.4 7.5 %collective-permute-start.28 = (bf16[24,3072]{1,0:T(8,128)(2,1)S(1)}, bf16[24,3072]{1,0:T(8,128)(2,1)S(1)}, u32[]{:S(2)}, u32[]{:S(2)}) collective-permute-start(bf16[24,3072]{1,0:T(8,128)(2,1)S(1)} %fusion.25), channel_id=1, source_target_pairs={{0,2},{1,3},{2,0},{3,1},{4,6},{5,7},{6,4},{7,5},{8,10},{9,11},{10,... | collective-permute-start | bytes 442376 | tf_op jit(solution)/shard_map/ppermute | solution.py:479
  435.2 7.7 %collective-permute-start.39 = (bf16[2,96,768]{2,1,0:T(8,128)(2,1)S(1)}, bf16[2,96,768]{2,1,0:T(8,128)(2,1)S(1)}, u32[]{:S(2)}, u32[]{:S(2)}) collective-permute-start(bf16[2,96,768]{2,1,0:T(8,128)(2,1)S(1)} %pad_maximum_fusion.4), channel_id=1, source_target_pairs={{0,1},{1,0},{2,3},{3,2},{4,5},{5,4},{6,7},{7,6},{8,9},{9,8},{10,11... | collective-permute-start | bytes 884744 | tf_op jit(solution)/shard_map/ppermute | solution.py:479
  437.9 8.2 %collective-permute-start.29 = (bf16[2,24,3072]{2,1,0:T(8,128)(2,1)S(1)}, bf16[2,24,3072]{2,1,0:T(8,128)(2,1)S(1)}, u32[]{:S(2)}, u32[]{:S(2)}) collective-permute-start(bf16[2,24,3072]{2,1,0:T(8,128)(2,1)S(1)} %pad_maximum_fusion.3), channel_id=1, source_target_pairs={{0,1},{1,0},{2,3},{3,2},{4,5},{5,4},{6,7},{7,6},{8,9},{9,8},{10,11... | collective-permute-start | bytes 884744 | tf_op jit(solution)/shard_map/ppermute | solution.py:479
  (31 other events, 187.5 us)

commit v3 on v2

--- a/solution.py
+++ b/solution.py
@@ -19,6 +19,7 @@
 MESH = pl.DeviceIdType.MESH
 epsilon = 1e-05
 MIB = 2**20
+VMEM_LIMIT = 62 * MIB
 ANY = pl.BlockSpec(memory_space=pl.ANY)
 SMEM = pl.BlockSpec(memory_space=pltpu.SMEM)
 ONE = pl.Buffered(1)
@@ -381,11 +382,288 @@
     )(length, *operands)
 
 
-def attention_backward_kernel(
-    length_ref, q_ref, k_ref, v_ref, mixed_ref, grad_ref, log_ref,
-    grad_q_ref, grad_k_ref, grad_v_ref, k_t, grad_q_t, probs_low, grads_low, sum_k, sum_v,
+PARTS = 3
+KINDS = 8
+
+
+class Chunk:
+    def __init__(self, source, own, stages, send, recv, local, places):
+        self.source, self.own = source, own
+        self.r1, self.r2a, self.r2b, self.r3, self.z1, self.z2, self.out = stages
+        self.send, self.recv, self.local, self.places = send, recv, local, places
+        self.cut = self.r3.shape[-1] // 2
+
+    def copy(self, kind):
+        seq, ctx, core, x, y, low = self.places
+        cut = self.cut
+        ways = (
+            lambda: (self.source.at[:, :, 1 - core], self.r1, {"seq": seq ^ 1}),
+            lambda: (self.r1.at[:, 1 - x, :, :, 0:cut], self.r2a, {"seq": seq ^ 2}),
+            lambda: (self.r1.at[1 - y, :, :, :, cut:], self.r2b, {"seq": seq ^ 4}),
+            lambda: (self.r2a.at[1 - y], self.r3.at[:, :, 0:cut], {"seq": seq ^ 4}),
+            lambda: (self.r2b.at[1 - x], self.r3.at[:, :, cut:], {"seq": seq ^ 2}),
+            lambda: (self.r3.at[1 - low], self.z1, {"ctx": ctx ^ 1}),
+            lambda: (self.z1, self.z2, {"ctx": ctx ^ 2}),
+            lambda: (self.out.at[low], self.out.at[low], {"ctx": ctx ^ 1}),
+        )
+        source, target, partner = ways[kind]()
+        return to_partner(source, target, self.send.at[kind], self.recv.at[kind], partner)
+
+    def own_copy(self):
+        core = self.places[2]
+        return pltpu.make_async_copy(self.source.at[:, :, core], self.own, self.local)
+
+    def event(self, number):
+        seq, ctx, core, x, y, low = self.places
+        cut = self.cut
+        if number == 0:
+            self.copy(0).start()
+            if self.own is not None:
+                self.own_copy().start()
+        if number == 1:
+            self.copy(0).wait_recv()
+            if self.own is not None:
+                self.own_copy().wait()
+            for along_y in range(2):
+                for along_x in range(2):
+                    if self.own is not None:
+                        kept = self.own[along_y, along_x]
+                    else:
+                        kept = self.source[along_y, along_x, core]
+                    self.r1[along_y, along_x] += kept
+            self.copy(1).start()
+            self.copy(2).start()
+        if number == 2:
+            self.copy(1).wait_recv()
+            self.copy(2).wait_recv()
+            for other in range(2):
+                self.r2a[other] += self.r1[other, x, :, :, 0:cut]
+                self.r2b[other] += self.r1[y, other, :, :, cut:]
+            self.copy(3).start()
+            self.copy(4).start()
+        if number == 3:
+            self.copy(3).wait_recv()
+            self.copy(4).wait_recv()
+            self.r3[:, :, 0:cut] += self.r2a[y]
+            self.r3[:, :, cut:] += self.r2b[x]
+            self.copy(5).start()
+        if number == 4:
+            self.copy(5).wait_recv()
+            self.z1[...] += self.r3[low]
+            self.copy(6).start()
+        if number == 5:
+            self.copy(6).wait_recv()
+            self.out[low] = self.z1[...] + self.z2[...]
+            self.copy(7).start()
+        if number == 6:
+            to_partner(
+                self.out.at[1 - low], self.out.at[1 - low], self.send.at[7], self.recv.at[7],
+                {"ctx": ctx ^ 1},
+            ).wait_recv()
+            for kind in range(KINDS):
+                self.copy(kind).wait_send()
+
+
+def chunk_scratch(rows, columns, held):
+    shapes = [
+        (2, 2, 2, rows, columns),
+        (2, 2, rows, columns // 2),
+        (2, 2, rows, columns // 2),
+        (2, rows, columns),
+        (rows, columns),
+        (rows, columns),
+        (2, rows, columns),
+    ]
+    if held:
+        shapes.insert(0, (2, 2, 2, rows, columns))
+    return [pltpu.VMEM(shape, BF16) for shape in shapes]
+
+
+PLAN = {
+    (0, 0): [(0, 0)],
+    (0, 3): [(1, 0), (2, 0)],
+    (1, 0): [(0, 1)],
+    (2, 0): [(3, 0)],
+    (2, 3): [(0, 2), (1, 1)],
+    (3, 0): [(2, 1), (3, 1)],
+    (4, 0): [(4, 0)],
+    (4, 1): [(0, 3)],
+    (4, 3): [(2, 2), (3, 2), (4, 1)],
+    (5, 0): [(0, 4)],
+    (5, 1): [(1, 2)],
+    (5, 3): [(2, 3), (3, 3)],
+}
+PLAN_BEFORE_NORM = [(5, 0), (4, 2), (1, 3), (0, 5), (2, 4), (3, 4)]
+PLAN_AFTER_NORM = [
+    "v0", (5, 1), (4, 3), "v1", (2, 5), (3, 5), (1, 4), "v2", (5, 2), (4, 4), "v3", (0, 6), (1, 5),
+    (5, 3), (4, 5), (5, 4), "v4", (2, 6), (3, 6), (1, 6), (5, 5), (4, 6), (5, 6), "v5",
+]
+
+
+def back_kernel(
+    fast, ctx, length_ref, q_ref, k_ref, v_ref, mixed_ref, grad_ref, log_ref, inputs_in, normed_in,
+    middle_in, weight_in, gain, norm_two, *rest,
 ):
-    length = length_ref[0]
+    rest = list(rest)
+    take = lambda count: [rest.pop(0) for _ in range(count)]
+    sources = take(3) if fast else []
+    (grad_tokens,) = take(1)
+    results = take(4) if fast else take(1)
+    (vector_out,) = take(1)
+    (inputs, normed, middle, weight, grad_normed, pair, partial, staged) = take(8)
+    (k_t, grad_q_t, probs_low, grads_low, sum_k, sum_v) = take(6)
+    (vectors, vectors_got, local, token_send, token_recv, v_send, v_recv) = take(7)
+    step = pl.program_id(0)
+    seq, me = lax.axis_index("seq"), lax.axis_index("ctx")
+    rows, width = normed.shape
+    blocks, block = staged.shape[0], staged.shape[1]
+    groups = width // LANES
+    chunks = []
+    if fast:
+        send, recv = take(2)
+        places = (seq, me, seq % 2, (seq // 2) % 2, seq // 4, me % 2)
+        for number in range(3 + PARTS):
+            held = number < 3
+            own = take(1)[0] if held else None
+            source = sources[number] if held else partial.at[number - 3]
+            chunks.append(
+                Chunk(
+                    source, own, take(7), send.at[number], recv.at[number],
+                    local.at[5 + number], places,
+                )
+            )
+
+    def run(name):
+        if not fast:
+            return
+        if isinstance(name, tuple):
+            chunks[name[0]].event(name[1])
+            return
+        number = int(name[1:])
+        partners = [{"seq": seq ^ 1}, {"seq": seq ^ 2}, {"seq": seq ^ 4}]
+        partners += [{"ctx": me ^ 1}, {"ctx": me ^ 2}]
+        exchange = lambda n: to_partner(
+            vectors.at[n], vectors_got.at[n], v_send.at[n], v_recv.at[n], partners[n]
+        )
+        if number:
+            exchange(number - 1).wait()
+            vectors[number] = vectors[number - 1] + vectors_got[number - 1]
+        if number < len(partners):
+            exchange(number).start()
+
+    loads = [
+        pltpu.make_async_copy(inputs_in, inputs, local.at[0]),
+        pltpu.make_async_copy(normed_in, normed, local.at[1]),
+        pltpu.make_async_copy(middle_in, middle, local.at[2]),
+        pltpu.make_async_copy(weight_in, weight, local.at[3]),
+    ]
+
+    @pl.when(step == 0)
+    def _():
+        partners = [{"ctx": me ^ offset} for offset in range(1, ctx)]
+        if fast:
+            partners += [{"seq": seq ^ 1}, {"seq": seq ^ 2}, {"seq": seq ^ 4}]
+        greet(partners)
+        for load in loads:
+            load.start()
+
+    def hook(i):
+        for group in range(groups):
+            if (group, i) in PLAN:
+
+                @pl.when(step == group)
+                def _():
+                    for name in PLAN[group, i]:
+                        run(name)
+
+    @pl.when(step < groups)
+    def _():
+        side = pl.ds(pl.multiple_of((step % 2) * LANES, LANES), LANES)
+        attend_backward(
+            hook, side, length_ref[0], q_ref, k_ref, v_ref, mixed_ref, grad_ref, log_ref, pair,
+            k_t, grad_q_t, probs_low, grads_low, sum_k, sum_v,
+        )
+
+    @pl.when(step == 1)
+    def _():
+        for load in loads:
+            load.wait()
+        grad_normed[...] = jnp.zeros_like(grad_normed)
+
+    @pl.when((step < groups) & (step % 2 == 1))
+    def _():
+        part = step // 2
+        for name in range(PARTS):
+            columns = slice(name * 2 * LANES, (name + 1) * 2 * LANES)
+            product = dot(normed[...], pair[name], 0, 0).astype(BF16)
+            if fast:
+                partial[part, :, :, :, :, :, columns] = product.reshape(
+                    2, 2, 2, 2, width // 16, 2 * LANES
+                )
+            else:
+                partial[part, :, columns] = product
+            there = pl.ds(
+                pl.multiple_of(name * width + part * 2 * LANES, 2 * LANES), 2 * LANES
+            )
+            grad_normed[...] += dot(pair[name], weight[:, there], 1, 1)
+
+    def token_copy(row):
+        return to_partner(
+            staged.at[row], grad_tokens.at[me], token_send.at[row], token_recv.at[me], {"ctx": row}
+        )
+
+    own_tokens = pltpu.make_async_copy(staged.at[me], grad_tokens.at[me], local.at[4])
+
+    @pl.when(step == groups)
+    def _():
+        for name in PLAN_BEFORE_NORM:
+            run(name)
+        gain_sum, shift_sum = 0.0, 0.0
+        for row in range(blocks):
+            there = slice(row * block, (row + 1) * block)
+            hat, inverse = normalise(inputs[row].astype(F32))
+            grad = grad_normed[there, :]
+            gain_sum = gain_sum + jnp.sum(grad * hat, axis=0, keepdims=True)
+            shift_sum = shift_sum + jnp.sum(grad, axis=0, keepdims=True)
+            total = middle[there, :] + normalise_backward(grad, hat, inverse, gain[...])
+            staged[row] = total.astype(BF16)
+
+            @pl.when(row != me)
+            def _():
+                token_copy(row).start()
+
+            @pl.when(row == me)
+            def _():
+                own_tokens.start()
+
+        vectors[0] = jnp.concatenate([gain_sum, shift_sum, norm_two[0:6, :]], axis=0)
+        for name in PLAN_AFTER_NORM:
+            run(name)
+        if fast:
+            for number in range(3):
+                results[number][...] = chunks[number].out[...]
+            for number in range(PARTS):
+                results[3][number] = chunks[3 + number].out[...]
+            vector_out[...] = vectors[5]
+        else:
+            results[0][...] = partial[...]
+            vector_out[...] = vectors[0]
+        own_tokens.wait()
+        for row in range(blocks):
+
+            @pl.when(row != me)
+            def _():
+                token_copy(row).wait_send()
+                to_partner(
+                    staged.at[row], grad_tokens.at[row], token_send.at[row], token_recv.at[row],
+                    {"ctx": row},
+                ).wait_recv()
+
+
+def attend_backward(
+    hook, side, length, q_ref, k_ref, v_ref, mixed_ref, grad_ref, log_ref, pair,
+    k_t, grad_q_t, probs_low, grads_low, sum_k, sum_v,
+):
     count = q_ref.shape[0] // BLOCK
     k_t[...] = k_ref[...].T
 
@@ -412,6 +690,8 @@
     for number, (i, head) in enumerate(steps):
         below = i * BLOCK
         span = below + BLOCK
+        if head == 0:
+            hook(i)
         following = products_of(*steps[number + 1]) if number + 1 < len(steps) else None
         scores, grad_probs = current
         scores = mask_diagonal(scores, BLOCK, below, length)
@@ -424,7 +704,7 @@
             k_t[head * HD : (head + 1) * HD, 0:span], grad_scores, 1, 0
         )
         if head == HEADS - 1:
-            grad_q_ref[below:span, :] = (grad_q_t[...].T * SCALE).astype(BF16)
+            pair[0, below:span, side] = (grad_q_t[...].T * SCALE).astype(BF16)
             grad_v = dot(probs_low[0:span, :], jnp.concatenate(prepared[i][1], 0), 1, 0)
             grad_k = dot(grads_low[0:span, :], jnp.concatenate(prepared[i][0], 0), 1, 0)
             if below:
@@ -433,46 +713,84 @@
             sum_v[below:span, :] = grad_v[below:]
             sum_k[below:span, :] = grad_k[below:]
         current = following
-    grad_k_ref[...] = (sum_k[...] * SCALE).astype(BF16)
-    grad_v_ref[...] = sum_v[...].astype(BF16)
-
-
-def column_blocks(rows, first):
-    return pl.BlockSpec((rows, LANES), lambda group, length: (0, first + group))
-
-
-def attention_backward(length, packed, mixed, grad_mixed, logs):
+    pair[1, :, side] = (sum_k[...] * SCALE).astype(BF16)
+    pair[2, :, side] = sum_v[...].astype(BF16)
+
+
+def back(
+    fast, ctx, length, packed, mixed, grad_mixed, logs, inputs, normed, middle, weight, gain,
+    norm_two, partials,
+):
     rows, width = mixed.shape
+    blocks, block, _ = inputs.shape
     groups = width // LANES
-    blocks = lambda part: column_blocks(rows, part * groups)
+    group_of = lambda step: jnp.minimum(step, groups - 1)
+    columns = lambda part: pl.BlockSpec(
+        (rows, LANES), lambda step: (0, part * groups + group_of(step))
+    )
+    if fast:
+        lead = (2, 2, 2, 2)
+        partials = [
+            grad.reshape(lead + (grad.shape[0] // 16, grad.shape[1])) for grad in partials
+        ]
+        sizes = [grad.shape[-2:] for grad in partials] + [(width // 16, width)] * PARTS
+        reduced = [(2,) + size for size in sizes[:3]] + [(PARTS, 2, width // 16, width)]
+        held = [PARTS] + list(lead) + [width // 16, width]
+        extra = [
+            pltpu.SemaphoreType.DMA((len(sizes), KINDS)),
+            pltpu.SemaphoreType.DMA((len(sizes), KINDS)),
+        ]
+        for number, size in enumerate(sizes):
+            extra += chunk_scratch(*size, held=number < 3)
+    else:
+        partials = []
+        reduced = [(PARTS, width, width)]
+        held = [PARTS, width, width]
+        extra = []
+    scratch = [
+        pltpu.VMEM(inputs.shape, BF16),
+        pltpu.VMEM((rows, width), BF16),
+        pltpu.VMEM((rows, width), F32),
+        pltpu.VMEM(weight.shape, BF16),
+        pltpu.VMEM((rows, width), F32),
+        pltpu.VMEM((PARTS, rows, 2 * LANES), BF16),
+        pltpu.VMEM(tuple(held), BF16),
+        pltpu.VMEM(inputs.shape, BF16),
+        pltpu.VMEM((LANES, rows), BF16),
+        pltpu.VMEM((LANES, BLOCK), F32),
+        pltpu.VMEM((rows, HEADS * BLOCK), BF16),
+        pltpu.VMEM((rows, HEADS * BLOCK), BF16),
+        pltpu.VMEM((rows, LANES), F32),
+        pltpu.VMEM((rows, LANES), F32),
+        pltpu.VMEM((6, 8, width), F32),
+        pltpu.VMEM((5, 8, width), F32),
+        pltpu.SemaphoreType.DMA((5 + 3 + PARTS,)),
+        pltpu.SemaphoreType.DMA((blocks,)),
+        pltpu.SemaphoreType.DMA((blocks,)),
+        pltpu.SemaphoreType.DMA((5,)),
+        pltpu.SemaphoreType.DMA((5,)),
+    ]
     return pl.pallas_call(
-        attention_backward_kernel,
-        grid_spec=pltpu.PrefetchScalarGridSpec(
-            num_scalar_prefetch=1,
-            grid=(groups,),
-            in_specs=[
-                blocks(0),
-                blocks(1),
-                blocks(2),
-                blocks(0),
-                blocks(0),
-                pl.BlockSpec((1, HEADS, rows), lambda group, length: (group, 0, 0)),
-            ],
-            out_specs=[blocks(0)] * 3,
-            scratch_shapes=[
-                pltpu.VMEM((LANES, rows), BF16),
-                pltpu.VMEM((LANES, BLOCK), F32),
-                pltpu.VMEM((rows, HEADS * BLOCK), BF16),
-                pltpu.VMEM((rows, HEADS * BLOCK), BF16),
-                pltpu.VMEM((rows, LANES), F32),
-                pltpu.VMEM((rows, LANES), F32),
-            ],
+        functools.partial(back_kernel, fast, ctx),
+        grid=(groups + 1,),
+        in_specs=[
+            SMEM, columns(0), columns(1), columns(2), columns(0), columns(0),
+            pl.BlockSpec((1, HEADS, rows), lambda step: (group_of(step), 0, 0)),
+            ANY, ANY, ANY, ANY, whole(gain.shape), whole(norm_two.shape),
+        ] + [ANY] * len(partials),
+        out_specs=[ANY] + [whole(shape) for shape in reduced] + [whole((8, width))],
+        out_shape=[struct(inputs.shape)]
+        + [struct(shape) for shape in reduced]
+        + [struct((8, width), F32)],
+        scratch_shapes=scratch + extra,
+        compiler_params=pltpu.CompilerParams(
+            vmem_limit_bytes=VMEM_LIMIT, collective_id=2, has_side_effects=True
         ),
-        out_shape=[jax.ShapeDtypeStruct((rows, width), BF16)] * 3,
-        compiler_params=pltpu.CompilerParams(vmem_limit_bytes=56 * MIB),
-        cost_estimate=pl.CostEstimate(flops=40 * 10**9, bytes_accessed=12 * 10**6, transcendentals=0),
-        name="attention_backward",
-    )(length, packed, packed, packed, mixed, grad_mixed, logs)
+        name="back",
+    )(
+        length, packed, packed, packed, mixed, grad_mixed, logs, inputs, normed, middle, weight,
+        gain, norm_two, *partials,
+    )
 
 
 def exchange(value, axis, size, bit):
@@ -515,17 +833,23 @@
 
 def sum_weight(grad, seq_size, ctx_size):
     rows, columns = grad.shape
-    blocks = grad.astype(BF16).reshape(seq_size, rows // seq_size, columns)
+    blocks = grad.reshape(seq_size, rows // seq_size, columns)
     order = list(range(seq_size.bit_length() - 1))
     other = order[:1] + order[1:][::-1]
     half = columns // 2
     first = scatter_over_seq(blocks[:, :, :half], seq_size, order)
     second = scatter_over_seq(blocks[:, :, half:], seq_size, other)
-    summed = jnp.concatenate([first, second], axis=-1)
-    return sum_over_ctx(summed, ctx_size).astype(F32)
+    return sum_over_ctx(jnp.concatenate([first, second], axis=-1), ctx_size)
+
+
+def unpair(parts, rows, width):
+    parts = parts.reshape(PARTS, rows, 3, width // PARTS)
+    return parts.transpose(1, 2, 0, 3).reshape(rows, 3 * width)
 
 
 def make_per_device(seq_size, ctx_size):
+    fast = seq_size == 8 and ctx_size == 4
+
     def per_device(
         tokens,
         lengths,
@@ -539,8 +863,7 @@
         ln2_shift,
         cotangent,
     ):
-        shape = tokens.shape
-        width = shape[-1]
+        width = tokens.shape[-1]
         length = lax.dynamic_slice_in_dim(lengths, lax.axis_index("ctx"), 1)
         row = lambda vector: vector.reshape(1, width)
         inputs, normed_low, packed, cotangent, mixed_low, logs = front(
@@ -550,27 +873,29 @@
             length, inputs, mixed_low, cotangent, attention_out_weight, up_weight, down_weight,
             row(ln2_gain), row(ln2_shift),
         )
-        grad_packed = jnp.concatenate(
-            attention_backward(length, packed, mixed_low, grad_mixed, logs), axis=-1
-        )
-        grad_qkv = dot(normed_low, grad_packed, 0, 0)
-        grad_normed = dot(grad_packed, query_key_value_weight, 1, 1)
-        hat, inverse = normalise(inputs.reshape(-1, width).astype(F32))
-        grad_gain_one = jnp.sum(grad_normed * hat, axis=0)
-        grad_shift_one = jnp.sum(grad_normed, axis=0)
-        grad_inputs = grad_middle + normalise_backward(grad_normed, hat, inverse, ln1_gain)
-        grad_tokens = lax.all_to_all(grad_inputs.astype(BF16).reshape(shape), "ctx", 0, 0, tiled=True)
-        vectors = jnp.stack([grad_gain_one, grad_shift_one, grad_norm_two[0], grad_norm_two[1]])
-        vectors = lax.psum(vectors, ("seq", "ctx"))
+        partials = [grad_down, grad_up, grad_out]
+        grad_tokens, *sums, vectors = back(
+            fast, ctx_size, length, packed, mixed_low, grad_mixed, logs, inputs, normed_low,
+            grad_middle, query_key_value_weight, row(ln1_gain), grad_norm_two, partials,
+        )
         share = width // seq_size
+        if fast:
+            down, up, out = [part.reshape(-1, part.shape[-1]) for part in sums[:3]]
+            qkv = unpair(sums[3], share, width)
+        else:
+            grad_qkv = unpair(sums[0], width, width)
+            down, up, out, qkv = [
+                sum_weight(part, seq_size, ctx_size) for part in partials + [grad_qkv]
+            ]
+            vectors = lax.psum(vectors, ("seq", "ctx"))
         vectors = lax.dynamic_slice_in_dim(vectors, lax.axis_index("seq") * share, share, 1)
         return (
             output,
             grad_tokens,
-            sum_weight(grad_qkv, seq_size, ctx_size),
-            sum_weight(grad_out, seq_size, ctx_size),
-            sum_weight(grad_up, seq_size, ctx_size),
-            sum_weight(grad_down, seq_size, ctx_size),
+            qkv.astype(F32),
+            out.astype(F32),
+            up.astype(F32),
+            down.astype(F32),
             vectors[0],
             vectors[1],
             vectors[2],

time: 459 us -> 305 us (0.66); the launches traced: 452 us -> 305 us
  Pallas kernels: 174 us -> 288 us
  waiting for transfers between devices: 110 us -> 0 us
  starting transfers between devices: 48.9 us -> 0 us
  blocking collectives: 40.2 us -> 0 us
  local copies, waits for them, and re-layouts: 45.9 us -> 13.1 us
  other arithmetic: 20 us -> 3.02 us
  matrix products: 11.3 us -> 0 us
    pallas_call x1, Pallas kernels: 43.1 us -> 157 us  [back(): pl.pallas_call(functools.partial(back_kernel, fast, ctx), grid=(groups +...]
    ppermute x40 -> x0, waiting for transfers between devices: 110 us -> none  [exchange(): return lax.ppermute(value, axis, [(i, i ^ 1 << bit) for i in range(size)])]
    psum x1 -> x0, blocking collectives: 40.2 us -> none  [per_device(): vectors = lax.psum(vectors, ('seq', 'ctx'))]
    ppermute x40 -> x0, starting transfers between devices: 32.6 us -> none  [exchange(): return lax.ppermute(value, axis, [(i, i ^ 1 << bit) for i in range(size)])]
    all_to_all x1 -> x0, starting transfers between devices: 16.3 us -> none  [per_device(): lax.all_to_all(grad_inputs.astype(BF16).reshape(shape), 'ctx', 0, 0, tile...]
    convert_element_type x37 -> x3, other arithmetic: 15.7 us -> 3.02 us  [the longest x1 1.15 us: per_device(): up.astype(F32)]
    squeeze x32 -> x0, local copies, waits for them, and re-layouts: 12.6 us -> none  [halve(): sent = lax.dynamic_index_in_dim(value, 1 - mine, dim, keepdims=False)]
    dot_general x2 -> x0, matrix products: 11.3 us -> none  [dot(): lax.dot_general(a, b, (((dim_a,), (dim_b,)), ((), ())), preferred_element...]
  transfers between devices with their start and end apart: 41 -> 0, of which waited for: 21 -> 0; matrix products, arithmetic and copies ran while one was open for 12% -> 0% of each run, Pallas kernels for 10% -> 0%
where the time goes in v3:
time: 305 us
  Pallas kernels  288 us (94%)
  local copies, waits for them, and re-layouts  13.1 us (4%)
    pallas_call x1, Pallas kernels, back(): pl.pallas_call(functools.partial(back_kernel, fast, ctx), grid=(groups +...  157 us
    pallas_call x1, Pallas kernels, front(): pl.pallas_call(functools.partial(front_kernel, ctx), grid=(1 + groups,),...  78.1 us
    pallas_call x1, Pallas kernels, feed_forward(): pl.pallas_call(functools.partial(feed_forward_kernel, blocks), grid=(step...  53.2 us

profile of v3, /device:TPU:0, one launch (start us, length us, event | category | flops | bytes accessed | tf_op | source)
XLA Modules:
  0.0 304.8 jit_solution(18071587255372325095)
XLA Ops:
  0.6 1.2 dynamic_slice.6.length_ref
  1.9 1.3 reshape.57.gain
  3.2 1.3 reshape.58.shift
  4.4 0.0 copy-start.5
  4.4 0.0 copy-start.6
  4.4 78.1 %front.1 = (bf16[4,256,768]{2,1,0:T(8,128)(2,1)}, bf16[1024,768]{1,0:T(8,128)(2,1)}, bf16[1024,2304]{1,0:T(8,128)(2,1)}, bf16[4,256,768]{2,1,0:T(8,128)(2,1)}, b...) custom-call(s32[1]{0:T(128)} %dynamic_slice.6.length_ref, bf16[4,256,768]{2,1,0:T(8,128)(2,1)} %tokens.1, ...), custom_call_target="tpu_custom_call" | custom-call | tf_op jit(solution)/shard_map/front/pallas_call | solution.py:201
  82.5 0.0 copy-done.5
  82.5 0.6 reshape.59.gain
  83.1 0.0 copy-done.6
  83.1 0.6 reshape.60.shift
  83.7 53.2 %feed_forward.1 = (bf16[4,256,768]{2,1,0:T(8,128)(2,1)}, f32[1024,768]{1,0:T(8,128)}, bf16[1024,768]{1,0:T(8,128)(2,1)}, bf16[3072,768]{1,0:T(8,128)(2,1)}, bf16...) custom-call(s32[1]{0:T(128)} %dynamic_slice.6.length_ref, ...), custom_call_target="tpu_custom_call" | custom-call | tf_op jit(solution)/shard_map/feed_forward/pallas_call | solution.py:345
  136.9 156.7 %back.1 = (bf16[4,256,768]{2,1,0:T(8,128)(2,1)}, bf16[2,192,768]{2,1,0:T(8,128)(2,1)}, bf16[2,48,3072]{2,1,0:T(8,128)(2,1)}, bf16[2,48,768]{2,1,0:T(8,128)(2,1)}...) custom-call(s32[1]{0:T(128)} %dynamic_slice.6.length_ref, bf16[1024,2304]{1,0:T(8,128)(2,1)} %get-tuple-element.33.q_ref.k_ref.v_ref, ...), custom_call_target="tpu_custom_call" | custom-call | tf_op jit(solution)/shard_map/back/pallas_call | solution.py:773
  293.6 1.6 reshape.68
  295.2 0.6 copy.22
  295.8 0.0 copy-start.4
  295.8 0.0 copy-start.3
  295.8 1.5 reshape.64
  297.3 0.0 copy-start.2
  297.3 0.0 copy-done.4
  297.3 0.7 bitcast_convert_fusion.2
  298.1 0.0 copy-done.3
  298.1 0.0 copy-start
  298.1 1.2 bitcast_convert_fusion.1
  299.2 0.0 copy-done.2
  299.2 1.1 bitcast_convert_fusion
  300.4 0.8 constant_dynamic-slice_fusion
  301.1 0.5 slice_bitcast_fusion
  301.7 0.0 copy-done
  301.7 0.0 copy-start.1
  301.7 1.1 copy.25
  302.8 0.8 copy-done.1
  303.7 1.1 copy.26
Async XLA Ops:
  4.4 78.1 %copy-start.5 = (f32[768]{0:T(1024)S(1)}, f32[768]{0:T(1024)}, u32[]{:S(2)}) copy-start(f32[768]{0:T(1024)} %param.19) | copy-start | bytes 9220
  4.4 78.7 %copy-start.6 = (f32[768]{0:T(1024)S(1)}, f32[768]{0:T(1024)}, u32[]{:S(2)}) copy-start(f32[768]{0:T(1024)} %param.20) | copy-start | bytes 9220
  295.8 1.5 copy-start.4
  295.8 2.3 copy-start.3
  297.3 1.9 copy-start.2
  298.1 3.6 %copy-start = (bf16[4,256,768]{2,1,0:T(8,128)(2,1)S(1)}, bf16[4,256,768]{2,1,0:T(8,128)(2,1)}, u32[]{:S(2)}) copy-start(bf16[4,256,768]{2,1,0:T(8,128)(2,1)} %get-tuple-element.62) | copy-start | bytes 4718596
  301.7 2.0 copy-start.1

commit v4 on v3

--- a/solution.py
+++ b/solution.py
@@ -23,6 +23,7 @@
 ANY = pl.BlockSpec(memory_space=pl.ANY)
 SMEM = pl.BlockSpec(memory_space=pltpu.SMEM)
 ONE = pl.Buffered(1)
+VECTOR = pl.BlockSpec(memory_space=pltpu.VMEM)
 
 
 def dot(a, b, dim_a, dim_b):
@@ -33,6 +34,10 @@
 
 def whole(shape):
     return pl.BlockSpec(shape, lambda step: (0,) * len(shape), pipeline_mode=ONE)
+
+
+def row_of(vector):
+    return vector[...].reshape(1, -1)
 
 
 def struct(shape, kind=BF16):
@@ -70,12 +75,8 @@
 
 
 def gelu_and_slope(value):
+    cdf = 0.5 * lax.erf(value * math.sqrt(0.5)) + 0.5
     bell = jnp.exp2(value * value * (-0.5 * math.log2(math.e)))
-    t = 1.0 / (1.0 + jnp.abs(value) * (0.3275911 * math.sqrt(0.5)))
-    series = (1.061405429 * t - 1.453152027) * t + 1.421413741
-    series = ((series * t - 0.284496736) * t + 0.254829592) * t
-    tail = (0.5 * series) * bell
-    cdf = jnp.where(value >= 0, 1.0 - tail, tail)
     return (value * cdf, cdf + value * (bell * (1.0 / math.sqrt(2.0 * math.pi))))
 
 
@@ -162,7 +163,7 @@
 
         def project(source):
             hat, _ = normalise(inputs[source].astype(F32))
-            low = (hat * gain[...] + shift[...]).astype(BF16)
+            low = (hat * row_of(gain) + row_of(shift)).astype(BF16)
             rows = pl.ds(pl.multiple_of(source * block, block), block)
             normed[rows, :] = low
             packed[rows, :] = dot(low, weight[...], 1, 0).astype(BF16)
@@ -183,7 +184,7 @@
 
     @pl.when(step > 0)
     def _():
-        attend(step - 1, length_ref[0], packed, mixed_ref, log_ref, v_t, mixed_t)
+        attend(step - 1, length_ref[me], packed, mixed_ref, log_ref, v_t, mixed_t)
 
     @pl.when(step == pl.num_programs(0) - 1)
     def _():
@@ -201,7 +202,7 @@
     return pl.pallas_call(
         functools.partial(front_kernel, ctx),
         grid=(1 + groups,),
-        in_specs=[SMEM, ANY, ANY, whole(weight.shape), whole(gain.shape), whole(shift.shape)],
+        in_specs=[SMEM, ANY, ANY, whole(weight.shape), VECTOR, VECTOR],
         out_specs=[
             ANY, ANY, ANY, ANY,
             pl.BlockSpec((rows, LANES), lambda step: (0, group_of(step))),
@@ -234,164 +235,16 @@
     )(length, tokens, cotangent, weight, gain, shift)
 
 
-def feed_forward_kernel(
-    blocks, length_ref, inputs, mixed, cotangent, out_weight, up_weight, down_weight, gain, shift,
-    output, grad_middle_ref, grad_mixed_ref, grad_down_ref, grad_up_ref, grad_out_ref, grad_norm_ref,
-    normed, upstream, branch, active, hidden, staged, send, recv, local,
-):
-    step = pl.program_id(0)
-    me = lax.axis_index("ctx")
-    block = staged.shape[1]
-    width = normed.shape[1]
-    wide = active.shape[1]
-    cuts = wide // width
-
-    def output_copy(row):
-        return to_partner(
-            staged.at[row], output.at[me], send.at[row], recv.at[me], {"ctx": row}
-        )
-
-    own_output = pltpu.make_async_copy(staged.at[me], output.at[me], local)
-
-    @pl.when(step == 0)
-    def _():
-        greet([{"ctx": me ^ offset} for offset in range(1, blocks)])
-        grad_norm_ref[...] = jnp.zeros_like(grad_norm_ref)
-
-    @pl.when(step < blocks)
-    def _():
-        rows = pl.ds(pl.multiple_of(step * block, block), block)
-        middle = inputs[step].astype(F32) + dot(mixed[rows, :], out_weight[...], 1, 0)
-        hat, inverse = normalise(middle)
-        low = (hat * gain[...] + shift[...]).astype(BF16)
-        normed[rows, :] = low
-        places = step * block + lax.broadcasted_iota(jnp.int32, (block, 1), 0)
-        valid = places < length_ref[0]
-        upstream_full = jnp.where(valid, cotangent[step].astype(F32), 0.0)
-        upstream_low = upstream_full.astype(BF16)
-        upstream[rows, :] = upstream_low
-
-        def products_of(cut):
-            part = slice(cut * width, (cut + 1) * width)
-            return (
-                dot(low, up_weight[:, part], 1, 0),
-                dot(upstream_low, down_weight[part, :], 1, 1),
-            )
-
-        current = products_of(0)
-        total, grad_normed = middle, 0.0
-        for cut in range(cuts):
-            part = slice(cut * width, (cut + 1) * width)
-            following = products_of(cut + 1) if cut + 1 < cuts else None
-            value, slope = gelu_and_slope(current[0])
-            value = value.astype(BF16)
-            grad_hidden = (slope * current[1]).astype(BF16)
-            active[rows, part] = value
-            hidden[rows, part] = grad_hidden
-            total = total + dot(value, down_weight[part, :], 1, 0)
-            grad_normed = grad_normed + dot(grad_hidden, up_weight[:, part], 1, 1)
-            current = following
-        staged[step] = jnp.where(valid, total, 0.0).astype(BF16)
-
-        @pl.when(step != me)
-        def _():
-            output_copy(step).start()
-
-        @pl.when(step == me)
-        def _():
-            own_output.start()
-
-        grad_norm_ref[0:1, :] += jnp.sum(grad_normed * hat, axis=0, keepdims=True)
-        grad_norm_ref[1:2, :] += jnp.sum(grad_normed, axis=0, keepdims=True)
-        grad_middle = upstream_full + normalise_backward(grad_normed, hat, inverse, gain[...])
-        grad_middle_ref[...] = grad_middle
-        grad_branch = grad_middle.astype(BF16)
-        branch[rows, :] = grad_branch
-        grad_mixed_ref[...] = dot(grad_branch, out_weight[...], 1, 1).astype(BF16)
-
-    @pl.when(step == blocks)
-    def _():
-        grad_out_ref[...] = dot(mixed[...], branch[...], 0, 0).astype(BF16)
-
-    @pl.when(step >= blocks)
-    def _():
-        size = grad_down_ref.shape[0]
-        part = pl.ds(pl.multiple_of((step - blocks) * size, size), size)
-        grad_down_ref[...] = dot(active[:, part], upstream[...], 0, 0).astype(BF16)
-        grad_up_ref[...] = dot(normed[...], hidden[:, part], 0, 0).astype(BF16)
-
-    @pl.when(step == pl.num_programs(0) - 1)
-    def _():
-        own_output.wait()
-        for row in range(blocks):
-
-            @pl.when(row != me)
-            def _():
-                copy = output_copy(row)
-                copy.wait_send()
-                to_partner(
-                    staged.at[row], output.at[row], send.at[row], recv.at[row], {"ctx": row}
-                ).wait_recv()
-
-
-def feed_forward(length, inputs, mixed, cotangent, out_weight, up_weight, down_weight, gain, shift):
-    blocks, block, width = inputs.shape
-    rows, wide = blocks * block, up_weight.shape[1]
-    size = 512
-    steps = blocks + wide // size
-    early = lambda step: jnp.minimum(step, blocks - 1)
-    late = lambda step: jnp.maximum(step - blocks, 0)
-    operands = (inputs, mixed, cotangent, out_weight, up_weight, down_weight, gain, shift)
-    return pl.pallas_call(
-        functools.partial(feed_forward_kernel, blocks),
-        grid=(steps,),
-        in_specs=[SMEM] + [whole(operand.shape) for operand in operands],
-        out_specs=[
-            ANY,
-            pl.BlockSpec((block, width), lambda step: (early(step), 0)),
-            pl.BlockSpec((block, width), lambda step: (early(step), 0)),
-            pl.BlockSpec((size, width), lambda step: (late(step), 0)),
-            pl.BlockSpec((width, size), lambda step: (0, late(step))),
-            whole((width, width)),
-            whole((8, width)),
-        ],
-        out_shape=[
-            struct(inputs.shape),
-            struct((rows, width), F32),
-            struct((rows, width)),
-            struct((wide, width)),
-            struct((width, wide)),
-            struct((width, width)),
-            struct((8, width), F32),
-        ],
-        scratch_shapes=[
-            pltpu.VMEM((rows, width), BF16),
-            pltpu.VMEM((rows, width), BF16),
-            pltpu.VMEM((rows, width), BF16),
-            pltpu.VMEM((rows, wide), BF16),
-            pltpu.VMEM((rows, wide), BF16),
-            pltpu.VMEM(inputs.shape, BF16),
-            pltpu.SemaphoreType.DMA((blocks,)),
-            pltpu.SemaphoreType.DMA((blocks,)),
-            pltpu.SemaphoreType.DMA,
-        ],
-        compiler_params=pltpu.CompilerParams(
-            vmem_limit_bytes=60 * MIB, collective_id=1, has_side_effects=True
-        ),
-        name="feed_forward",
-    )(length, *operands)
-
-
 PARTS = 3
 KINDS = 8
 
 
 class Chunk:
-    def __init__(self, source, own, stages, send, recv, local, places):
-        self.source, self.own = source, own
+    def __init__(self, source, own, stages, send, recv, local, places, second=False):
+        self.source, self.own, self.second = source, own, second
         self.r1, self.r2a, self.r2b, self.r3, self.z1, self.z2, self.out = stages
         self.send, self.recv, self.local, self.places = send, recv, local, places
-        self.cut = self.r3.shape[-1] // 2
+        self.cut = self.r2a.shape[-1]
 
     def copy(self, kind):
         seq, ctx, core, x, y, low = self.places
@@ -412,6 +265,20 @@
     def own_copy(self):
         core = self.places[2]
         return pltpu.make_async_copy(self.source.at[:, :, core], self.own, self.local)
+
+    def add_second(self):
+        _, _, _, x, y, _ = self.places
+        cut = self.cut
+        self.copy(1).wait_recv()
+        self.copy(2).wait_recv()
+        for other in range(2):
+            self.r2a[other] += self.r1[other, x, :, :, 0:cut]
+            self.r2b[other] += self.r1[y, other, :, :, cut:]
+
+    def finish_second(self):
+        self.add_second()
+        for kind in range(3):
+            self.copy(kind).wait_send()
 
     def event(self, number):
         seq, ctx, core, x, y, low = self.places
@@ -434,11 +301,8 @@
             self.copy(1).start()
             self.copy(2).start()
         if number == 2:
-            self.copy(1).wait_recv()
-            self.copy(2).wait_recv()
-            for other in range(2):
-                self.r2a[other] += self.r1[other, x, :, :, 0:cut]
-                self.r2b[other] += self.r1[y, other, :, :, cut:]
+            if not self.second:
+                self.add_second()
             self.copy(3).start()
             self.copy(4).start()
         if number == 3:
@@ -460,11 +324,267 @@
                 self.out.at[1 - low], self.out.at[1 - low], self.send.at[7], self.recv.at[7],
                 {"ctx": ctx ^ 1},
             ).wait_recv()
-            for kind in range(KINDS):
+            for kind in range(3 if self.second else 0, KINDS):
                 self.copy(kind).wait_send()
 
 
-def chunk_scratch(rows, columns, held):
+CUT = 512
+PIECES = 8
+
+
+def feed_forward_kernel(
+    fast, blocks, length_ref, inputs, mixed, out_weight, gain, shift, up_in, down_in,
+    cotangent_in,
+    output, grad_down_out, grad_middle_ref, grad_mixed_ref, grad_up_ref, grad_out_ref,
+    grad_norm_ref, *rest,
+):
+    rest = list(rest)
+    take = lambda count: [rest.pop(0) for _ in range(count)]
+    carried = take(2) if fast else []
+    (up_weight, down_weight, normed, upstream, branch, active, hidden, scaled, inverse_of) = take(9)
+    (staged, cotangent, grad_down, output_send, output_recv, local) = take(6)
+    step = pl.program_id(0)
+    seq, me = lax.axis_index("seq"), lax.axis_index("ctx")
+    block, width = staged.shape[1:]
+    wide = active.shape[1]
+    cuts = wide // CUT
+    backward = blocks + 1
+    late = backward + blocks
+    chunk = None
+    if fast:
+        send, recv, r1, r2a, r2b = take(5)
+        places = (seq, me, seq % 2, (seq // 2) % 2, seq // 4, me % 2)
+        chunk = Chunk(
+            grad_down, None, (r1, r2a, r2b, None, None, None, None), send, recv, None, places
+        )
+
+    def output_copy(row):
+        return to_partner(
+            staged.at[row], output.at[me], output_send.at[row], output_recv.at[me], {"ctx": row}
+        )
+
+    own_output = pltpu.make_async_copy(staged.at[me], output.at[me], local.at[0])
+    cotangent_load = pltpu.make_async_copy(cotangent_in, cotangent, local.at[4])
+    up_load = pltpu.make_async_copy(up_in, up_weight, local.at[1])
+    down_load = pltpu.make_async_copy(down_in, down_weight, local.at[2])
+
+    @pl.when(step == 0)
+    def _():
+        up_load.start()
+        down_load.start()
+        partners = [{"ctx": me ^ offset} for offset in range(1, blocks)]
+        if fast:
+            partners += [{"seq": seq ^ 1}, {"seq": seq ^ 2}, {"seq": seq ^ 4}]
+        greet(partners)
+        cotangent_load.start()
+        grad_norm_ref[...] = jnp.zeros_like(grad_norm_ref)
+
+    def rows_of(number):
+        return pl.ds(pl.multiple_of(number * block, block), block)
+
+    def valid_rows(number):
+        places = number * block + lax.broadcasted_iota(jnp.int32, (block, 1), 0)
+        return places < length_ref[me]
+
+    @pl.when(step < blocks)
+    def _():
+        row = me ^ ((step + blocks // 2) % blocks)
+        rows = rows_of(row)
+        middle = inputs[row].astype(F32) + dot(mixed[rows, :], out_weight[...], 1, 0)
+        hat, inverse = normalise(middle)
+        scaled[rows, :] = hat
+        inverse_of[rows, :] = inverse
+        low = (hat * row_of(gain) + row_of(shift)).astype(BF16)
+        normed[rows, :] = low
+
+        @pl.when(step == 0)
+        def _():
+            up_load.wait()
+            down_load.wait()
+
+        product_of = lambda cut: dot(low, up_weight[:, cut * CUT : (cut + 1) * CUT], 1, 0)
+        current = product_of(0)
+        total = middle
+        for cut in range(cuts):
+            part = slice(cut * CUT, (cut + 1) * CUT)
+            following = product_of(cut + 1) if cut + 1 < cuts else None
+            value, slope = gelu_and_slope(current)
+            value = value.astype(BF16)
+            active[rows, part] = value
+            hidden[rows, part] = slope.astype(BF16)
+            total = total + dot(value, down_weight[part, :], 1, 0)
+            current = following
+        staged[row] = jnp.where(valid_rows(row), total, 0.0).astype(BF16)
+
+        @pl.when(row != me)
+        def _():
+            output_copy(row).start()
+
+        @pl.when(row == me)
+        def _():
+            own_output.start()
+
+    @pl.when(step == blocks)
+    def _():
+        cotangent_load.wait()
+        for row in range(blocks):
+            kept = jnp.where(valid_rows(row), cotangent[row], 0)
+            upstream[row * block : (row + 1) * block, :] = kept
+        size = wide // PIECES
+
+        @pl.loop(0, PIECES)
+        def _(piece):
+            columns = pl.ds(pl.multiple_of(piece * size, LANES), size)
+            product = dot(active[:, columns], upstream[...], 0, 0)
+            product = product.astype(BF16).reshape(2, size // 2, width)
+            grad_down[piece // 4, (piece // 2) % 2, piece % 2] = product
+
+        if fast:
+            chunk.event(0)
+        else:
+            pltpu.make_async_copy(grad_down, grad_down_out, local.at[3]).start()
+
+    @pl.when((step >= backward) & (step < late))
+    def _():
+        number = step - backward
+        rows = rows_of(number)
+        upstream_low = upstream[rows, :]
+
+        @pl.when(number == 2)
+        def _():
+            if fast:
+                chunk.event(1)
+
+        product_of = lambda cut: dot(
+            upstream_low, down_weight[cut * CUT : (cut + 1) * CUT, :], 1, 1
+        )
+        current = product_of(0)
+        grad_normed = 0.0
+        for cut in range(cuts):
+            part = slice(cut * CUT, (cut + 1) * CUT)
+            following = product_of(cut + 1) if cut + 1 < cuts else None
+            grad_hidden = (hidden[rows, part].astype(F32) * current).astype(BF16)
+            hidden[rows, part] = grad_hidden
+            grad_normed = grad_normed + dot(grad_hidden, up_weight[:, part], 1, 1)
+            current = following
+        hat = scaled[rows, :]
+        grad_norm_ref[0:1, :] += jnp.sum(grad_normed * hat, axis=0, keepdims=True)
+        grad_norm_ref[1:2, :] += jnp.sum(grad_normed, axis=0, keepdims=True)
+        through = normalise_backward(grad_normed, hat, inverse_of[rows, :], row_of(gain))
+        grad_middle = upstream_low.astype(F32) + through
+        grad_middle_ref[...] = grad_middle
+        grad_branch = grad_middle.astype(BF16)
+        branch[rows, :] = grad_branch
+        grad_mixed_ref[...] = dot(grad_branch, out_weight[...], 1, 1).astype(BF16)
+
+    @pl.when(step == late)
+    def _():
+        grad_out_ref[...] = dot(mixed[...], branch[...], 0, 0).astype(BF16)
+
+    @pl.when(step >= late)
+    def _():
+        size = grad_up_ref.shape[1]
+        part = pl.ds(pl.multiple_of((step - late) * size, size), size)
+        grad_up_ref[...] = dot(normed[...], hidden[:, part], 0, 0).astype(BF16)
+
+    @pl.when(step == pl.num_programs(0) - 1)
+    def _():
+        own_output.wait()
+        for row in range(blocks):
+
+            @pl.when(row != me)
+            def _():
+                output_copy(row).wait_send()
+                to_partner(
+                    staged.at[row], output.at[row], output_send.at[row], output_recv.at[row],
+                    {"ctx": row},
+                ).wait_recv()
+
+        if fast:
+            chunk.finish_second()
+            for there, here in zip(carried, (r2a, r2b)):
+                there[...] = here[...]
+        else:
+            pltpu.make_async_copy(grad_down, grad_down_out, local.at[3]).wait()
+
+
+def feed_forward(
+    fast, length, inputs, mixed, cotangent, out_weight, up_weight, down_weight, gain, shift
+):
+    blocks, block, width = inputs.shape
+    rows, wide = blocks * block, up_weight.shape[1]
+    size = 512
+    late = 2 * blocks + 1
+    steps = late + wide // size
+    back_row = lambda step: jnp.clip(step - blocks - 1, 0, blocks - 1)
+    up_part = lambda step: jnp.maximum(step - late, 0)
+    operands = (inputs, mixed, out_weight)
+    piece = wide // PIECES // 2
+    lead = (2, 2, 2, 2)
+    half = (2, 2, piece, width // 2)
+    grad_down_shape = lead + (piece, width) if not fast else (8, LANES)
+    carried = [whole(half)] * 2 if fast else []
+    extra = []
+    if fast:
+        extra = [
+            pltpu.SemaphoreType.DMA((KINDS,)),
+            pltpu.SemaphoreType.DMA((KINDS,)),
+            pltpu.VMEM((2, 2, 2, piece, width), BF16),
+            pltpu.VMEM(half, BF16),
+            pltpu.VMEM(half, BF16),
+        ]
+    return pl.pallas_call(
+        functools.partial(feed_forward_kernel, fast, blocks),
+        grid=(steps,),
+        in_specs=[SMEM]
+        + [whole(operand.shape) for operand in operands]
+        + [VECTOR, VECTOR, ANY, ANY, ANY],
+        out_specs=[
+            ANY,
+            ANY,
+            pl.BlockSpec((block, width), lambda step: (back_row(step), 0)),
+            pl.BlockSpec((block, width), lambda step: (back_row(step), 0)),
+            pl.BlockSpec((width, size), lambda step: (0, up_part(step))),
+            whole((width, width)),
+            whole((8, width)),
+        ]
+        + carried,
+        out_shape=[
+            struct(inputs.shape),
+            struct(grad_down_shape),
+            struct((rows, width), F32),
+            struct((rows, width)),
+            struct((width, wide)),
+            struct((width, width)),
+            struct((8, width), F32),
+        ]
+        + [struct(half)] * len(carried),
+        scratch_shapes=[
+            pltpu.VMEM(up_weight.shape, BF16),
+            pltpu.VMEM(down_weight.shape, BF16),
+            pltpu.VMEM((rows, width), BF16),
+            pltpu.VMEM((rows, width), BF16),
+            pltpu.VMEM((rows, width), BF16),
+            pltpu.VMEM((rows, wide), BF16),
+            pltpu.VMEM((rows, wide), BF16),
+            pltpu.VMEM((rows, width), F32),
+            pltpu.VMEM((rows, 1), F32),
+            pltpu.VMEM(inputs.shape, BF16),
+            pltpu.VMEM(inputs.shape, BF16),
+            pltpu.VMEM(lead + (piece, width), BF16),
+            pltpu.SemaphoreType.DMA((blocks,)),
+            pltpu.SemaphoreType.DMA((blocks,)),
+            pltpu.SemaphoreType.DMA((5,)),
+        ]
+        + extra,
+        compiler_params=pltpu.CompilerParams(
+            vmem_limit_bytes=VMEM_LIMIT, collective_id=1, has_side_effects=True
+        ),
+        name="feed_forward",
+    )(length, *operands, gain, shift, up_weight, down_weight, cotangent)
+
+
+def chunk_scratch(rows, columns, number):
     shapes = [
         (2, 2, 2, rows, columns),
         (2, 2, rows, columns // 2),
@@ -474,29 +594,31 @@
         (rows, columns),
         (2, rows, columns),
     ]
-    if held:
+    if number == 0:
+        shapes = shapes[3:]
+    elif number < 3:
         shapes.insert(0, (2, 2, 2, rows, columns))
     return [pltpu.VMEM(shape, BF16) for shape in shapes]
 
 
 PLAN = {
-    (0, 0): [(0, 0)],
-    (0, 3): [(1, 0), (2, 0)],
-    (1, 0): [(0, 1)],
-    (2, 0): [(3, 0)],
-    (2, 3): [(0, 2), (1, 1)],
-    (3, 0): [(2, 1), (3, 1)],
-    (4, 0): [(4, 0)],
-    (4, 1): [(0, 3)],
-    (4, 3): [(2, 2), (3, 2), (4, 1)],
-    (5, 0): [(0, 4)],
-    (5, 1): [(1, 2)],
-    (5, 3): [(2, 3), (3, 3)],
+    (0, 0): [(0, 2), (1, 0), (2, 0)],
+    (1, 0): [(1, 1)],
+    (1, 1): [(0, 3)],
+    (2, 0): [(0, 4), (3, 0)],
+    (2, 3): [(1, 2), (2, 1), (3, 1)],
+    (3, 2): [(2, 2), (3, 2)],
+    (3, 3): [(1, 3), (2, 3)],
+    (4, 0): [(0, 5), (4, 0), (3, 3)],
+    (4, 2): [(1, 4), (2, 4), (4, 1)],
+    (5, 0): [(3, 4), (4, 2)],
+    (5, 2): [(2, 5), (4, 3)],
+    (5, 3): [(3, 5), (4, 4)],
 }
-PLAN_BEFORE_NORM = [(5, 0), (4, 2), (1, 3), (0, 5), (2, 4), (3, 4)]
+PLAN_BEFORE_NORM = [(1, 5), (4, 5)]
 PLAN_AFTER_NORM = [
-    "v0", (5, 1), (4, 3), "v1", (2, 5), (3, 5), (1, 4), "v2", (5, 2), (4, 4), "v3", (0, 6), (1, 5),
-    (5, 3), (4, 5), (5, 4), "v4", (2, 6), (3, 6), (1, 6), (5, 5), (4, 6), (5, 6), "v5",
+    (5, 0), "v0", (5, 1), "v1", (5, 2), "v2", (5, 3), "v3", (0, 6), (2, 6), (3, 6), (1, 6), (4, 6),
+    (5, 4), "v4", (5, 5), "v5", (5, 6),
 ]
 
 
@@ -506,7 +628,7 @@
 ):
     rest = list(rest)
     take = lambda count: [rest.pop(0) for _ in range(count)]
-    sources = take(3) if fast else []
+    sources = take(4) if fast else []
     (grad_tokens,) = take(1)
     results = take(4) if fast else take(1)
     (vector_out,) = take(1)
@@ -523,13 +645,18 @@
         send, recv = take(2)
         places = (seq, me, seq % 2, (seq // 2) % 2, seq // 4, me % 2)
         for number in range(3 + PARTS):
-            held = number < 3
-            own = take(1)[0] if held else None
-            source = sources[number] if held else partial.at[number - 3]
+            own, stages = None, [None] * 7
+            if number == 0:
+                stages[1:] = sources[:2] + take(4)
+            elif number < 3:
+                own, *stages = take(8)
+            else:
+                stages = take(7)
+            source = sources[number + 1] if number < 3 else partial.at[number - 3]
             chunks.append(
                 Chunk(
-                    source, own, take(7), send.at[number], recv.at[number],
-                    local.at[5 + number], places,
+                    source, own, stages, send.at[number], recv.at[number], local.at[5 + number],
+                    places, second=number == 0,
                 )
             )
 
@@ -580,7 +707,7 @@
     def _():
         side = pl.ds(pl.multiple_of((step % 2) * LANES, LANES), LANES)
         attend_backward(
-            hook, side, length_ref[0], q_ref, k_ref, v_ref, mixed_ref, grad_ref, log_ref, pair,
+            hook, side, length_ref[me], q_ref, k_ref, v_ref, mixed_ref, grad_ref, log_ref, pair,
             k_t, grad_q_t, probs_low, grads_low, sum_k, sum_v,
         )
 
@@ -590,22 +717,29 @@
             load.wait()
         grad_normed[...] = jnp.zeros_like(grad_normed)
 
-    @pl.when((step < groups) & (step % 2 == 1))
-    def _():
-        part = step // 2
-        for name in range(PARTS):
-            columns = slice(name * 2 * LANES, (name + 1) * 2 * LANES)
+    def weight_gradient(part):
+        @pl.loop(0, PARTS)
+        def _(name):
+            columns = pl.ds(pl.multiple_of(name * 2 * LANES, 2 * LANES), 2 * LANES)
             product = dot(normed[...], pair[name], 0, 0).astype(BF16)
             if fast:
-                partial[part, :, :, :, :, :, columns] = product.reshape(
-                    2, 2, 2, 2, width // 16, 2 * LANES
-                )
+                product = product.reshape(2, 2, 2, 2, width // 16, 2 * LANES)
+                partial[part, :, :, :, :, :, columns] = product
             else:
                 partial[part, :, columns] = product
-            there = pl.ds(
-                pl.multiple_of(name * width + part * 2 * LANES, 2 * LANES), 2 * LANES
-            )
-            grad_normed[...] += dot(pair[name], weight[:, there], 1, 1)
+
+    @pl.when((step < groups) & (step % 2 == 1))
+    def _():
+        part = step // 2
+
+        @pl.loop(0, PARTS)
+        def _(name):
+            there = pl.multiple_of(name * width + part * 2 * LANES, 2 * LANES)
+            grad_normed[...] += dot(pair[name], weight[:, pl.ds(there, 2 * LANES)], 1, 1)
+
+        @pl.when(step < groups - 1)
+        def _():
+            weight_gradient(part)
 
     def token_copy(row):
         return to_partner(
@@ -625,7 +759,7 @@
             grad = grad_normed[there, :]
             gain_sum = gain_sum + jnp.sum(grad * hat, axis=0, keepdims=True)
             shift_sum = shift_sum + jnp.sum(grad, axis=0, keepdims=True)
-            total = middle[there, :] + normalise_backward(grad, hat, inverse, gain[...])
+            total = middle[there, :] + normalise_backward(grad, hat, inverse, row_of(gain))
             staged[row] = total.astype(BF16)
 
             @pl.when(row != me)
@@ -637,6 +771,7 @@
                 own_tokens.start()
 
         vectors[0] = jnp.concatenate([gain_sum, shift_sum, norm_two[0:6, :]], axis=0)
+        weight_gradient(PARTS - 1)
         for name in PLAN_AFTER_NORM:
             run(name)
         if fast:
@@ -730,10 +865,13 @@
     )
     if fast:
         lead = (2, 2, 2, 2)
+        carried, partials = partials[:2], partials[2:]
         partials = [
             grad.reshape(lead + (grad.shape[0] // 16, grad.shape[1])) for grad in partials
         ]
-        sizes = [grad.shape[-2:] for grad in partials] + [(width // 16, width)] * PARTS
+        sizes = [(carried[0].shape[2], width)] + [grad.shape[-2:] for grad in partials]
+        sizes += [(width // 16, width)] * PARTS
+        partials = carried + partials
         reduced = [(2,) + size for size in sizes[:3]] + [(PARTS, 2, width // 16, width)]
         held = [PARTS] + list(lead) + [width // 16, width]
         extra = [
@@ -741,7 +879,7 @@
             pltpu.SemaphoreType.DMA((len(sizes), KINDS)),
         ]
         for number, size in enumerate(sizes):
-            extra += chunk_scratch(*size, held=number < 3)
+            extra += chunk_scratch(*size, number)
     else:
         partials = []
         reduced = [(PARTS, width, width)]
@@ -776,8 +914,8 @@
         in_specs=[
             SMEM, columns(0), columns(1), columns(2), columns(0), columns(0),
             pl.BlockSpec((1, HEADS, rows), lambda step: (group_of(step), 0, 0)),
-            ANY, ANY, ANY, ANY, whole(gain.shape), whole(norm_two.shape),
-        ] + [ANY] * len(partials),
+            ANY, ANY, ANY, ANY, VECTOR, whole(norm_two.shape),
+        ] + [whole(partial.shape) if number < 2 else ANY for number, partial in enumerate(partials)],
         out_specs=[ANY] + [whole(shape) for shape in reduced] + [whole((8, width))],
         out_shape=[struct(inputs.shape)]
         + [struct(shape) for shape in reduced]
@@ -847,6 +985,52 @@
     return parts.transpose(1, 2, 0, 3).reshape(rows, 3 * width)
 
 
+def finish_kernel(output, tokens, qkv, out, up, down, *results):
+    *results, copies = results
+    output_out, tokens_out, qkv_out, out_out, up_out, down_out = results[:6]
+    moves = [
+        pltpu.make_async_copy(output, output_out, copies.at[0]),
+        pltpu.make_async_copy(tokens, tokens_out, copies.at[1]),
+    ]
+    for move in moves:
+        move.start()
+    for source, target in ((out, out_out), (up, up_out), (down, down_out)):
+        rows = source.shape[1]
+        for half in range(2):
+            target[half * rows : (half + 1) * rows, :] = source[half].astype(F32)
+    rows, width = qkv.shape[2:]
+    step = width // 3
+    for part in range(PARTS):
+        for half in range(2):
+            for name in range(3):
+                first = name * width + part * step
+                value = qkv[part, half, :, name * step : (name + 1) * step]
+                qkv_out[half * rows : (half + 1) * rows, first : first + step] = value.astype(F32)
+    for move in moves:
+        move.wait()
+
+
+def finish(output, tokens, qkv, out, up, down):
+    flat = lambda part: struct((2 * part.shape[1], part.shape[2]), F32)
+    memory = pl.BlockSpec(memory_space=pltpu.VMEM)
+    return pl.pallas_call(
+        finish_kernel,
+        in_specs=[ANY, ANY] + [memory] * 4,
+        out_specs=[ANY, ANY] + [memory] * 4,
+        out_shape=[
+            struct(output.shape),
+            struct(tokens.shape),
+            struct((2 * qkv.shape[2], 3 * qkv.shape[3]), F32),
+            flat(out),
+            flat(up),
+            flat(down),
+        ],
+        scratch_shapes=[pltpu.SemaphoreType.DMA((2,))],
+        compiler_params=pltpu.CompilerParams(vmem_limit_bytes=24 * MIB),
+        name="finish",
+    )(output, tokens, qkv, out, up, down)
+
+
 def make_per_device(seq_size, ctx_size):
     fast = seq_size == 8 and ctx_size == 4
 
@@ -864,28 +1048,32 @@
         cotangent,
     ):
         width = tokens.shape[-1]
-        length = lax.dynamic_slice_in_dim(lengths, lax.axis_index("ctx"), 1)
-        row = lambda vector: vector.reshape(1, width)
         inputs, normed_low, packed, cotangent, mixed_low, logs = front(
-            ctx_size, length, tokens, cotangent, query_key_value_weight, row(ln1_gain), row(ln1_shift)
-        )
-        output, grad_middle, grad_mixed, grad_down, grad_up, grad_out, grad_norm_two = feed_forward(
-            length, inputs, mixed_low, cotangent, attention_out_weight, up_weight, down_weight,
-            row(ln2_gain), row(ln2_shift),
-        )
-        partials = [grad_down, grad_up, grad_out]
+            ctx_size, lengths, tokens, cotangent, query_key_value_weight, ln1_gain, ln1_shift
+        )
+        (
+            output, grad_down, grad_middle, grad_mixed, grad_up, grad_out, grad_norm_two, *carried
+        ) = feed_forward(
+            fast, lengths, inputs, mixed_low, cotangent, attention_out_weight, up_weight,
+            down_weight, ln2_gain, ln2_shift,
+        )
+        partials = carried + [grad_up, grad_out]
         grad_tokens, *sums, vectors = back(
-            fast, ctx_size, length, packed, mixed_low, grad_mixed, logs, inputs, normed_low,
-            grad_middle, query_key_value_weight, row(ln1_gain), grad_norm_two, partials,
+            fast, ctx_size, lengths, packed, mixed_low, grad_mixed, logs, inputs, normed_low,
+            grad_middle, query_key_value_weight, ln1_gain, grad_norm_two, partials,
         )
         share = width // seq_size
         if fast:
-            down, up, out = [part.reshape(-1, part.shape[-1]) for part in sums[:3]]
-            qkv = unpair(sums[3], share, width)
+            down, up, out, qkv = sums
+            output, grad_tokens, qkv, out, up, down = finish(
+                output, grad_tokens, qkv, out, up, down
+            )
         else:
             grad_qkv = unpair(sums[0], width, width)
+            grad_down = grad_down.reshape(-1, width)
             down, up, out, qkv = [
-                sum_weight(part, seq_size, ctx_size) for part in partials + [grad_qkv]
+                sum_weight(part, seq_size, ctx_size)
+                for part in (grad_down, grad_up, grad_out, grad_qkv)
             ]
             vectors = lax.psum(vectors, ("seq", "ctx"))
         vectors = lax.dynamic_slice_in_dim(vectors, lax.axis_index("seq") * share, share, 1)

time: 305 us -> 268 us (0.88)
  Pallas kernels: 288 us -> 259 us
  local copies, waits for them, and re-layouts: 13.1 us -> 6.76 us
    pallas_call x1, Pallas kernels: 157 us -> 125 us  [back(): pl.pallas_call(functools.partial(back_kernel, fast, ctx), grid=(groups +...]
    pallas_call x1 -> x2, Pallas kernels: 53.2 us -> 57.3 us  [the longest x1 53.8 us: feed_forward(): pl.pallas_call(functools.partial(feed_forward_kernel, fast, blocks), grid...]
    reshape x4 -> x0, local copies, waits for them, and re-layouts: 3.69 us -> none  [per_device(): row = lambda vector: vector.reshape(1, width)]
    convert_element_type x3 -> x0, local copies, waits for them, and re-layouts: 3.68 us -> none  [per_device(): qkv.astype(F32)]
where the time goes in v4:
time: 268 us; the launch traced here: 267 us
  Pallas kernels  259 us (97%)
  local copies, waits for them, and re-layouts  6.76 us (3%)
    pallas_call x1, Pallas kernels, back(): pl.pallas_call(functools.partial(back_kernel, fast, ctx), grid=(groups +...  125 us
    pallas_call x1, Pallas kernels, front(): pl.pallas_call(functools.partial(front_kernel, ctx), grid=(1 + groups,),...  77.4 us
    pallas_call x1, Pallas kernels, feed_forward(): pl.pallas_call(functools.partial(feed_forward_kernel, fast, blocks), grid...  53.8 us
    unnamed x12, local copies, waits for them, and re-layouts  5.45 us

profile of v4, /device:TPU:0, one launch (start us, length us, event | category | flops | bytes accessed | tf_op | source)
XLA Modules:
  0.0 266.9 jit_solution(1053819229824461676)
XLA Ops:
  0.6 77.4 %front.1 = (bf16[4,256,768]{2,1,0:T(8,128)(2,1)}, bf16[1024,768]{1,0:T(8,128)(2,1)}, bf16[1024,2304]{1,0:T(8,128)(2,1)}, bf16[4,256,768]{2,1,0:T(8,128)(2,1)}, b...) custom-call(s32[4]{0:T(128)} %length_ref.5, bf16[4,256,768]{2,1,0:T(8,128)(2,1)} %tokens.1, ...), custom_call_target="tpu_custom_call" | custom-call | tf_op jit(solution)/shard_map/front/pallas_call | solution.py:202
  78.1 53.8 %feed_forward.1 = (bf16[4,256,768]{2,1,0:T(8,128)(2,1)}, bf16[8,128]{1,0:T(8,128)(2,1)}, f32[1024,768]{1,0:T(8,128)}, bf16[1024,768]{1,0:T(8,128)(2,1)}, bf16[76...) custom-call(s32[4]{0:T(128)} %length_ref.5, ...), custom_call_target="tpu_custom_call" | custom-call | tf_op jit(solution)/shard_map/feed_forward/pallas_call | solution.py:536
  131.9 0.0 copy-start
  131.9 124.7 %back.1 = (bf16[4,256,768]{2,1,0:T(8,128)(2,1)}, bf16[2,192,768]{2,1,0:T(8,128)(2,1)}, bf16[2,48,3072]{2,1,0:T(8,128)(2,1)}, bf16[2,48,768]{2,1,0:T(8,128)(2,1)}...) custom-call(s32[4]{0:T(128)} %length_ref.5, bf16[1024,2304]{1,0:T(8,128)(2,1)} %get-tuple-element.40.q_ref.k_ref.v_ref, ...), custom_call_target="tpu_custom_call" | custom-call | tf_op jit(solution)/shard_map/back/pallas_call | solution.py:911
  256.6 0.0 copy-done
  256.6 0.0 copy-start.1
  256.6 1.4 copy-done.1
  258.0 0.0 copy-start.2
  258.0 1.1 copy-done.2
  259.1 0.0 copy-start.3
  259.1 1.1 copy-done.3
  260.1 0.0 copy-start.4
  260.1 1.0 copy-done.4
  261.2 0.0 copy-start.5
  261.2 0.9 copy-done.5
  262.1 3.5 %finish.1 = (bf16[4,256,768]{2,1,0:T(8,128)(2,1)}, bf16[4,256,768]{2,1,0:T(8,128)(2,1)}, f32[96,2304]{1,0:T(8,128)}, f32[96,768]{1,0:T(8,128)}, f32[96,3072]{1,0:T(8,128)}, /*index=5*/f32[384,768]{1,0:T(8,128)}) custom-call(bf16[4,256,768]{2,1,0:T(8,128)(2,1)S(1)} %copy-done, bf16[4,256,768]{2,1,0:T(8,128)(2,1)S(1)} %copy-done.1, ...), custom_call_target="tpu_custom_call" | custom-call | tf_op jit(solution)/shard_map/finish/pallas_call | solution.py:1016
  265.5 0.8 constant_dynamic-slice_fusion
  266.3 0.5 slice_bitcast_fusion
Async XLA Ops:
  131.9 124.7 %copy-start = (bf16[4,256,768]{2,1,0:T(8,128)(2,1)S(1)}, bf16[4,256,768]{2,1,0:T(8,128)(2,1)}, u32[]{:S(2)}) copy-start(bf16[4,256,768]{2,1,0:T(8,128)(2,1)} %get-tuple-element.39.output) | copy-start | bytes 4718596
  256.6 1.4 copy-start.1
  258.0 1.1 copy-start.2
  259.1 1.1 copy-start.3
  260.1 1.0 copy-start.4
  261.2 0.9 copy-start.5

commit v5 on v4

--- a/solution.py
+++ b/solution.py
@@ -602,24 +602,23 @@
 
 
 PLAN = {
-    (0, 0): [(0, 2), (1, 0), (2, 0)],
-    (1, 0): [(1, 1)],
-    (1, 1): [(0, 3)],
-    (2, 0): [(0, 4), (3, 0)],
-    (2, 3): [(1, 2), (2, 1), (3, 1)],
-    (3, 2): [(2, 2), (3, 2)],
-    (3, 3): [(1, 3), (2, 3)],
-    (4, 0): [(0, 5), (4, 0), (3, 3)],
-    (4, 2): [(1, 4), (2, 4), (4, 1)],
-    (5, 0): [(3, 4), (4, 2)],
-    (5, 2): [(2, 5), (4, 3)],
-    (5, 3): [(3, 5), (4, 4)],
+    (0, "start"): [(2, 0), (1, 0), (0, 2)],
+    (1, "start"): [(2, 1), (1, 1), (0, 3)],
+    (1, "end"): [(2, 2)],
+    (2, "start"): [(0, 4), (3, 0)],
+    (3, "start"): [(1, 2), (2, 3)],
+    (3, "end"): [(2, 4), (3, 1), (1, 3)],
+    (4, "start"): [(0, 5)],
+    (5, "start"): [(3, 2), (4, 0), (1, 4)],
 }
-PLAN_BEFORE_NORM = [(1, 5), (4, 5)]
-PLAN_AFTER_NORM = [
-    (5, 0), "v0", (5, 1), "v1", (5, 2), "v2", (5, 3), "v3", (0, 6), (2, 6), (3, 6), (1, 6), (4, 6),
-    (5, 4), "v4", (5, 5), "v5", (5, 6),
+PLAN_BEFORE_NORM = [(3, 3)]
+PLAN_AFTER_NORM = ["t0", "v0", "v1", "t1"]
+PLAN_LAST = [
+    (5, 0), (4, 1), (5, 1), "v2", (3, 4), (5, 2), (5, 3), (1, 5), (2, 5), "v3", (4, 2), "t2",
+    (2, 6), (4, 3), (3, 5), (0, 6), (5, 4), "v4", (4, 4), "t3", (1, 6), (5, 5), "v5", (3, 6),
+    (4, 5), (5, 6), (4, 6),
 ]
+TOKEN_PIECES = 4
 
 
 def back_kernel(
@@ -660,7 +659,23 @@
                 )
             )
 
+    def token_copy(row, piece, slot):
+        size = block // TOKEN_PIECES
+        rows_there = slice(piece * size, (piece + 1) * size)
+        return to_partner(
+            staged.at[row, rows_there], grad_tokens.at[slot, rows_there],
+            token_send.at[row, piece], token_recv.at[slot, piece], {"ctx": row},
+        )
+
     def run(name):
+        if name[0] == "t":
+            for row in range(blocks):
+
+                @pl.when(row != me)
+                def _():
+                    token_copy(row, int(name[1:]), me).start()
+
+            return
         if not fast:
             return
         if isinstance(name, tuple):
@@ -694,22 +709,26 @@
         for load in loads:
             load.start()
 
-    def hook(i):
+    def hook(place):
         for group in range(groups):
-            if (group, i) in PLAN:
+            if (group, place) in PLAN:
 
                 @pl.when(step == group)
                 def _():
-                    for name in PLAN[group, i]:
+                    for name in PLAN[group, place]:
                         run(name)
+
+    hook("start")
 
     @pl.when(step < groups)
     def _():
         side = pl.ds(pl.multiple_of((step % 2) * LANES, LANES), LANES)
         attend_backward(
-            hook, side, length_ref[me], q_ref, k_ref, v_ref, mixed_ref, grad_ref, log_ref, pair,
+            side, length_ref[me], q_ref, k_ref, v_ref, mixed_ref, grad_ref, log_ref, pair,
             k_t, grad_q_t, probs_low, grads_low, sum_k, sum_v,
         )
+
+    hook("end")
 
     @pl.when(step == 1)
     def _():
@@ -740,11 +759,6 @@
         @pl.when(step < groups - 1)
         def _():
             weight_gradient(part)
-
-    def token_copy(row):
-        return to_partner(
-            staged.at[row], grad_tokens.at[me], token_send.at[row], token_recv.at[me], {"ctx": row}
-        )
 
     own_tokens = pltpu.make_async_copy(staged.at[me], grad_tokens.at[me], local.at[4])
 
@@ -762,17 +776,12 @@
             total = middle[there, :] + normalise_backward(grad, hat, inverse, row_of(gain))
             staged[row] = total.astype(BF16)
 
-            @pl.when(row != me)
-            def _():
-                token_copy(row).start()
-
-            @pl.when(row == me)
-            def _():
-                own_tokens.start()
-
+        own_tokens.start()
         vectors[0] = jnp.concatenate([gain_sum, shift_sum, norm_two[0:6, :]], axis=0)
+        for name in PLAN_AFTER_NORM:
+            run(name)
         weight_gradient(PARTS - 1)
-        for name in PLAN_AFTER_NORM:
+        for name in PLAN_LAST:
             run(name)
         if fast:
             for number in range(3):
@@ -788,15 +797,13 @@
 
             @pl.when(row != me)
             def _():
-                token_copy(row).wait_send()
-                to_partner(
-                    staged.at[row], grad_tokens.at[row], token_send.at[row], token_recv.at[row],
-                    {"ctx": row},
-                ).wait_recv()
+                for piece in range(TOKEN_PIECES):
+                    token_copy(row, piece, me).wait_send()
+                    token_copy(row, piece, row).wait_recv()
 
 
 def attend_backward(
-    hook, side, length, q_ref, k_ref, v_ref, mixed_ref, grad_ref, log_ref, pair,
+    side, length, q_ref, k_ref, v_ref, mixed_ref, grad_ref, log_ref, pair,
     k_t, grad_q_t, probs_low, grads_low, sum_k, sum_v,
 ):
     count = q_ref.shape[0] // BLOCK
@@ -825,8 +832,6 @@
     for number, (i, head) in enumerate(steps):
         below = i * BLOCK
         span = below + BLOCK
-        if head == 0:
-            hook(i)
         following = products_of(*steps[number + 1]) if number + 1 < len(steps) else None
         scores, grad_probs = current
         scores = mask_diagonal(scores, BLOCK, below, length)
@@ -903,8 +908,8 @@
         pltpu.VMEM((6, 8, width), F32),
         pltpu.VMEM((5, 8, width), F32),
         pltpu.SemaphoreType.DMA((5 + 3 + PARTS,)),
-        pltpu.SemaphoreType.DMA((blocks,)),
-        pltpu.SemaphoreType.DMA((blocks,)),
+        pltpu.SemaphoreType.DMA((blocks, TOKEN_PIECES)),
+        pltpu.SemaphoreType.DMA((blocks, TOKEN_PIECES)),
         pltpu.SemaphoreType.DMA((5,)),
         pltpu.SemaphoreType.DMA((5,)),
     ]
@@ -986,14 +991,23 @@
 
 
 def finish_kernel(output, tokens, qkv, out, up, down, *results):
-    *results, copies = results
-    output_out, tokens_out, qkv_out, out_out, up_out, down_out = results[:6]
+    output_out, tokens_out, qkv_out, out_out, up_out, down_out, *held, copies = results
+    sources = (output, tokens, qkv, out, up, down)
+    loads = [
+        pltpu.make_async_copy(source, target, copies.at[number])
+        for number, (source, target) in enumerate(zip(sources, held))
+    ]
+    for load in loads:
+        load.start()
+    for load in loads:
+        load.wait()
     moves = [
-        pltpu.make_async_copy(output, output_out, copies.at[0]),
-        pltpu.make_async_copy(tokens, tokens_out, copies.at[1]),
+        pltpu.make_async_copy(held[0], output_out, copies.at[0]),
+        pltpu.make_async_copy(held[1], tokens_out, copies.at[1]),
     ]
     for move in moves:
         move.start()
+    qkv, out, up, down = held[2:]
     for source, target in ((out, out_out), (up, up_out), (down, down_out)):
         rows = source.shape[1]
         for half in range(2):
@@ -1013,10 +1027,11 @@
 def finish(output, tokens, qkv, out, up, down):
     flat = lambda part: struct((2 * part.shape[1], part.shape[2]), F32)
     memory = pl.BlockSpec(memory_space=pltpu.VMEM)
+    held = pl.BlockSpec(memory_space=pltpu.HBM)
     return pl.pallas_call(
         finish_kernel,
-        in_specs=[ANY, ANY] + [memory] * 4,
-        out_specs=[ANY, ANY] + [memory] * 4,
+        in_specs=[held] * 6,
+        out_specs=[held, held] + [memory] * 4,
         out_shape=[
             struct(output.shape),
             struct(tokens.shape),
@@ -1025,8 +1040,9 @@
             flat(up),
             flat(down),
         ],
-        scratch_shapes=[pltpu.SemaphoreType.DMA((2,))],
-        compiler_params=pltpu.CompilerParams(vmem_limit_bytes=24 * MIB),
+        scratch_shapes=[pltpu.VMEM(part.shape, BF16) for part in (output, tokens, qkv, out, up, down)]
+        + [pltpu.SemaphoreType.DMA((6,))],
+        compiler_params=pltpu.CompilerParams(vmem_limit_bytes=VMEM_LIMIT),
         name="finish",
     )(output, tokens, qkv, out, up, down)
 

time: 268 us -> 254 us (0.948)
  Pallas kernels: 259 us -> 251 us
  local copies, waits for them, and re-layouts: 6.76 us -> 1.3 us
    pallas_call x1, Pallas kernels: 125 us -> 114 us  [back(): pl.pallas_call(functools.partial(back_kernel, fast, ctx), grid=(groups +...]
    unnamed x12 -> x0, local copies, waits for them, and re-layouts: 5.45 us -> none
where the time goes in v5:
time: 254 us; the launch traced here: 253 us
  Pallas kernels  251 us (99%)
    pallas_call x1, Pallas kernels, back(): pl.pallas_call(functools.partial(back_kernel, fast, ctx), grid=(groups +...  114 us
    pallas_call x1, Pallas kernels, front(): pl.pallas_call(functools.partial(front_kernel, ctx), grid=(1 + groups,),...  77.4 us
    pallas_call x1, Pallas kernels, feed_forward(): pl.pallas_call(functools.partial(feed_forward_kernel, fast, blocks), grid...  53.8 us
    pallas_call x1, Pallas kernels, finish(): pl.pallas_call(finish_kernel, in_specs=[held] * 6, out_specs=[held, held]...  5.87 us

profile of v5, /device:TPU:0, one launch (start us, length us, event | category | flops | bytes accessed | tf_op | source)
XLA Modules:
  0.0 253.4 jit_solution(15370139081878599944)
XLA Ops:
  0.6 77.4 %front.1 = (bf16[4,256,768]{2,1,0:T(8,128)(2,1)}, bf16[1024,768]{1,0:T(8,128)(2,1)}, bf16[1024,2304]{1,0:T(8,128)(2,1)}, bf16[4,256,768]{2,1,0:T(8,128)(2,1)}, b...) custom-call(s32[4]{0:T(128)} %length_ref.5, bf16[4,256,768]{2,1,0:T(8,128)(2,1)} %tokens.1, ...), custom_call_target="tpu_custom_call" | custom-call | tf_op jit(solution)/shard_map/front/pallas_call | solution.py:202
  78.1 53.8 %feed_forward.1 = (bf16[4,256,768]{2,1,0:T(8,128)(2,1)}, bf16[8,128]{1,0:T(8,128)(2,1)}, f32[1024,768]{1,0:T(8,128)}, bf16[1024,768]{1,0:T(8,128)(2,1)}, bf16[76...) custom-call(s32[4]{0:T(128)} %length_ref.5, ...), custom_call_target="tpu_custom_call" | custom-call | tf_op jit(solution)/shard_map/feed_forward/pallas_call | solution.py:536
  131.9 114.3 %back.1 = (bf16[4,256,768]{2,1,0:T(8,128)(2,1)}, bf16[2,192,768]{2,1,0:T(8,128)(2,1)}, bf16[2,48,3072]{2,1,0:T(8,128)(2,1)}, bf16[2,48,768]{2,1,0:T(8,128)(2,1)}...) custom-call(s32[4]{0:T(128)} %length_ref.5, bf16[1024,2304]{1,0:T(8,128)(2,1)} %get-tuple-element.40.q_ref.k_ref.v_ref, ...), custom_call_target="tpu_custom_call" | custom-call | tf_op jit(solution)/shard_map/back/pallas_call | solution.py:916
  246.2 5.9 %finish.1 = (bf16[4,256,768]{2,1,0:T(8,128)(2,1)}, bf16[4,256,768]{2,1,0:T(8,128)(2,1)}, f32[96,2304]{1,0:T(8,128)}, f32[96,768]{1,0:T(8,128)}, f32[96,3072]{1,0:T(8,128)}, /*index=5*/f32[384,768]{1,0:T(8,128)}) custom-call(bf16[4,256,768]{2,1,0:T(8,128)(2,1)} %get-tuple-element.39.output, bf16[4,256,768]{2,1,0:T(8,128)(2,1)} %get-tuple-element.50.tokens, ...), custom_call_target="tpu_custom_call" | custom-call | tf_op jit(solution)/shard_map/finish/pallas_call | solution.py:1031
  252.1 0.8 constant_dynamic-slice_fusion
  252.9 0.5 slice_bitcast_fusion

commit v6 on v5

--- a/solution.py
+++ b/solution.py
@@ -20,6 +20,7 @@
 epsilon = 1e-05
 MIB = 2**20
 VMEM_LIMIT = 62 * MIB
+COT_TAIL = 64
 ANY = pl.BlockSpec(memory_space=pl.ANY)
 SMEM = pl.BlockSpec(memory_space=pltpu.SMEM)
 ONE = pl.Buffered(1)
@@ -142,11 +143,11 @@
 
     def cotangent_copy(offset):
         return to_partner(
-            cotangent.at[me ^ offset], cotangent_out.at[me], cot_send.at[offset],
+            cotangent.at[me ^ offset, 0:head], cotangent_out.at[me], cot_send.at[offset],
             cot_recv.at[offset], {"ctx": me ^ offset},
         )
 
-    own_cotangent = pltpu.make_async_copy(cotangent.at[me], cotangent_out.at[me], local.at[1])
+    head = cotangent_out.shape[1]
     keeps = [
         pltpu.make_async_copy(inputs, inputs_out, local.at[2]),
         pltpu.make_async_copy(normed, normed_out, local.at[3]),
@@ -175,7 +176,6 @@
             if offset == offsets[-1]:
                 for earlier in offsets:
                     token_copy(earlier).wait_send()
-                own_cotangent.start()
                 for later in offsets[::-1]:
                     cotangent_copy(later).start()
             project(me ^ offset)
@@ -190,7 +190,6 @@
     def _():
         for keep in keeps:
             keep.wait()
-        own_cotangent.wait()
         for offset in offsets:
             cotangent_copy(offset).wait()
 
@@ -212,7 +211,7 @@
             struct(tokens.shape),
             struct((rows, width)),
             struct((rows, 3 * width)),
-            struct(tokens.shape),
+            struct((blocks, block - COT_TAIL, width)),
             struct((rows, width)),
             struct((groups, HEADS, rows), F32),
         ],
@@ -333,8 +332,8 @@
 
 
 def feed_forward_kernel(
-    fast, blocks, length_ref, inputs, mixed, out_weight, gain, shift, up_in, down_in,
-    cotangent_in,
+    fast, blocks, length_ref, inputs, mixed, out_weight, gain, shift, up_in, down_in, cot_head,
+    cot_in,
     output, grad_down_out, grad_middle_ref, grad_mixed_ref, grad_up_ref, grad_out_ref,
     grad_norm_ref, *rest,
 ):
@@ -342,7 +341,8 @@
     take = lambda count: [rest.pop(0) for _ in range(count)]
     carried = take(2) if fast else []
     (up_weight, down_weight, normed, upstream, branch, active, hidden, scaled, inverse_of) = take(9)
-    (staged, cotangent, grad_down, output_send, output_recv, local) = take(6)
+    (staged, cotangent, grad_down) = take(3)
+    (output_send, output_recv, cot_send, cot_recv, local) = take(5)
     step = pl.program_id(0)
     seq, me = lax.axis_index("seq"), lax.axis_index("ctx")
     block, width = staged.shape[1:]
@@ -364,7 +364,21 @@
         )
 
     own_output = pltpu.make_async_copy(staged.at[me], output.at[me], local.at[0])
-    cotangent_load = pltpu.make_async_copy(cotangent_in, cotangent, local.at[4])
+    head = cot_head.shape[1]
+    own_cotangent = pltpu.make_async_copy(cot_in.at[me], cotangent.at[me], local.at[4])
+
+    def head_copy(offset):
+        other = me ^ offset
+        return pltpu.make_async_copy(
+            cot_head.at[other], cotangent.at[other, 0:head], local.at[4 + offset]
+        )
+
+    def tail_copy(offset):
+        return to_partner(
+            cot_in.at[me ^ offset, head:block], cotangent.at[me, head:block],
+            cot_send.at[offset], cot_recv.at[offset], {"ctx": me ^ offset},
+        )
+
     up_load = pltpu.make_async_copy(up_in, up_weight, local.at[1])
     down_load = pltpu.make_async_copy(down_in, down_weight, local.at[2])
 
@@ -376,7 +390,10 @@
         if fast:
             partners += [{"seq": seq ^ 1}, {"seq": seq ^ 2}, {"seq": seq ^ 4}]
         greet(partners)
-        cotangent_load.start()
+        own_cotangent.start()
+        for offset in range(blocks - 1, 0, -1):
+            tail_copy(offset).start()
+            head_copy(offset).start()
         grad_norm_ref[...] = jnp.zeros_like(grad_norm_ref)
 
     def rows_of(number):
@@ -389,6 +406,15 @@
     @pl.when(step < blocks)
     def _():
         row = me ^ ((step + blocks // 2) % blocks)
+
+        @pl.when(step == blocks - 1)
+        def _():
+            for offset in range(1, blocks):
+                tail_copy(offset).wait()
+            output_copy(me ^ 2).start()
+            output_copy(me ^ 3).start()
+            own_output.start()
+
         rows = rows_of(row)
         middle = inputs[row].astype(F32) + dot(mixed[rows, :], out_weight[...], 1, 0)
         hat, inverse = normalise(middle)
@@ -416,17 +442,15 @@
             current = following
         staged[row] = jnp.where(valid_rows(row), total, 0.0).astype(BF16)
 
-        @pl.when(row != me)
+        @pl.when(step == blocks - 1)
         def _():
             output_copy(row).start()
 
-        @pl.when(row == me)
-        def _():
-            own_output.start()
-
     @pl.when(step == blocks)
     def _():
-        cotangent_load.wait()
+        own_cotangent.wait()
+        for offset in range(1, blocks):
+            head_copy(offset).wait()
         for row in range(blocks):
             kept = jnp.where(valid_rows(row), cotangent[row], 0)
             upstream[row * block : (row + 1) * block, :] = kept
@@ -509,7 +533,8 @@
 
 
 def feed_forward(
-    fast, length, inputs, mixed, cotangent, out_weight, up_weight, down_weight, gain, shift
+    fast, length, inputs, mixed, cot_head, cotangent, out_weight, up_weight, down_weight, gain,
+    shift,
 ):
     blocks, block, width = inputs.shape
     rows, wide = blocks * block, up_weight.shape[1]
@@ -538,7 +563,7 @@
         grid=(steps,),
         in_specs=[SMEM]
         + [whole(operand.shape) for operand in operands]
-        + [VECTOR, VECTOR, ANY, ANY, ANY],
+        + [VECTOR, VECTOR, ANY, ANY, ANY, ANY],
         out_specs=[
             ANY,
             ANY,
@@ -574,14 +599,16 @@
             pltpu.VMEM(lead + (piece, width), BF16),
             pltpu.SemaphoreType.DMA((blocks,)),
             pltpu.SemaphoreType.DMA((blocks,)),
-            pltpu.SemaphoreType.DMA((5,)),
+            pltpu.SemaphoreType.DMA((blocks,)),
+            pltpu.SemaphoreType.DMA((blocks,)),
+            pltpu.SemaphoreType.DMA((4 + blocks,)),
         ]
         + extra,
         compiler_params=pltpu.CompilerParams(
             vmem_limit_bytes=VMEM_LIMIT, collective_id=1, has_side_effects=True
         ),
         name="feed_forward",
-    )(length, *operands, gain, shift, up_weight, down_weight, cotangent)
+    )(length, *operands, gain, shift, up_weight, down_weight, cot_head, cotangent)
 
 
 def chunk_scratch(rows, columns, number):
@@ -669,12 +696,8 @@
 
     def run(name):
         if name[0] == "t":
-            for row in range(blocks):
-
-                @pl.when(row != me)
-                def _():
-                    token_copy(row, int(name[1:]), me).start()
-
+            for offset in range(ctx - 1, 0, -1):
+                token_copy(me ^ offset, int(name[1:]), me).start()
             return
         if not fast:
             return
@@ -766,18 +789,19 @@
     def _():
         for name in PLAN_BEFORE_NORM:
             run(name)
-        gain_sum, shift_sum = 0.0, 0.0
-        for row in range(blocks):
-            there = slice(row * block, (row + 1) * block)
+        vectors[0] = jnp.concatenate([jnp.zeros((2, width), F32), norm_two[0:6, :]], axis=0)
+
+        @pl.loop(0, blocks)
+        def _(row):
+            there = pl.ds(pl.multiple_of(row * block, block), block)
             hat, inverse = normalise(inputs[row].astype(F32))
             grad = grad_normed[there, :]
-            gain_sum = gain_sum + jnp.sum(grad * hat, axis=0, keepdims=True)
-            shift_sum = shift_sum + jnp.sum(grad, axis=0, keepdims=True)
+            vectors[0, 0:1, :] += jnp.sum(grad * hat, axis=0, keepdims=True)
+            vectors[0, 1:2, :] += jnp.sum(grad, axis=0, keepdims=True)
             total = middle[there, :] + normalise_backward(grad, hat, inverse, row_of(gain))
             staged[row] = total.astype(BF16)
 
         own_tokens.start()
-        vectors[0] = jnp.concatenate([gain_sum, shift_sum, norm_two[0:6, :]], axis=0)
         for name in PLAN_AFTER_NORM:
             run(name)
         weight_gradient(PARTS - 1)
@@ -991,57 +1015,53 @@
 
 
 def finish_kernel(output, tokens, qkv, out, up, down, *results):
-    output_out, tokens_out, qkv_out, out_out, up_out, down_out, *held, copies = results
+    targets, held, wide, copies = results[:6], results[6:12], results[12:16], results[16]
     sources = (output, tokens, qkv, out, up, down)
     loads = [
         pltpu.make_async_copy(source, target, copies.at[number])
         for number, (source, target) in enumerate(zip(sources, held))
     ]
+    stores = [
+        pltpu.make_async_copy(source, target, copies.at[6 + number])
+        for number, (source, target) in enumerate(zip(list(held[:2]) + list(wide), targets))
+    ]
     for load in loads:
         load.start()
-    for load in loads:
-        load.wait()
-    moves = [
-        pltpu.make_async_copy(held[0], output_out, copies.at[0]),
-        pltpu.make_async_copy(held[1], tokens_out, copies.at[1]),
-    ]
-    for move in moves:
-        move.start()
-    qkv, out, up, down = held[2:]
-    for source, target in ((out, out_out), (up, up_out), (down, down_out)):
-        rows = source.shape[1]
-        for half in range(2):
-            target[half * rows : (half + 1) * rows, :] = source[half].astype(F32)
-    rows, width = qkv.shape[2:]
-    step = width // 3
-    for part in range(PARTS):
-        for half in range(2):
-            for name in range(3):
-                first = name * width + part * step
-                value = qkv[part, half, :, name * step : (name + 1) * step]
-                qkv_out[half * rows : (half + 1) * rows, first : first + step] = value.astype(F32)
-    for move in moves:
-        move.wait()
+    for number in range(6):
+        loads[number].wait()
+        source = held[number]
+        if number == 2:
+            rows, width = source.shape[2:]
+            step = width // 3
+            for part in range(PARTS):
+                for half in range(2):
+                    for name in range(3):
+                        first = name * width + part * step
+                        value = source[part, half, :, name * step : (name + 1) * step]
+                        wide[0][half * rows : (half + 1) * rows, first : first + step] = (
+                            value.astype(F32)
+                        )
+        if number > 2:
+            rows = source.shape[1]
+            for half in range(2):
+                there = slice(half * rows, (half + 1) * rows)
+                wide[number - 2][there, :] = source[half].astype(F32)
+        stores[number].start()
+    for store in stores:
+        store.wait()
 
 
 def finish(output, tokens, qkv, out, up, down):
     flat = lambda part: struct((2 * part.shape[1], part.shape[2]), F32)
-    memory = pl.BlockSpec(memory_space=pltpu.VMEM)
-    held = pl.BlockSpec(memory_space=pltpu.HBM)
+    wide = [struct((2 * qkv.shape[2], 3 * qkv.shape[3]), F32), flat(out), flat(up), flat(down)]
     return pl.pallas_call(
         finish_kernel,
-        in_specs=[held] * 6,
-        out_specs=[held, held] + [memory] * 4,
-        out_shape=[
-            struct(output.shape),
-            struct(tokens.shape),
-            struct((2 * qkv.shape[2], 3 * qkv.shape[3]), F32),
-            flat(out),
-            flat(up),
-            flat(down),
-        ],
+        in_specs=[ANY] * 6,
+        out_specs=[ANY] * 6,
+        out_shape=[struct(output.shape), struct(tokens.shape)] + wide,
         scratch_shapes=[pltpu.VMEM(part.shape, BF16) for part in (output, tokens, qkv, out, up, down)]
-        + [pltpu.SemaphoreType.DMA((6,))],
+        + [pltpu.VMEM(part.shape, F32) for part in wide]
+        + [pltpu.SemaphoreType.DMA((12,))],
         compiler_params=pltpu.CompilerParams(vmem_limit_bytes=VMEM_LIMIT),
         name="finish",
     )(output, tokens, qkv, out, up, down)
@@ -1064,13 +1084,13 @@
         cotangent,
     ):
         width = tokens.shape[-1]
-        inputs, normed_low, packed, cotangent, mixed_low, logs = front(
+        inputs, normed_low, packed, cot_head, mixed_low, logs = front(
             ctx_size, lengths, tokens, cotangent, query_key_value_weight, ln1_gain, ln1_shift
         )
         (
             output, grad_down, grad_middle, grad_mixed, grad_up, grad_out, grad_norm_two, *carried
         ) = feed_forward(
-            fast, lengths, inputs, mixed_low, cotangent, attention_out_weight, up_weight,
+            fast, lengths, inputs, mixed_low, cot_head, cotangent, attention_out_weight, up_weight,
             down_weight, ln2_gain, ln2_shift,
         )
         partials = carried + [grad_up, grad_out]

time: 254 us -> 248 us (0.976)
  Pallas kernels: 251 us -> 246 us
    pallas_call x1, Pallas kernels: 77.4 us -> 71.9 us  [front(): pl.pallas_call(functools.partial(front_kernel, ctx), grid=(1 + groups,),...]
where the time goes in v6:
time: 248 us
  Pallas kernels  246 us (99%)
    pallas_call x1, Pallas kernels, back(): pl.pallas_call(functools.partial(back_kernel, fast, ctx), grid=(groups +...  116 us
    pallas_call x1, Pallas kernels, front(): pl.pallas_call(functools.partial(front_kernel, ctx), grid=(1 + groups,),...  71.9 us
    pallas_call x1, Pallas kernels, feed_forward(): pl.pallas_call(functools.partial(feed_forward_kernel, fast, blocks), grid...  54 us

profile of v6, /device:TPU:0, one launch (start us, length us, event | category | flops | bytes accessed | tf_op | source)
XLA Modules:
  0.0 247.9 jit_solution(410182354531052518)
XLA Ops:
  0.6 71.9 %front.1 = (bf16[4,256,768]{2,1,0:T(8,128)(2,1)}, bf16[1024,768]{1,0:T(8,128)(2,1)}, bf16[1024,2304]{1,0:T(8,128)(2,1)}, bf16[4,192,768]{2,1,0:T(8,128)(2,1)}, b...) custom-call(s32[4]{0:T(128)} %length_ref.5, bf16[4,256,768]{2,1,0:T(8,128)(2,1)} %tokens.1, bf16[4,256,768]{2,1,0:T(8,128)(2,1)} %cot_in.1, ...), custom_call_target="tpu_custom_call" | custom-call | tf_op jit(solution)/shard_map/front/pallas_call | solution.py:201
  72.5 54.0 %feed_forward.1 = (bf16[4,256,768]{2,1,0:T(8,128)(2,1)}, bf16[8,128]{1,0:T(8,128)(2,1)}, f32[1024,768]{1,0:T(8,128)}, bf16[1024,768]{1,0:T(8,128)(2,1)}, bf16[76...) custom-call(s32[4]{0:T(128)} %length_ref.5, ...), custom_call_target="tpu_custom_call" | custom-call | tf_op jit(solution)/shard_map/feed_forward/pallas_call | solution.py:561
  126.5 115.8 %back.1 = (bf16[4,256,768]{2,1,0:T(8,128)(2,1)}, bf16[2,192,768]{2,1,0:T(8,128)(2,1)}, bf16[2,48,3072]{2,1,0:T(8,128)(2,1)}, bf16[2,48,768]{2,1,0:T(8,128)(2,1)}...) custom-call(s32[4]{0:T(128)} %length_ref.5, bf16[1024,2304]{1,0:T(8,128)(2,1)} %get-tuple-element.40.q_ref.k_ref.v_ref, ...), custom_call_target="tpu_custom_call" | custom-call | tf_op jit(solution)/shard_map/back/pallas_call | solution.py:940
  242.3 4.3 %finish.1 = (bf16[4,256,768]{2,1,0:T(8,128)(2,1)}, bf16[4,256,768]{2,1,0:T(8,128)(2,1)}, f32[96,2304]{1,0:T(8,128)}, f32[96,768]{1,0:T(8,128)}, f32[96,3072]{1,0:T(8,128)}, /*index=5*/f32[384,768]{1,0:T(8,128)}) custom-call(bf16[4,256,768]{2,1,0:T(8,128)(2,1)} %get-tuple-element.39.output, bf16[4,256,768]{2,1,0:T(8,128)(2,1)} %get-tuple-element.50.tokens, ...), custom_call_target="tpu_custom_call" | custom-call | tf_op jit(solution)/shard_map/finish/pallas_call | solution.py:1057
  246.6 0.8 constant_dynamic-slice_fusion
  247.4 0.5 slice_bitcast_fusion

commit v7 on v6

--- a/solution.py
+++ b/solution.py
@@ -101,7 +101,10 @@
     columns = [
         pl.ds(pl.multiple_of(part * width + group * LANES, LANES), LANES) for part in range(3)
     ]
-    v_t[...] = packed[:, columns[2]].T
+    values = packed[:, columns[2]].T
+    for head in range(HEADS):
+        v_t[head, 0:HD, :] = values[head * HD : (head + 1) * HD, :]
+        v_t[head, HD:, :] = jnp.ones((v_t.shape[1] - HD, rows), BF16)
 
     def scores_of(i, head):
         span = (i + 1) * BLOCK
@@ -116,9 +119,9 @@
         following = scores_of(*steps[number + 1]) if number + 1 < len(steps) else None
         summit = jnp.max(scores, axis=0, keepdims=True)
         expo = jnp.exp2(scores * SCALE_LOG2 - summit * SCALE_LOG2)
-        denom = jnp.sum(expo, axis=0, keepdims=True)
-        part = dot(v_t[head * HD : (head + 1) * HD, 0:span], expo.astype(BF16), 1, 0)
-        mixed_t[head * HD : (head + 1) * HD, :] = part / denom
+        part = dot(v_t[head, :, 0:span], expo.astype(BF16), 1, 0)
+        denom = part[HD : HD + 1]
+        mixed_t[head * HD : (head + 1) * HD, :] = part[:HD] / denom
         log_ref[0, head : head + 1, i * BLOCK : span] = summit * SCALE_LOG2 + jnp.log2(denom)
         if head == HEADS - 1:
             mixed_ref[i * BLOCK : span, :] = mixed_t[...].T.astype(BF16)
@@ -219,7 +222,7 @@
             pltpu.VMEM(tokens.shape, BF16),
             pltpu.VMEM((rows, width), BF16),
             pltpu.VMEM((rows, 3 * width), BF16),
-            pltpu.VMEM((LANES, rows), BF16),
+            pltpu.VMEM((HEADS, HD + 16, rows), BF16),
             pltpu.VMEM((LANES, BLOCK), F32),
             pltpu.SemaphoreType.DMA((ctx,)),
             pltpu.SemaphoreType.DMA((ctx,)),
@@ -332,7 +335,7 @@
 
 
 def feed_forward_kernel(
-    fast, blocks, length_ref, inputs, mixed, out_weight, gain, shift, up_in, down_in, cot_head,
+    fast, blocks, length_ref, gain, shift, inputs_in, mixed_in, out_in, up_in, down_in, cot_head,
     cot_in,
     output, grad_down_out, grad_middle_ref, grad_mixed_ref, grad_up_ref, grad_out_ref,
     grad_norm_ref, *rest,
@@ -341,7 +344,7 @@
     take = lambda count: [rest.pop(0) for _ in range(count)]
     carried = take(2) if fast else []
     (up_weight, down_weight, normed, upstream, branch, active, hidden, scaled, inverse_of) = take(9)
-    (staged, cotangent, grad_down) = take(3)
+    (staged, cotangent, grad_down, inputs, mixed, out_weight) = take(6)
     (output_send, output_recv, cot_send, cot_recv, local) = take(5)
     step = pl.program_id(0)
     seq, me = lax.axis_index("seq"), lax.axis_index("ctx")
@@ -382,8 +385,16 @@
     up_load = pltpu.make_async_copy(up_in, up_weight, local.at[1])
     down_load = pltpu.make_async_copy(down_in, down_weight, local.at[2])
 
+    first_loads = [
+        pltpu.make_async_copy(out_in, out_weight, local.at[4 + blocks]),
+        pltpu.make_async_copy(mixed_in, mixed, local.at[5 + blocks]),
+        pltpu.make_async_copy(inputs_in, inputs, local.at[6 + blocks]),
+    ]
+
     @pl.when(step == 0)
     def _():
+        for load in first_loads:
+            load.start()
         up_load.start()
         down_load.start()
         partners = [{"ctx": me ^ offset} for offset in range(1, blocks)]
@@ -395,6 +406,8 @@
             tail_copy(offset).start()
             head_copy(offset).start()
         grad_norm_ref[...] = jnp.zeros_like(grad_norm_ref)
+        for load in first_loads:
+            load.wait()
 
     def rows_of(number):
         return pl.ds(pl.multiple_of(number * block, block), block)
@@ -538,12 +551,12 @@
 ):
     blocks, block, width = inputs.shape
     rows, wide = blocks * block, up_weight.shape[1]
-    size = 512
+    size = 1024
     late = 2 * blocks + 1
     steps = late + wide // size
     back_row = lambda step: jnp.clip(step - blocks - 1, 0, blocks - 1)
     up_part = lambda step: jnp.maximum(step - late, 0)
-    operands = (inputs, mixed, out_weight)
+    operands = (inputs, mixed, out_weight, up_weight, down_weight, cot_head, cotangent)
     piece = wide // PIECES // 2
     lead = (2, 2, 2, 2)
     half = (2, 2, piece, width // 2)
@@ -561,9 +574,7 @@
     return pl.pallas_call(
         functools.partial(feed_forward_kernel, fast, blocks),
         grid=(steps,),
-        in_specs=[SMEM]
-        + [whole(operand.shape) for operand in operands]
-        + [VECTOR, VECTOR, ANY, ANY, ANY, ANY],
+        in_specs=[SMEM, VECTOR, VECTOR] + [ANY] * len(operands),
         out_specs=[
             ANY,
             ANY,
@@ -597,18 +608,21 @@
             pltpu.VMEM(inputs.shape, BF16),
             pltpu.VMEM(inputs.shape, BF16),
             pltpu.VMEM(lead + (piece, width), BF16),
+            pltpu.VMEM(inputs.shape, BF16),
+            pltpu.VMEM(mixed.shape, BF16),
+            pltpu.VMEM(out_weight.shape, BF16),
             pltpu.SemaphoreType.DMA((blocks,)),
             pltpu.SemaphoreType.DMA((blocks,)),
             pltpu.SemaphoreType.DMA((blocks,)),
             pltpu.SemaphoreType.DMA((blocks,)),
-            pltpu.SemaphoreType.DMA((4 + blocks,)),
+            pltpu.SemaphoreType.DMA((7 + blocks,)),
         ]
         + extra,
         compiler_params=pltpu.CompilerParams(
             vmem_limit_bytes=VMEM_LIMIT, collective_id=1, has_side_effects=True
         ),
         name="feed_forward",
-    )(length, *operands, gain, shift, up_weight, down_weight, cot_head, cotangent)
+    )(length, gain, shift, *operands)
 
 
 def chunk_scratch(rows, columns, number):
@@ -639,12 +653,8 @@
     (5, "start"): [(3, 2), (4, 0), (1, 4)],
 }
 PLAN_BEFORE_NORM = [(3, 3)]
-PLAN_AFTER_NORM = ["t0", "v0", "v1", "t1"]
-PLAN_LAST = [
-    (5, 0), (4, 1), (5, 1), "v2", (3, 4), (5, 2), (5, 3), (1, 5), (2, 5), "v3", (4, 2), "t2",
-    (2, 6), (4, 3), (3, 5), (0, 6), (5, 4), "v4", (4, 4), "t3", (1, 6), (5, 5), "v5", (3, 6),
-    (4, 5), (5, 6), (4, 6),
-]
+PLAN_AFTER_NORM = ['t0', 't1', 'v0', 'v1']
+PLAN_LAST = [(5, 0), (4, 1), (5, 1), 'v2', 't2', (3, 4), (5, 2), (1, 5), (2, 5), (5, 3), 'v3', 't3', (4, 2), (2, 6), (4, 3), (3, 5), (0, 6), (5, 4), 'v4', (4, 4), (1, 6), (5, 5), 'v5', (3, 6), (4, 5), (5, 6), (4, 6)]
 TOKEN_PIECES = 4
 
 

time: 248 us -> 246 us (level)
  no operation moved by 1% of the time
where the time goes in v7:
time: 246 us
  Pallas kernels  244 us (99%)
    pallas_call x1, Pallas kernels, back(): pl.pallas_call(functools.partial(back_kernel, fast, ctx), grid=(groups +...  115 us
    pallas_call x1, Pallas kernels, front(): pl.pallas_call(functools.partial(front_kernel, ctx), grid=(1 + groups,),...  71 us
    pallas_call x1, Pallas kernels, feed_forward(): pl.pallas_call(functools.partial(feed_forward_kernel, fast, blocks), grid...  53.5 us

profile of v7, /device:TPU:0, one launch (start us, length us, event | category | flops | bytes accessed | tf_op | source)
XLA Modules:
  0.0 245.6 jit_solution(10938897633207760881)
XLA Ops:
  0.6 71.0 %front.1 = (bf16[4,256,768]{2,1,0:T(8,128)(2,1)}, bf16[1024,768]{1,0:T(8,128)(2,1)}, bf16[1024,2304]{1,0:T(8,128)(2,1)}, bf16[4,192,768]{2,1,0:T(8,128)(2,1)}, b...) custom-call(s32[4]{0:T(128)} %length_ref.5, bf16[4,256,768]{2,1,0:T(8,128)(2,1)} %tokens.1, bf16[4,256,768]{2,1,0:T(8,128)(2,1)} %cot_in.1, ...), custom_call_target="tpu_custom_call" | custom-call | tf_op jit(solution)/shard_map/front/pallas_call | solution.py:204
  71.6 53.5 %feed_forward.1 = (bf16[4,256,768]{2,1,0:T(8,128)(2,1)}, bf16[8,128]{1,0:T(8,128)(2,1)}, f32[1024,768]{1,0:T(8,128)}, bf16[1024,768]{1,0:T(8,128)(2,1)}, bf16[76...) custom-call(s32[4]{0:T(128)} %length_ref.5, ...), custom_call_target="tpu_custom_call" | custom-call | tf_op jit(solution)/shard_map/feed_forward/pallas_call | solution.py:574
  125.1 114.9 %back.1 = (bf16[4,256,768]{2,1,0:T(8,128)(2,1)}, bf16[2,192,768]{2,1,0:T(8,128)(2,1)}, bf16[2,48,3072]{2,1,0:T(8,128)(2,1)}, bf16[2,48,768]{2,1,0:T(8,128)(2,1)}...) custom-call(s32[4]{0:T(128)} %length_ref.5, bf16[1024,2304]{1,0:T(8,128)(2,1)} %get-tuple-element.40.q_ref.k_ref.v_ref, ...), custom_call_target="tpu_custom_call" | custom-call | tf_op jit(solution)/shard_map/back/pallas_call | solution.py:950
  240.0 4.3 %finish.1 = (bf16[4,256,768]{2,1,0:T(8,128)(2,1)}, bf16[4,256,768]{2,1,0:T(8,128)(2,1)}, f32[96,2304]{1,0:T(8,128)}, f32[96,768]{1,0:T(8,128)}, f32[96,3072]{1,0:T(8,128)}, /*index=5*/f32[384,768]{1,0:T(8,128)}) custom-call(bf16[4,256,768]{2,1,0:T(8,128)(2,1)} %get-tuple-element.39.output, bf16[4,256,768]{2,1,0:T(8,128)(2,1)} %get-tuple-element.50.tokens, ...), custom_call_target="tpu_custom_call" | custom-call | tf_op jit(solution)/shard_map/finish/pallas_call | solution.py:1067
  244.3 0.8 constant_dynamic-slice_fusion
  245.1 0.5 slice_bitcast_fusion

commit v8 on v7

--- a/solution.py
+++ b/solution.py
@@ -20,6 +20,7 @@
 epsilon = 1e-05
 MIB = 2**20
 VMEM_LIMIT = 62 * MIB
+X_PIECES = 4
 COT_TAIL = 64
 ANY = pl.BlockSpec(memory_space=pl.ANY)
 SMEM = pl.BlockSpec(memory_space=pltpu.SMEM)
@@ -138,10 +139,12 @@
     block = tokens.shape[1]
     offsets = [1] + list(range(2, ctx))
 
-    def token_copy(offset):
+    def token_copy(offset, piece):
+        size = block // X_PIECES
+        there = slice(piece * size, (piece + 1) * size)
         return to_partner(
-            tokens.at[me ^ offset], inputs.at[me], send.at[offset], recv.at[offset],
-            {"ctx": me ^ offset},
+            tokens.at[me ^ offset, there], inputs.at[me, there], send.at[offset, piece],
+            recv.at[offset, piece], {"ctx": me ^ offset},
         )
 
     def cotangent_copy(offset):
@@ -162,8 +165,9 @@
         own = pltpu.make_async_copy(tokens.at[me], inputs.at[me], local.at[0])
         own.start()
         greet([{"ctx": me ^ offset} for offset in offsets])
-        for offset in offsets[::-1]:
-            token_copy(offset).start()
+        for piece in range(X_PIECES):
+            for offset in offsets[::-1]:
+                token_copy(offset, piece).start()
 
         def project(source):
             hat, _ = normalise(inputs[source].astype(F32))
@@ -175,10 +179,12 @@
         own.wait()
         project(me)
         for offset in offsets:
-            token_copy(offset).wait_recv()
+            for piece in range(X_PIECES):
+                token_copy(offset, piece).wait_recv()
             if offset == offsets[-1]:
                 for earlier in offsets:
-                    token_copy(earlier).wait_send()
+                    for piece in range(X_PIECES):
+                        token_copy(earlier, piece).wait_send()
                 for later in offsets[::-1]:
                     cotangent_copy(later).start()
             project(me ^ offset)
@@ -224,8 +230,8 @@
             pltpu.VMEM((rows, 3 * width), BF16),
             pltpu.VMEM((HEADS, HD + 16, rows), BF16),
             pltpu.VMEM((LANES, BLOCK), F32),
-            pltpu.SemaphoreType.DMA((ctx,)),
-            pltpu.SemaphoreType.DMA((ctx,)),
+            pltpu.SemaphoreType.DMA((ctx, X_PIECES)),
+            pltpu.SemaphoreType.DMA((ctx, X_PIECES)),
             pltpu.SemaphoreType.DMA((ctx,)),
             pltpu.SemaphoreType.DMA((ctx,)),
             pltpu.SemaphoreType.DMA((5,)),
@@ -439,10 +445,14 @@
         @pl.when(step == 0)
         def _():
             up_load.wait()
-            down_load.wait()
 
         product_of = lambda cut: dot(low, up_weight[:, cut * CUT : (cut + 1) * CUT], 1, 0)
         current = product_of(0)
+
+        @pl.when(step == 0)
+        def _():
+            down_load.wait()
+
         total = middle
         for cut in range(cuts):
             part = slice(cut * CUT, (cut + 1) * CUT)

time: 246 us -> 247 us (level)
  no operation moved by 1% of the time
where the time goes in v8:
time: 247 us; the launch traced here: 246 us
  Pallas kernels  244 us (99%)
    pallas_call x1, Pallas kernels, back(): pl.pallas_call(functools.partial(back_kernel, fast, ctx), grid=(groups +...  115 us
    pallas_call x1, Pallas kernels, front(): pl.pallas_call(functools.partial(front_kernel, ctx), grid=(1 + groups,),...  71.2 us
    pallas_call x1, Pallas kernels, feed_forward(): pl.pallas_call(functools.partial(feed_forward_kernel, fast, blocks), grid...  53.8 us

profile of v8, /device:TPU:0, one launch (start us, length us, event | category | flops | bytes accessed | tf_op | source)
XLA Modules:
  0.0 246.3 jit_solution(12615824893523577186)
XLA Ops:
  0.6 71.2 %front.1 = (bf16[4,256,768]{2,1,0:T(8,128)(2,1)}, bf16[1024,768]{1,0:T(8,128)(2,1)}, bf16[1024,2304]{1,0:T(8,128)(2,1)}, bf16[4,192,768]{2,1,0:T(8,128)(2,1)}, b...) custom-call(s32[4]{0:T(128)} %length_ref.5, bf16[4,256,768]{2,1,0:T(8,128)(2,1)} %tokens.1, bf16[4,256,768]{2,1,0:T(8,128)(2,1)} %cot_in.1, ...), custom_call_target="tpu_custom_call" | custom-call | tf_op jit(solution)/shard_map/front/pallas_call | solution.py:210
  71.9 53.8 %feed_forward.1 = (bf16[4,256,768]{2,1,0:T(8,128)(2,1)}, bf16[8,128]{1,0:T(8,128)(2,1)}, f32[1024,768]{1,0:T(8,128)}, bf16[1024,768]{1,0:T(8,128)(2,1)}, bf16[76...) custom-call(s32[4]{0:T(128)} %length_ref.5, ...), custom_call_target="tpu_custom_call" | custom-call | tf_op jit(solution)/shard_map/feed_forward/pallas_call | solution.py:584
  125.7 115.0 %back.1 = (bf16[4,256,768]{2,1,0:T(8,128)(2,1)}, bf16[2,192,768]{2,1,0:T(8,128)(2,1)}, bf16[2,48,3072]{2,1,0:T(8,128)(2,1)}, bf16[2,48,768]{2,1,0:T(8,128)(2,1)}...) custom-call(s32[4]{0:T(128)} %length_ref.5, bf16[1024,2304]{1,0:T(8,128)(2,1)} %get-tuple-element.40.q_ref.k_ref.v_ref, ...), custom_call_target="tpu_custom_call" | custom-call | tf_op jit(solution)/shard_map/back/pallas_call | solution.py:960
  240.7 4.3 %finish.1 = (bf16[4,256,768]{2,1,0:T(8,128)(2,1)}, bf16[4,256,768]{2,1,0:T(8,128)(2,1)}, f32[96,2304]{1,0:T(8,128)}, f32[96,768]{1,0:T(8,128)}, f32[96,3072]{1,0:T(8,128)}, /*index=5*/f32[384,768]{1,0:T(8,128)}) custom-call(bf16[4,256,768]{2,1,0:T(8,128)(2,1)} %get-tuple-element.39.output, bf16[4,256,768]{2,1,0:T(8,128)(2,1)} %get-tuple-element.50.tokens, ...), custom_call_target="tpu_custom_call" | custom-call | tf_op jit(solution)/shard_map/finish/pallas_call | solution.py:1077
  245.0 0.8 constant_dynamic-slice_fusion
  245.8 0.5 slice_bitcast_fusion
